TPU v7x, 32 devices: a whole 2x2x4 slice. The times are simulated.
32 devices in a mesh: section: 8 (over z, core), tensor: 4 (over y, x).
Axes of the slice: x: 2, y: 2, z: 4, core: 2. Of those that a mesh axis runs over, the one named last changes fastest.
Arguments:
- layer_inputs: bfloat16 [8, 8192, 128], P('section', 'tensor'), may hold values from -160 to 160
- norm_gains: float32 [8, 8192], P('section', 'tensor'), may hold values from 0.1 to 1.9
- projection: bfloat16 [8, 8192, 2048], P('section', None, 'tensor'), may hold values from -0.125 to 0.125
- head_grads: bfloat16 [8, 128, 2048], P('section', None, 'tensor'), may hold values from -2 to 2
- top_grads: bfloat16 [8192, 128], P('tensor'), may hold values from -6 to 6
Outputs:
- input_grads: bfloat16 [8, 8192, 128], P('section', 'tensor')
- gain_grads: float32 [8, 8192], P('section', 'tensor')
All inputs are finite; a program needn't handle non-finite values.
Results may differ from a plain program's by a relative error of at most 0.017.
Values may be sent and summed in bfloat16 or wider, within the bound.
No kernel may reach another device: no remote copies, remote signals or barrier semaphores. Data moves between devices by JAX's collectives and lax.ppermute only.
A program may use at most 64 MiB of HBM per device.

v0:
```python
import jax
import jax.numpy as jnp
from jax import lax
from jax.sharding import PartitionSpec as P

D = 8192


epsilon = 1e-05


def prefix(value, axis, join, neutral):
    count = lax.axis_size(axis)
    place = lax.axis_index(axis)
    ahead = count - 1 - place
    gathered = lax.all_gather(value.astype(jnp.bfloat16), axis)
    state = jnp.zeros_like(value) + jnp.asarray(neutral, value.dtype)

    def one(turn, state):
        source = count - 1 - turn
        return join(state, lax.dynamic_index_in_dim(gathered, source, 0, False).astype(value.dtype))

    return lax.fori_loop(0, ahead, one, state)


def combine(earlier, later):
    return earlier + later


def local(layer_inputs, norm_gains, projection, head_grads, top_grads):
    values = layer_inputs[0].astype(jnp.float32)
    gains = norm_gains[0]
    weight = projection[0]
    grads = head_grads[0]
    partial_value = lax.psum_scatter(
        lax.dot_general(
            weight, grads, (((1,), (1,)), ((), ())), preferred_element_type=jnp.float32
        ).astype(jnp.bfloat16),
        "tensor",
        scatter_dimension=0,
        tiled=True,
    ).astype(jnp.float32)
    weighted = gains[:, None] * partial_value
    squares_part = jnp.sum(values * values, axis=0)
    inner_part = jnp.sum(weighted * values, axis=0)
    squares_all, inner = lax.psum((squares_part, inner_part), "tensor")
    scale = jnp.sqrt(squares_all / D + epsilon)
    branch = weighted / scale - values * (inner / (D * scale**3))
    gain_grad = jnp.sum(partial_value * values / scale, axis=1)
    later = prefix(branch, "section", combine, jnp.zeros_like(branch))
    result = (top_grads.astype(jnp.float32) + branch + later).astype(jnp.bfloat16)
    return (result[None], gain_grad[None])


def solution(mesh):
    placed = (
        P("section", "tensor", None),
        P("section", "tensor"),
        P("section", None, "tensor"),
        P("section", None, "tensor"),
        P("tensor", None),
    )
    return jax.shard_map(
        local,
        mesh=mesh,
        in_specs=placed,
        out_specs=(P("section", "tensor", None), P("section", "tensor")),
        check_vma=False,
    )
```

profile of v0, /device:TPU:0, one launch (start us, length us, event | category | flops | bytes accessed | tf_op | source)
XLA Modules:
  0.0 130.7 jit_solution(14546408826443918998)
XLA Ops:
  7.2 0.0 copy-start
  7.2 0.0 copy-start.1
  7.2 0.0 copy-start.4
  7.2 0.0 reduce-scatter.2.cloned.1.call-start
  7.2 0.8 copy-done
  8.1 7.1 %convolution_convert_fusion = bf16[8192,128]{1,0:T(8,128)(2,1)} fusion(bf16[1,8192,512]{2,1,0:T(8,128)(2,1)} %param.9, bf16[1,128,512]{2,1,0:T(8,128)(2,1)S(1)} %copy-done), kind=kOutput, calls=%fused_computation.1 | convolution fusion | flops 1074790400 | bytes 10616832 | tf_op jit(solution)/shard_map/dot_general | solution.py:36
  15.2 0.0 reduce-scatter.2.cloned.1.call-update
  15.2 0.0 all-gather.3.cloned.1.call-start
  15.2 0.0 copy-done.1
  15.2 0.3 fusion.3
  15.5 11.4 %psum.14 = f32[128]{0:T(128)S(1)} all-reduce(f32[128]{0:T(128)S(1)} %fusion.3), channel_id=1, replica_groups=mesh['section'=8,'tensor'=4] {'tensor'}, use_global_device_ids=true, to_apply=%region_2.0 | all-reduce | flops 128 | bytes 1024 | tf_op jit(solution)/shard_map/psum | solution.py:46
  27.0 26.2 %reduce-scatter.2.cloned.1.call-done = bf16[2048,128]{1,0:T(8,128)(2,1)} async-done(((bf16[8192,128]{1,0:T(8,128)(2,1)}), bf16[2048,128]{1,0:T(8,128)(2,1)}) %reduce-scatter.2.cloned.1.call-update) | async-done | bytes 524304 | tf_op jit(solution)/shard_map/reduce_scatter | solution.py:35
  53.2 0.0 copy-done.4
  53.2 2.4 %fusion.6 = (f32[2048]{0:T(1024)}, f32[128]{0:T(128)S(1)}) fusion(bf16[2048,128]{1,0:T(8,128)(2,1)} %reduce-scatter.2.cloned.1.call-done, bf16[1,2048,128]{2,1,0:T(8,128)(2,1)S(1)} %copy-done.1, f32[128]{0:T(128)S(1)} %add_sqrt_fusion, f32[2048]{0:T(1024)S(1)} %bitcast.27), kind=kLoop, calls=%fused_computation.14 | loop fusion | flops 2094976 | bytes 1065984 | tf_op jit(solution)/shard_map/reduce_sum | solution.py:49
  55.6 8.9 %psum.15 = f32[128]{0:T(128)S(1)} all-reduce(f32[128]{0:T(128)S(1)} %get-tuple-element.60), channel_id=1, replica_groups=mesh['section'=8,'tensor'=4] {'tensor'}, use_global_device_ids=true, to_apply=%region_4.0 | all-reduce | flops 128 | bytes 1024 | tf_op jit(solution)/shard_map/psum | solution.py:46
  64.5 2.2 %fusion.11 = bf16[2048,128]{1,0:T(8,128)(2,1)} fusion(f32[128]{0:T(128)S(1)} %fusion.10, bf16[1,2048,128]{2,1,0:T(8,128)(2,1)S(1)} %copy-done.1, f32[128]{0:T(128)S(1)} %add_sqrt_fusion, bf16[2048,128]{1,0:T(8,128)(2,1)} %reduce-scatter.2.cloned.1.call-done, f32[2048]{0:T(1024)S(1)} %bitcast.28), kind=kLoop, calls=%fused_computation.21 | loop fusion | flops 1835008 | bytes 1582080 | tf_op jit(solution)/shard_map/convert_element_type | solution.py:16
  66.7 0.0 all-gather.3.cloned.1.call-update
  66.7 47.2 %all-gather.3.cloned.1.call-done = bf16[16384,128]{1,0:T(8,128)(2,1)} async-done(((bf16[2048,128]{1,0:T(8,128)(2,1)}), bf16[16384,128]{1,0:T(8,128)(2,1)}) %all-gather.3.cloned.1.call-update) | async-done | bytes 4194320 | tf_op jit(solution)/shard_map/all_gather | solution.py:16
  114.0 0.1 broadcast_in_dim.12
  114.0 0.0 copy-start.2
  114.0 0.0 copy-start.3
  114.0 8.5 %while.12 = (s32[]{:T(128)}, f32[2048,128]{1,0:T(8,128)S(1)}, s32[]{:T(128)}, bf16[8,2048,128]{2,1,0:T(8,128)(2,1)}, s32[]{:T(128)}, /*index=5*/s32[]{:T(128)}, s32[]{:T(128)}, s32[]{:T(128)}) while((s32[]{:T(128)}, f32[2048,128]{1,0:T(8,128)S(1)}, s32[]{:T(128)}, bf16[8,2048,128]{2,1,0:T(8,128)(2,1)}, s32[]{:T(128)}, /*index=5*/s32[]{:T(128)}, ...), condition=%wide.region_6.7_spmd, body=%wide.region_5.0_spmd.sunk | while | flops 524294 | bytes 2621583 | solution.py:23
  114.1 1.3 convert_add_fusion.2
  115.4 1.2 convert_add_fusion.2
  116.6 1.2 convert_add_fusion.2
  117.8 1.2 convert_add_fusion.2
  119.0 1.2 convert_add_fusion.2
  120.2 1.2 convert_add_fusion.2
  121.4 1.2 convert_add_fusion.2
  122.6 0.0 copy-done.2
  122.6 0.0 copy-done.3
  122.6 1.2 fusion.7
  (2 shorter events, 0.0 us)
Async XLA Ops:
  7.2 0.9 copy-start
  7.2 8.1 %copy-start.1 = (bf16[1,2048,128]{2,1,0:T(8,128)(2,1)S(1)}, bf16[1,2048,128]{2,1,0:T(8,128)(2,1)}, u32[]{:S(2)}) copy-start(bf16[1,2048,128]{2,1,0:T(8,128)(2,1)} %param.7) | copy-start | bytes 1572868
  7.2 46.0 %copy-start.4 = (f32[1,2048]{1,0:T(1,128)S(1)}, f32[1,2048]{1,0:T(1,128)}, u32[]{:S(2)}) copy-start(f32[1,2048]{1,0:T(1,128)} %param.8) | copy-start | bytes 24580
  7.2 46.0 %reduce-scatter.2.cloned.1.call-start = ((), (), s32[]{:S(2)}) async-start(), calls=%async_computation.1 | async-start | bytes 2621440 | tf_op jit(solution)/shard_map/reduce_scatter | solution.py:35
  15.2 98.8 %all-gather.3.cloned.1.call-start = ((), (), s32[]{:S(2)}) async-start(), calls=%async_computation.2 | async-start | bytes 4718592 | tf_op jit(solution)/shard_map/all_gather | solution.py:16
  114.0 8.6 %copy-start.2 = (bf16[2048,128]{1,0:T(8,128)(2,1)S(1)}, bf16[2048,128]{1,0:T(8,128)(2,1)}, u32[]{:S(2)}) copy-start(bf16[2048,128]{1,0:T(8,128)(2,1)} %reduce-scatter.2.cloned.1.call-done) | copy-start | bytes 1572868
  114.0 8.6 %copy-start.3 = (bf16[2048,128]{1,0:T(8,128)(2,1)S(1)}, bf16[2048,128]{1,0:T(8,128)(2,1)}, u32[]{:S(2)}) copy-start(bf16[2048,128]{1,0:T(8,128)(2,1)} %param.11) | copy-start | bytes 1572868
Sparse Core Ops, SparseCore 0:
  15.3 37.8 reduce-scatter.1
  66.8 47.0 all-gather.2
where the time goes:
time: 131 us
  waiting for transfers between devices  73.5 us (56%)
  blocking collectives  20.3 us (15%)
  other arithmetic  14.4 us (11%)
  between operations  14.1 us (11%)
  matrix products  7.08 us (5%)
    all_gather x1, waiting for transfers between devices, prefix(): gathered = lax.all_gather(value.astype(jnp.bfloat16), axis)  47.2 us
    reduce_scatter x1, waiting for transfers between devices, local(): lax.psum_scatter(lax.dot_general(weight, grads, (((1,), (1,)), ((), ())),...  26.2 us
    psum x2, blocking collectives, local(): squares_all, inner = lax.psum((squares_part, inner_part), 'tensor')  20.3 us
    add x7, other arithmetic, combine(): return earlier + later  8.37 us
    dot_general x1, matrix products, local(): lax.dot_general(weight, grads, (((1,), (1,)), ((), ())), preferred_elemen...  7.08 us
  transfers between devices with their start and end apart: 2, of which 2 were waited for; matrix products, arithmetic and copies ran while one was open for 0% of the time, Pallas kernels for 0%

commit v1 on v0

v1 whole, which is shorter than its diff:
```python
import functools

import jax
import jax.numpy as jnp
from jax import lax
from jax.experimental import pallas as pl
from jax.experimental.pallas import tpu as pltpu
from jax.sharding import PartitionSpec as P

epsilon = 1e-05
F32 = jnp.float32
BF16 = jnp.bfloat16
BOTH = ("section", "tensor")


def product_kernel(order_ref, weight_ref, grads_ref, out_ref):
    out_ref[...] = lax.dot_general(
        weight_ref[...], grads_ref[...], (((1,), (1,)), ((), ())), preferred_element_type=F32
    ).astype(out_ref.dtype)


def product(order, weight, grads, blocks):
    features, depth = weight.shape
    tokens = grads.shape[0]
    rows = features // blocks
    count = order.shape[0]
    tile = min(rows, 1024)
    steps = rows // tile
    return pl.pallas_call(
        product_kernel,
        out_shape=jax.ShapeDtypeStruct((count * rows, tokens), BF16),
        grid_spec=pltpu.PrefetchScalarGridSpec(
            num_scalar_prefetch=1,
            grid=(count, steps),
            in_specs=[
                pl.BlockSpec((tile, depth), lambda j, r, order: (order[j] * steps + r, 0)),
                pl.BlockSpec((tokens, depth), lambda j, r, order: (0, 0)),
            ],
            out_specs=pl.BlockSpec((tile, tokens), lambda j, r, order: (j * steps + r, 0)),
        ),
        cost_estimate=pl.CostEstimate(
            flops=2 * count * rows * depth * tokens,
            bytes_accessed=count * rows * (depth + tokens) * 2,
            transcendentals=0,
        ),
    )(order, weight, grads)


def masks_of(count, parity):
    masks = [1 << b for b in range(count.bit_length() - 1)]
    return masks if parity == 0 else masks[::-1]


def sigma_of(count, parity):
    masks = masks_of(count, parity)
    steps = len(masks)
    table = []
    for j in range(count):
        value = 0
        for step in range(steps):
            if j >> (steps - 1 - step) & 1:
                value ^= masks[step]
        table.append(value)
    return table


def token_sum(value):
    count = lax.axis_size("tensor")
    low = 1
    while low < count:
        group = [low] if 2 * low >= count else [low, 2 * low, 3 * low]
        parts = [lax.ppermute(value, "tensor", [(i, i ^ m) for i in range(count)]) for m in group]
        value = functools.reduce(jnp.add, parts, value)
        low *= 4
    return value


def local(features, layer_inputs, norm_gains, projection, head_grads, top_grads):
    count = lax.axis_size("tensor")
    layers = lax.axis_size("section")
    place = lax.axis_index("tensor")
    layer = lax.axis_index("section")
    core = layer % 2
    values = layer_inputs[0].astype(F32)
    gains = norm_gains[0]
    weight = projection[0]
    grads = head_grads[0]
    rows, tokens = values.shape

    sigma = jnp.where(core == 0, jnp.array(sigma_of(count, 0), jnp.int32), jnp.array(sigma_of(count, 1), jnp.int32))
    order = place ^ sigma

    def exchange(value, step):
        pairs = []
        for s in range(layers):
            mask = masks_of(count, s % 2)[step]
            pairs += [(s * count + t, s * count + (t ^ mask)) for t in range(count)]
        return lax.ppermute(value, BOTH, pairs)

    half = count // 2
    sent = product(order[half:], weight, grads, count)
    came = exchange(sent, 0)
    kept = product(order[:half], weight, grads, count)
    squares = token_sum(jnp.sum(values * values, axis=0, keepdims=True))
    steps = count.bit_length() - 1
    held = [kept]
    for step in range(1, steps):
        half //= 2
        size = half * rows
        total = sum(a[size:].astype(F32) for a in held) + came[size:].astype(F32)
        held = [a[:size] for a in held] + [came[:size]]
        came = exchange(total.astype(BF16), step)
    partial_value = sum(a.astype(F32) for a in held) + came.astype(F32)

    scale = jnp.sqrt(squares / features + epsilon)
    weighted = gains[:, None] * partial_value
    inner = token_sum(jnp.sum(weighted * values, axis=0, keepdims=True))
    branch = weighted / scale - values * (inner / (features * scale**3))
    gain_grad = jnp.sum(partial_value * values / scale, axis=1)

    part = rows // 2
    swap = [(s, s ^ 1) for s in range(layers)]

    def section(value, pairs):
        return lax.ppermute(value, "section", pairs)

    mine = lax.dynamic_slice_in_dim(branch, core * part, part, 0)
    other = lax.dynamic_slice_in_dim(branch, (1 - core) * part, part, 0)
    pair = section(other.astype(BF16), swap).astype(F32)
    chip = mine + pair
    later = jnp.zeros_like(chip)
    distance = 2
    while distance < layers:
        came = section(
            (chip + later).astype(BF16), [(s, s - distance) for s in range(distance, layers)]
        )
        later = later + came.astype(F32)
        distance *= 2
    mate = section(jnp.where(core == 1, later + mine, later).astype(BF16), swap).astype(F32)
    own = later + jnp.where(core == 0, pair, 0.0)
    tail = jnp.where(core == 0, jnp.concatenate([own, mate]), jnp.concatenate([mate, own]))
    result = (top_grads.astype(F32) + branch + tail).astype(BF16)
    return (result[None], gain_grad[None])


def solution(mesh):
    placed = (
        P("section", "tensor", None),
        P("section", "tensor"),
        P("section", None, "tensor"),
        P("section", None, "tensor"),
        P("tensor", None),
    )

    def whole(layer_inputs, norm_gains, projection, head_grads, top_grads):
        return jax.shard_map(
            functools.partial(local, layer_inputs.shape[1]),
            mesh=mesh,
            in_specs=placed,
            out_specs=(P("section", "tensor", None), P("section", "tensor")),
            check_vma=False,
        )(layer_inputs, norm_gains, projection, head_grads, top_grads)

    return whole
```

time: 131 us -> 78.1 us (0.60)
  waiting for transfers between devices: 73.5 us -> 41.9 us
  blocking collectives: 20.3 us -> 0 us
  starting transfers between devices: 0.08 us -> 14.8 us
  between operations: 14.1 us -> 0.75 us
  Pallas kernels: 0 us -> 11.1 us
  matrix products: 7.08 us -> 0 us
  other arithmetic: 14.4 us -> 8.27 us
    all_gather x1 -> x0, waiting for transfers between devices: 47.2 us -> none  [prefix(): gathered = lax.all_gather(value.astype(jnp.bfloat16), axis)]
    ppermute x0 -> x12, waiting for transfers between devices: none -> 41.9 us  [the longest x4 26.6 us: section(): return lax.ppermute(value, 'section', pairs)]
    reduce_scatter x1 -> x0, waiting for transfers between devices: 26.2 us -> none  [local(): lax.psum_scatter(lax.dot_general(weight, grads, (((1,), (1,)), ((), ())),...]
    psum x2 -> x0, blocking collectives: 20.3 us -> none  [local(): squares_all, inner = lax.psum((squares_part, inner_part), 'tensor')]
    ppermute x0 -> x12, starting transfers between devices: none -> 14.8 us  [the longest x6 7.05 us: token_sum(): lax.ppermute(value, 'tensor', [(i, i ^ m) for i in range(count)])]
    pallas_call x0 -> x2, Pallas kernels: none -> 11.1 us  [product(): pl.pallas_call(product_kernel, out_shape=jax.ShapeDtypeStruct((count * ro...]
    add x7 -> x0, other arithmetic: 8.37 us -> none  [combine(): return earlier + later]
    dot_general x1 -> x0, matrix products: 7.08 us -> none  [local(): lax.dot_general(weight, grads, (((1,), (1,)), ((), ())), preferred_elemen...]
  transfers between devices with their start and end apart: 2 -> 12, of which waited for: 2 -> 9; matrix products, arithmetic and copies ran while one was open for 0% -> 0% of each run, Pallas kernels for 0% -> 7%
where the time goes in v1:
time: 78.1 us; the launch traced here: 77.5 us
  waiting for transfers between devices  41.9 us (54%)
  starting transfers between devices  14.8 us (19%)
  Pallas kernels  11.1 us (14%)
  other arithmetic  8.27 us (11%)
    ppermute x4, waiting for transfers between devices, section(): return lax.ppermute(value, 'section', pairs)  26.6 us
    pallas_call x2, Pallas kernels, product(): pl.pallas_call(product_kernel, out_shape=jax.ShapeDtypeStruct((count * ro...  11.1 us
    ppermute x6, waiting for transfers between devices, token_sum(): lax.ppermute(value, 'tensor', [(i, i ^ m) for i in range(count)])  7.84 us
    ppermute x2, waiting for transfers between devices, exchange(): return lax.ppermute(value, BOTH, pairs)  7.48 us
    ppermute x6, starting transfers between devices, token_sum(): lax.ppermute(value, 'tensor', [(i, i ^ m) for i in range(count)])  7.05 us
    ppermute x2, starting transfers between devices, exchange(): return lax.ppermute(value, BOTH, pairs)  5.06 us
    ppermute x4, starting transfers between devices, section(): return lax.ppermute(value, 'section', pairs)  2.73 us
    reduce_sum x1, other arithmetic, local(): gain_grad = jnp.sum(partial_value * values / scale, axis=1)  2.34 us
  transfers between devices with their start and end apart: 12, of which 9 were waited for; matrix products, arithmetic and copies ran while one was open for 0% of the time, Pallas kernels for 7%

profile of v1, /device:TPU:0, one launch (start us, length us, event | category | flops | bytes accessed | tf_op | source)
XLA Modules:
  0.0 77.5 jit_solution(7377799175214133338)
XLA Ops:
  0.6 0.7 fusion.14
  1.3 0.6 fusion.16
  1.9 5.6 %shard_map.87 = bf16[4096,128]{1,0:T(8,128)(2,1)} custom-call(s32[2]{0:T(128)} %get-tuple-element.7.order_ref, bf16[8192,512]{1,0:T(8,128)(2,1)} %bitcast.19, bf16[128,512]{1,0:T(8,128)(2,1)} %bitcast.21), custom_call_target="tpu_custom_call" | custom-call | flops 536870912 | bytes 5242880 | tf_op jit(solution)/shard_map/pallas_call | solution.py:29
  7.5 2.9 %collective-permute-start = (bf16[4096,128]{1,0:T(8,128)(2,1)}, bf16[4096,128]{1,0:T(8,128)(2,1)S(1)}, u32[]{:S(2)}, u32[]{:S(2)}) collective-permute-start(bf16[4096,128]{1,0:T(8,128)(2,1)} %shard_map.87), channel_id=1, source_target_pairs={{0,1},{1,0},{2,3},{3,2},{4,6},{5,7},{6,4},{7,5},{8,9},{9,8},{10,11... | collective-permute-start | bytes 3145736 | tf_op jit(solution)/shard_map/ppermute | solution.py:98
  10.4 5.5 %shard_map.86 = bf16[4096,128]{1,0:T(8,128)(2,1)} custom-call(s32[2]{0:T(128)} %get-tuple-element.6.order_ref, bf16[8192,512]{1,0:T(8,128)(2,1)} %bitcast.20, bf16[128,512]{1,0:T(8,128)(2,1)} %bitcast.22), custom_call_target="tpu_custom_call" | custom-call | flops 536870912 | bytes 5242880 | tf_op jit(solution)/shard_map/pallas_call | solution.py:29
  16.0 7.5 %collective-permute-done = bf16[4096,128]{1,0:T(8,128)(2,1)S(1)} collective-permute-done((bf16[4096,128]{1,0:T(8,128)(2,1)}, bf16[4096,128]{1,0:T(8,128)(2,1)S(1)}, u32[]{:S(2)}, u32[]{:S(2)}) %collective-permute-start) | collective-permute-done | bytes 1048608 | tf_op jit(solution)/shard_map/ppermute | solution.py:98
  23.4 1.2 %add_convert_fusion = bf16[2048,128]{1,0:T(8,128)(2,1)S(1)} fusion(bf16[4096,128]{1,0:T(8,128)(2,1)S(1)} %collective-permute-done, bf16[4096,128]{1,0:T(8,128)(2,1)} %shard_map.86), kind=kLoop, calls=%fused_computation.12 | loop fusion | flops 1048576 | bytes 1572864 | tf_op jit(solution)/shard_map/convert_element_type | solution.py:112
  24.6 2.1 %collective-permute-start.1 = (bf16[2048,128]{1,0:T(8,128)(2,1)S(1)}, bf16[2048,128]{1,0:T(8,128)(2,1)S(1)}, u32[]{:S(2)}, u32[]{:S(2)}) collective-permute-start(bf16[2048,128]{1,0:T(8,128)(2,1)S(1)} %add_convert_fusion), channel_id=1, source_target_pairs={{0,2},{1,3},{2,0},{3,1},{4,5},{5,4},{6,7},{7,6},{8,10},{9,11},{10,... | collective-permute-start | bytes 1572872 | tf_op jit(solution)/shard_map/ppermute | solution.py:98
  26.7 0.3 fusion
  27.0 1.5 %collective-permute-start.2 = (f32[1,128]{1,0:T(1,128)S(1)}, f32[1,128]{1,0:T(1,128)S(1)}, u32[]{:S(2)}, u32[]{:S(2)}) collective-permute-start(f32[1,128]{1,0:T(1,128)S(1)} %bitcast.28), channel_id=1, source_target_pairs={{0,1},{1,0},{2,3},{3,2},{4,5},{5,4},{6,7},{7,6},{8,9},{9,8},{10,11... | collective-permute-start | bytes 1544 | tf_op jit(solution)/shard_map/ppermute | solution.py:72
  28.6 0.5 collective-permute-start.3
  29.1 1.5 %collective-permute-start.4 = (f32[1,128]{1,0:T(1,128)S(1)}, f32[1,128]{1,0:T(1,128)S(1)}, u32[]{:S(2)}, u32[]{:S(2)}) collective-permute-start(f32[1,128]{1,0:T(1,128)S(1)} %bitcast.30), channel_id=1, source_target_pairs={{0,3},{1,2},{2,1},{3,0},{4,7},{5,6},{6,5},{7,4},{8,11},{9,10},{10,... | collective-permute-start | bytes 1544 | tf_op jit(solution)/shard_map/ppermute | solution.py:72
  30.6 0.1 collective-permute-done.2
  30.7 3.3 %collective-permute-done.3 = f32[1,128]{1,0:T(1,128)S(1)} collective-permute-done((f32[1,128]{1,0:T(1,128)S(1)}, f32[1,128]{1,0:T(1,128)S(1)}, u32[]{:S(2)}, u32[]{:S(2)}) %collective-permute-start.3) | collective-permute-done | bytes 544 | tf_op jit(solution)/shard_map/ppermute | solution.py:72
  34.0 2.3 %fusion.6 = (f32[2048]{0:T(1024)}, f32[128]{0:T(128)S(1)}) fusion(bf16[1,2048,128]{2,1,0:T(8,128)(2,1)S(1)} %copy-done, f32[128]{0:T(128)S(1)} %bitcast.26, bf16[2048,128]{1,0:T(8,128)(2,1)S(1)} %collective-permute-done.1, bf16[4096,128]{1,0:T(8,128)(2,1)S(1)} %collective-permute-done, bf16[4096,128]{1,0:T(8,128)(2,1)} %shard_map.86, f32[2048]{0:T(1024)S(1)} %bitcast.23), kind=kLoop, calls=%fused_computation.13 | loop fusion | flops 3143552 | bytes 2114560 | tf_op jit(solution)/shard_map/reduce_sum | solution.py:119
  36.4 2.0 %collective-permute-start.5 = (f32[1,128]{1,0:T(1,128)S(1)}, f32[1,128]{1,0:T(1,128)S(1)}, u32[]{:S(2)}, u32[]{:S(2)}) collective-permute-start(f32[1,128]{1,0:T(1,128)S(1)} %bitcast.31), channel_id=1, source_target_pairs={{0,1},{1,0},{2,3},{3,2},{4,5},{5,4},{6,7},{7,6},{8,9},{9,8},{10,11... | collective-permute-start | bytes 1544 | tf_op jit(solution)/shard_map/ppermute | solution.py:72
  38.3 1.5 %collective-permute-start.6 = (f32[1,128]{1,0:T(1,128)S(1)}, f32[1,128]{1,0:T(1,128)S(1)}, u32[]{:S(2)}, u32[]{:S(2)}) collective-permute-start(f32[1,128]{1,0:T(1,128)S(1)} %bitcast.32), channel_id=1, source_target_pairs={{0,2},{1,3},{2,0},{3,1},{4,6},{5,7},{6,4},{7,5},{8,10},{9,11},{10,... | collective-permute-start | bytes 1544 | tf_op jit(solution)/shard_map/ppermute | solution.py:72
  39.9 2.0 %collective-permute-done.6 = f32[1,128]{1,0:T(1,128)S(1)} collective-permute-done((f32[1,128]{1,0:T(1,128)S(1)}, f32[1,128]{1,0:T(1,128)S(1)}, u32[]{:S(2)}, u32[]{:S(2)}) %collective-permute-start.6) | collective-permute-done | bytes 544 | tf_op jit(solution)/shard_map/ppermute | solution.py:72
  41.9 2.4 %collective-permute-done.7 = f32[1,128]{1,0:T(1,128)S(1)} collective-permute-done((f32[1,128]{1,0:T(1,128)S(1)}, f32[1,128]{1,0:T(1,128)S(1)}, u32[]{:S(2)}, u32[]{:S(2)}) %collective-permute-start.7) | collective-permute-done | bytes 544 | tf_op jit(solution)/shard_map/ppermute | solution.py:72
  44.3 1.4 %fusion.2 = f32[2048,128]{1,0:T(8,128)S(1)} fusion(bf16[1,2048,128]{2,1,0:T(8,128)(2,1)S(1)} %copy-done, f32[128]{0:T(128)S(1)} %fusion.15, f32[128]{0:T(128)S(1)} %bitcast.27, f32[2048]{0:T(1024)S(1)} %bitcast.24, bf16[2048,128]{1,0:T(8,128)(2,1)S(1)} %collective-permute-done.1, bf16[4096,128]{1,0:T(8,128)(2,1)S(1)} %collective-permute-done, ...), kind=kLoop, calls=%fused_computation.6 | loop fusion | flops 2621440 | bytes 3154944 | tf_op jit(solution)/shard_map/sub | solution.py:118
  45.8 0.1 collective-permute-start.8
  45.9 1.5 %collective-permute-done.8 = bf16[1024,128]{1,0:T(8,128)(2,1)S(1)} collective-permute-done((bf16[1024,128]{1,0:T(8,128)(2,1)S(1)}, bf16[1024,128]{1,0:T(8,128)(2,1)S(1)}, u32[]{:S(2)}, u32[]{:S(2)}) %collective-permute-start.8) | collective-permute-done | bytes 262176 | tf_op jit(solution)/shard_map/ppermute | solution.py:125
  47.4 0.1 fusion.11
  47.4 1.3 %collective-permute-start.9 = (bf16[1024,128]{1,0:T(8,128)(2,1)S(1)}, bf16[1024,128]{1,0:T(8,128)(2,1)S(1)}, u32[]{:S(2)}, u32[]{:S(2)}) collective-permute-start(bf16[1024,128]{1,0:T(8,128)(2,1)S(1)} %fusion.11), channel_id=1, source_target_pairs={{8,0},{12,4},{16,8},{20,12},{24,16},{28,20},{9,1},{13,5},{17,9},{2... | collective-permute-start | bytes 786440 | tf_op jit(solution)/shard_map/ppermute | solution.py:125
  48.7 8.9 %collective-permute-done.9 = bf16[1024,128]{1,0:T(8,128)(2,1)S(1)} collective-permute-done((bf16[1024,128]{1,0:T(8,128)(2,1)S(1)}, bf16[1024,128]{1,0:T(8,128)(2,1)S(1)}, u32[]{:S(2)}, u32[]{:S(2)}) %collective-permute-start.9) | collective-permute-done | bytes 262176 | tf_op jit(solution)/shard_map/ppermute | solution.py:125
  57.7 0.1 fusion.8
  57.8 1.3 %collective-permute-start.10 = (bf16[1024,128]{1,0:T(8,128)(2,1)S(1)}, bf16[1024,128]{1,0:T(8,128)(2,1)S(1)}, u32[]{:S(2)}, u32[]{:S(2)}) collective-permute-start(bf16[1024,128]{1,0:T(8,128)(2,1)S(1)} %fusion.8), channel_id=1, source_target_pairs={{16,0},{20,4},{24,8},{28,12},{17,1},{21,5},{25,9},{29,13},{18,2},{... | collective-permute-start | bytes 786440 | tf_op jit(solution)/shard_map/ppermute | solution.py:125
  59.1 14.6 %collective-permute-done.10 = bf16[1024,128]{1,0:T(8,128)(2,1)S(1)} collective-permute-done((bf16[1024,128]{1,0:T(8,128)(2,1)S(1)}, bf16[1024,128]{1,0:T(8,128)(2,1)S(1)}, u32[]{:S(2)}, u32[]{:S(2)}) %collective-permute-start.10) | collective-permute-done | bytes 262176 | tf_op jit(solution)/shard_map/ppermute | solution.py:125
  73.7 0.2 fusion.9
  73.9 0.1 collective-permute-start.11
  73.9 1.5 %collective-permute-done.11 = bf16[1024,128]{1,0:T(8,128)(2,1)S(1)} collective-permute-done((bf16[1024,128]{1,0:T(8,128)(2,1)S(1)}, bf16[1024,128]{1,0:T(8,128)(2,1)S(1)}, u32[]{:S(2)}, u32[]{:S(2)}) %collective-permute-start.11) | collective-permute-done | bytes 262176 | tf_op jit(solution)/shard_map/ppermute | solution.py:125
  75.5 2.0 %fusion.10 = bf16[1,2048,128]{2,1,0:T(8,128)(2,1)} fusion(f32[1024,128]{1,0:T(8,128)S(1)} %get-tuple-element.5, f32[1024,128]{1,0:T(8,128)S(1)} %convert_element_type.70, f32[2048,128]{1,0:T(8,128)S(1)} %fusion.2, bf16[2048,128]{1,0:T(8,128)(2,1)} %param.11, pred[]{:T(512)S(6)} %eq.10), kind=kLoop, calls=%fused_computation.23 | loop fusion | flops 1835008 | bytes 3145729 | tf_op jit(solution)/shard_map/broadcast_in_dim | solution.py:143
  (12 shorter events, 0.1 us)
Async XLA Ops:
  1.9 24.8 %copy-start = (bf16[1,2048,128]{2,1,0:T(8,128)(2,1)S(1)}, bf16[1,2048,128]{2,1,0:T(8,128)(2,1)}, u32[]{:S(2)}) copy-start(bf16[1,2048,128]{2,1,0:T(8,128)(2,1)} %param.7) | copy-start | bytes 1572868
  1.9 32.1 %copy-start.1 = (f32[1,2048]{1,0:T(1,128)S(1)}, f32[1,2048]{1,0:T(1,128)}, u32[]{:S(2)}) copy-start(f32[1,2048]{1,0:T(1,128)} %param.8) | copy-start | bytes 24580
  7.5 15.9 %collective-permute-start = (bf16[4096,128]{1,0:T(8,128)(2,1)}, bf16[4096,128]{1,0:T(8,128)(2,1)S(1)}, u32[]{:S(2)}, u32[]{:S(2)}) collective-permute-start(bf16[4096,128]{1,0:T(8,128)(2,1)} %shard_map.87), channel_id=1, source_target_pairs={{0,1},{1,0},{2,3},{3,2},{4,6},{5,7},{6,4},{7,5},{8,9},{9,8},{10,11... | collective-permute-start | bytes 3145736 | tf_op jit(solution)/shard_map/ppermute | solution.py:98
  24.6 9.4 %collective-permute-start.1 = (bf16[2048,128]{1,0:T(8,128)(2,1)S(1)}, bf16[2048,128]{1,0:T(8,128)(2,1)S(1)}, u32[]{:S(2)}, u32[]{:S(2)}) collective-permute-start(bf16[2048,128]{1,0:T(8,128)(2,1)S(1)} %add_convert_fusion), channel_id=1, source_target_pairs={{0,2},{1,3},{2,0},{3,1},{4,5},{5,4},{6,7},{7,6},{8,10},{9,11},{10,... | collective-permute-start | bytes 1572872 | tf_op jit(solution)/shard_map/ppermute | solution.py:98
  27.0 3.7 %collective-permute-start.2 = (f32[1,128]{1,0:T(1,128)S(1)}, f32[1,128]{1,0:T(1,128)S(1)}, u32[]{:S(2)}, u32[]{:S(2)}) collective-permute-start(f32[1,128]{1,0:T(1,128)S(1)} %bitcast.28), channel_id=1, source_target_pairs={{0,1},{1,0},{2,3},{3,2},{4,5},{5,4},{6,7},{7,6},{8,9},{9,8},{10,11... | collective-permute-start | bytes 1544 | tf_op jit(solution)/shard_map/ppermute | solution.py:72
  28.6 5.4 %collective-permute-start.3 = (f32[1,128]{1,0:T(1,128)S(1)}, f32[1,128]{1,0:T(1,128)S(1)}, u32[]{:S(2)}, u32[]{:S(2)}) collective-permute-start(f32[1,128]{1,0:T(1,128)S(1)} %bitcast.29), channel_id=1, source_target_pairs={{0,2},{1,3},{2,0},{3,1},{4,6},{5,7},{6,4},{7,5},{8,10},{9,11},{10,... | collective-permute-start | bytes 1544 | tf_op jit(solution)/shard_map/ppermute | solution.py:72
  29.1 4.9 %collective-permute-start.4 = (f32[1,128]{1,0:T(1,128)S(1)}, f32[1,128]{1,0:T(1,128)S(1)}, u32[]{:S(2)}, u32[]{:S(2)}) collective-permute-start(f32[1,128]{1,0:T(1,128)S(1)} %bitcast.30), channel_id=1, source_target_pairs={{0,3},{1,2},{2,1},{3,0},{4,7},{5,6},{6,5},{7,4},{8,11},{9,10},{10,... | collective-permute-start | bytes 1544 | tf_op jit(solution)/shard_map/ppermute | solution.py:72
  36.4 3.5 %collective-permute-start.5 = (f32[1,128]{1,0:T(1,128)S(1)}, f32[1,128]{1,0:T(1,128)S(1)}, u32[]{:S(2)}, u32[]{:S(2)}) collective-permute-start(f32[1,128]{1,0:T(1,128)S(1)} %bitcast.31), channel_id=1, source_target_pairs={{0,1},{1,0},{2,3},{3,2},{4,5},{5,4},{6,7},{7,6},{8,9},{9,8},{10,11... | collective-permute-start | bytes 1544 | tf_op jit(solution)/shard_map/ppermute | solution.py:72
  38.3 3.5 %collective-permute-start.6 = (f32[1,128]{1,0:T(1,128)S(1)}, f32[1,128]{1,0:T(1,128)S(1)}, u32[]{:S(2)}, u32[]{:S(2)}) collective-permute-start(f32[1,128]{1,0:T(1,128)S(1)} %bitcast.32), channel_id=1, source_target_pairs={{0,2},{1,3},{2,0},{3,1},{4,6},{5,7},{6,4},{7,5},{8,10},{9,11},{10,... | collective-permute-start | bytes 1544 | tf_op jit(solution)/shard_map/ppermute | solution.py:72
  39.9 4.4 %collective-permute-start.7 = (f32[1,128]{1,0:T(1,128)S(1)}, f32[1,128]{1,0:T(1,128)S(1)}, u32[]{:S(2)}, u32[]{:S(2)}) collective-permute-start(f32[1,128]{1,0:T(1,128)S(1)} %bitcast.33), channel_id=1, source_target_pairs={{0,3},{1,2},{2,1},{3,0},{4,7},{5,6},{6,5},{7,4},{8,11},{9,10},{10,... | collective-permute-start | bytes 1544 | tf_op jit(solution)/shard_map/ppermute | solution.py:72
  45.8 1.6 %collective-permute-start.8 = (bf16[1024,128]{1,0:T(8,128)(2,1)S(1)}, bf16[1024,128]{1,0:T(8,128)(2,1)S(1)}, u32[]{:S(2)}, u32[]{:S(2)}) collective-permute-start(bf16[1024,128]{1,0:T(8,128)(2,1)S(1)} %dynamic-slice_convert_fusion), channel_id=1, source_target_pairs={{0,4},{4,0},{8,12},{12,8},{16,20},{20,16},{24,28},{28,24},{1,5},{5... | collective-permute-start | bytes 786440 | tf_op jit(solution)/shard_map/ppermute | solution.py:125
  47.4 10.2 %collective-permute-start.9 = (bf16[1024,128]{1,0:T(8,128)(2,1)S(1)}, bf16[1024,128]{1,0:T(8,128)(2,1)S(1)}, u32[]{:S(2)}, u32[]{:S(2)}) collective-permute-start(bf16[1024,128]{1,0:T(8,128)(2,1)S(1)} %fusion.11), channel_id=1, source_target_pairs={{8,0},{12,4},{16,8},{20,12},{24,16},{28,20},{9,1},{13,5},{17,9},{2... | collective-permute-start | bytes 786440 | tf_op jit(solution)/shard_map/ppermute | solution.py:125
  57.8 15.9 %collective-permute-start.10 = (bf16[1024,128]{1,0:T(8,128)(2,1)S(1)}, bf16[1024,128]{1,0:T(8,128)(2,1)S(1)}, u32[]{:S(2)}, u32[]{:S(2)}) collective-permute-start(bf16[1024,128]{1,0:T(8,128)(2,1)S(1)} %fusion.8), channel_id=1, source_target_pairs={{16,0},{20,4},{24,8},{28,12},{17,1},{21,5},{25,9},{29,13},{18,2},{... | collective-permute-start | bytes 786440 | tf_op jit(solution)/shard_map/ppermute | solution.py:125
  73.9 1.6 %collective-permute-start.11 = (bf16[1024,128]{1,0:T(8,128)(2,1)S(1)}, bf16[1024,128]{1,0:T(8,128)(2,1)S(1)}, u32[]{:S(2)}, u32[]{:S(2)}) collective-permute-start(bf16[1024,128]{1,0:T(8,128)(2,1)S(1)} %get-tuple-element.4), channel_id=1, source_target_pairs={{0,4},{4,0},{8,12},{12,8},{16,20},{20,16},{24,28},{28,24},{1,5},{5... | collective-permute-start | bytes 786440 | tf_op jit(solution)/shard_map/ppermute | solution.py:125

commit v2 on v0

v2 whole, which is shorter than its diff:
```python
import jax
import jax.numpy as jnp
from jax import lax
from jax.experimental import pallas as pl
from jax.experimental.pallas import tpu as pltpu
from jax.sharding import PartitionSpec as P

epsilon = 1e-05
F32 = jnp.float32
BF16 = jnp.bfloat16
BOTH = ("section", "tensor")
WHOLE = pl.BlockSpec(memory_space=pltpu.VMEM)
LIMIT = pltpu.CompilerParams(vmem_limit_bytes=16 << 20)


def near(value):
    return pltpu.with_memory_space_constraint(value, pltpu.VMEM)


def far(value):
    return pltpu.with_memory_space_constraint(value, pltpu.HBM)


def block_of(stream, j, count):
    bits = count.bit_length() - 1
    if stream == 1:
        return j
    out = 0
    for b in range(bits):
        out = out | (((j >> b) & 1) << (bits - 1 - b))
    return out


def mask_of(stream, step, count):
    return 1 << step if stream == 0 else count >> (step + 1)


def multiply(first_ref, second_ref, grads_ref, first_out, second_out):
    for weight, out in ((first_ref, first_out), (second_ref, second_out)):
        out[0] = lax.dot_general(
            weight[...], grads_ref[...], (((1,), (1,)), ((), ())), preferred_element_type=F32
        ).astype(out.dtype)


def keep_kernel(first_ref, second_ref, grads_ref, inputs_ref, first_out, second_out, squares_out):
    rows, tokens = inputs_ref.shape
    width = min(rows, 128)

    @pl.when(pl.program_id(0) == 0)
    def _():
        def step(i, total):
            at = pl.ds(pl.multiple_of(i * width, width), width)
            value = inputs_ref[at].astype(F32)
            return total + jnp.sum((value * value).reshape(width // 8, 8, tokens), axis=0)

        squares_out[...] = lax.fori_loop(0, rows // width, step, jnp.zeros((8, tokens), F32))

    multiply(first_ref, second_ref, grads_ref, first_out, second_out)


def product(base, weight, grads, count, extra=()):
    features, depth = weight.shape
    tokens = grads.shape[0]
    part = features // count // 2
    units = count // 2

    def rows_of(stream):
        def at(i):
            block = lax.axis_index("tensor") ^ block_of(stream, i + base, count)
            return (block * 2 + stream, 0)

        return at

    out = pltpu.VMEM((units, part, tokens), BF16)
    out_shape, out_specs = [out, out], [pl.BlockSpec((1, part, tokens), lambda i: (i, 0, 0))] * 2
    if extra:
        out_shape.append(pltpu.VMEM((8, tokens), F32))
        out_specs.append(WHOLE)
    return pl.pallas_call(
        keep_kernel if extra else multiply,
        out_shape=out_shape,
        grid=(units,),
        in_specs=[
            pl.BlockSpec((part, depth), rows_of(0)),
            pl.BlockSpec((part, depth), rows_of(1)),
            pl.BlockSpec((tokens, depth), lambda i: (0, 0)),
        ]
        + [WHOLE] * len(extra),
        out_specs=out_specs,
        compiler_params=LIMIT,
        cost_estimate=pl.CostEstimate(
            flops=4 * units * part * depth * tokens,
            bytes_accessed=4 * units * part * (depth + tokens),
            transcendentals=0,
        ),
    )(far(weight), far(weight), far(grads), *extra)


def add_kernel(*refs):
    outs = refs[-2:]
    for h, out in enumerate(outs):
        units = out.shape[0]
        parts = refs[h : len(refs) - 2 : 2]
        rows = min(out.shape[1], 64)

        def step(i, _):
            at = pl.ds(pl.multiple_of(i * rows, rows), rows)
            for u in range(units):
                total = sum(p[u + units, at].astype(F32) for p in parts)
                out[u, at] = total.astype(out.dtype)
            return 0

        lax.fori_loop(0, out.shape[1] // rows, step, 0)


def tile_of(part):
    return min(part, 128)


def wide(gains_ref, start, width, tokens):
    return jnp.broadcast_to(gains_ref[:, start : start + width], (tokens, width)).T


def sum_kernel(held, *refs):
    blocks = refs[: 2 * held]
    inputs_ref, gains_ref, squares_ref, partial_out, sums_out = refs[2 * held :]
    part, tokens = blocks[0].shape[1:]
    width = tile_of(part)
    inner = jnp.zeros((8, tokens), F32)
    for start in range(0, 2 * part, width):
        h, at = start // part, pl.ds(start % part, width)
        total = sum(b[0, at].astype(F32) for b in blocks[h::2])
        partial_out[h, at] = total
        product = total * wide(gains_ref, start, width, tokens) * inputs_ref[pl.ds(start, width)].astype(F32)
        inner = inner + jnp.sum(product.reshape(width // 8, 8, tokens), axis=0)
    sums_out[...] = jnp.concatenate([squares_ref[...], inner])


def branch_kernel(features, partial_ref, inputs_ref, gains_ref, *refs):
    sums, (branch_out, other_out, upside_out) = refs[:-3], refs[-3:]
    part, tokens = partial_ref.shape[1:]
    width = tile_of(part)
    both = jnp.sum(sum(s[...] for s in sums).reshape(2, 8, tokens), axis=1)
    upside = lax.rsqrt(both[:1] / features + epsilon)
    factor = both[1:] * (upside * upside * upside / features)
    upside_out[...] = jnp.broadcast_to(upside, upside_out.shape)
    for start in range(0, 2 * part, width):
        h, at = start // part, pl.ds(start % part, width)
        weighted = partial_ref[h, at] * wide(gains_ref, start, width, tokens)
        branch_out[h, at] = weighted * upside - inputs_ref[pl.ds(start, width)].astype(F32) * factor
    core = lax.axis_index("section") & 1
    other_out[...] = branch_out[1 - core].astype(other_out.dtype)


def pair_kernel(branch_ref, came_ref, out_ref):
    core = lax.axis_index("section") & 1
    out_ref[...] = (branch_ref[core] + came_ref[...].astype(F32)).astype(out_ref.dtype)


def later_kernel(terms_ref, later_out):
    chips, sub, tokens = terms_ref.shape
    total = jnp.zeros((sub, tokens), F32)
    for z in range(chips - 1, -1, -1):
        later_out[z] = total.astype(later_out.dtype)
        total = total + terms_ref[z].astype(F32)


def mate_kernel(later_ref, branch_ref, out_ref):
    core = lax.axis_index("section") & 1
    own = branch_ref[core] * core.astype(F32)
    out_ref[...] = (later_ref[...].astype(F32) + own).astype(out_ref.dtype)


def end_kernel(branch_ref, top_ref, later_ref, came_ref, mate_ref, out_ref):
    core = lax.axis_index("section") & 1
    half = core ^ pl.program_id(0)
    own = branch_ref[half] + top_ref[half].astype(F32)

    @pl.when(pl.program_id(0) == 0)
    def _():
        pair = came_ref[...].astype(F32) * (1 - core).astype(F32)
        out_ref[0] = (own + later_ref[...].astype(F32) + pair).astype(out_ref.dtype)

    @pl.when(pl.program_id(0) == 1)
    def _():
        out_ref[0] = (own + mate_ref[...].astype(F32)).astype(out_ref.dtype)


def call(kernel, out_shape, *arrays):
    return pl.pallas_call(
        kernel,
        out_shape=out_shape,
        in_specs=[WHOLE] * len(arrays),
        out_specs=jax.tree.map(lambda _: WHOLE, out_shape),
        compiler_params=LIMIT,
    )(*(near(a) for a in arrays))


def local(features, layer_inputs, norm_gains, projection, head_grads, top_grads):
    count = lax.axis_size("tensor")
    layers = lax.axis_size("section")
    chips = layers // 2
    weight = projection[0]
    grads = head_grads[0]
    inputs = layer_inputs[0]
    rows, tokens = inputs.shape
    part = rows // 2
    sub = part // chips
    steps = count.bit_length() - 1

    def exchange(value, mask):
        return lax.ppermute(value, "tensor", [(i, i ^ mask) for i in range(count)])

    def swap(value):
        return lax.ppermute(value, "section", [(s, s ^ 1) for s in range(layers)])

    def all_to_all(value, axis, groups):
        return lax.all_to_all(value, axis, 0, 0, tiled=True, axis_index_groups=groups)

    units = count // 2
    sent = product(units, weight, grads, count)
    came = [exchange(sent[h], mask_of(h, 0, count)) for h in range(2)]
    *kept, squares = product(0, weight, grads, count, (inputs,))

    held = [*kept, *came]
    for step in range(1, steps):
        units //= 2
        total = call(add_kernel, [pltpu.VMEM((units, part, tokens), BF16)] * 2, *held)
        held += [exchange(total[h], mask_of(h, step, count)) for h in range(2)]
    partial_value, sums = call(
        lambda *refs: sum_kernel(len(held) // 2, *refs),
        [pltpu.VMEM((2, part, tokens), F32), pltpu.VMEM((16, tokens), F32)],
        *held,
        inputs,
        norm_gains,
        squares,
    )

    sums, low = [sums], 1
    while low < count:
        group = [low] if 2 * low >= count else [low, 2 * low, 3 * low]
        total = sum(sums)
        sums = [total] + [exchange(total, m) for m in group]
        low *= 4
    half = pltpu.VMEM((part, tokens), BF16)
    branch, other, upside = call(
        lambda *refs: branch_kernel(features, *refs),
        [pltpu.VMEM((2, part, tokens), F32), half, pltpu.VMEM((8, tokens), F32)],
        partial_value,
        inputs,
        norm_gains,
        *sums,
    )

    groups = [[2 * z + c for z in range(chips)] for c in range(2)]
    pair = swap(other)
    terms = all_to_all(call(pair_kernel, half, branch, pair), "section", groups)
    later = call(
        later_kernel, pltpu.VMEM((chips, sub, tokens), BF16), terms.reshape(chips, sub, tokens)
    )
    later = all_to_all(later.reshape(part, tokens), "section", groups)
    mate = swap(call(mate_kernel, half, later, branch))
    values = inputs.reshape(2, part, tokens).astype(F32)
    gain_grad = jnp.sum(partial_value * values * upside[:1], axis=2).reshape(1, rows)
    arrays = (branch, top_grads.reshape(2, part, tokens), later, pair, mate)
    result = pl.pallas_call(
        end_kernel,
        out_shape=jax.ShapeDtypeStruct((2, part, tokens), BF16),
        grid=(2,),
        in_specs=[WHOLE] * len(arrays),
        out_specs=pl.BlockSpec(
            (1, part, tokens), lambda i: ((lax.axis_index("section") & 1) ^ i, 0, 0)
        ),
        compiler_params=LIMIT,
    )(*(near(a) for a in arrays))
    return (result.reshape(1, rows, tokens), gain_grad)


def solution(mesh):
    placed = (
        P("section", "tensor", None),
        P("section", "tensor"),
        P("section", None, "tensor"),
        P("section", None, "tensor"),
        P("tensor", None),
    )

    def whole(layer_inputs, norm_gains, projection, head_grads, top_grads):
        def part(*arrays):
            return local(layer_inputs.shape[1], *arrays)

        return jax.shard_map(
            part,
            mesh=mesh,
            in_specs=placed,
            out_specs=(P("section", "tensor", None), P("section", "tensor")),
            check_vma=False,
        )(layer_inputs, norm_gains, projection, head_grads, top_grads)

    return whole
```

time: 131 us -> 64.6 us (0.49)
  waiting for transfers between devices: 73.5 us -> 18.8 us
  other arithmetic: 14.4 us -> 0.36 us
  between operations: 14.1 us -> 0.72 us
  starting transfers between devices: 0.08 us -> 10.3 us
  Pallas kernels: 0 us -> 8.78 us
  matrix products: 7.08 us -> 0 us
  blocking collectives: 20.3 us -> 24.8 us
    all_gather x1 -> x0, waiting for transfers between devices: 47.2 us -> none  [prefix(): gathered = lax.all_gather(value.astype(jnp.bfloat16), axis)]
    reduce_scatter x1 -> x0, waiting for transfers between devices: 26.2 us -> none  [local(): lax.psum_scatter(lax.dot_general(weight, grads, (((1,), (1,)), ((), ())),...]
    all_to_all x0 -> x2, blocking collectives: none -> 24.8 us  [all_to_all(): lax.all_to_all(value, axis, 0, 0, tiled=True, axis_index_groups=groups)]
    psum x2 -> x0, blocking collectives: 20.3 us -> none  [local(): squares_all, inner = lax.psum((squares_part, inner_part), 'tensor')]
    ppermute x0 -> x9, waiting for transfers between devices: none -> 18.8 us  [the longest x7 16.7 us: exchange(): return lax.ppermute(value, 'tensor', [(i, i ^ mask) for i in range(count)])]
    ppermute x0 -> x9, starting transfers between devices: none -> 10.3 us  [the longest x7 10.2 us: exchange(): return lax.ppermute(value, 'tensor', [(i, i ^ mask) for i in range(count)])]
    pallas_call x0 -> x9, Pallas kernels: none -> 8.78 us  [the longest x2 6.51 us: product(): pl.pallas_call(keep_kernel if extra else multiply, out_shape=out_shape, g...]
    add x7 -> x0, other arithmetic: 8.37 us -> none  [combine(): return earlier + later]
  transfers between devices with their start and end apart: 2 -> 9, of which waited for: 2 -> 8; matrix products, arithmetic and copies ran while one was open for 0% -> 2% of each run, Pallas kernels for 0% -> 5%
where the time goes in v2:
time: 64.6 us; the launch traced here: 64.4 us
  blocking collectives  24.8 us (38%)
  waiting for transfers between devices  18.8 us (29%)
  starting transfers between devices  10.3 us (16%)
  Pallas kernels  8.78 us (14%)
  between operations  0.72 us (1%)
    all_to_all x2, blocking collectives, all_to_all(): lax.all_to_all(value, axis, 0, 0, tiled=True, axis_index_groups=groups)  24.8 us
    ppermute x7, waiting for transfers between devices, exchange(): return lax.ppermute(value, 'tensor', [(i, i ^ mask) for i in range(count)])  16.7 us
    ppermute x7, starting transfers between devices, exchange(): return lax.ppermute(value, 'tensor', [(i, i ^ mask) for i in range(count)])  10.2 us
    pallas_call x2, Pallas kernels, product(): pl.pallas_call(keep_kernel if extra else multiply, out_shape=out_shape, g...  6.51 us
    ppermute x2, waiting for transfers between devices, swap(): return lax.ppermute(value, 'section', [(s, s ^ 1) for s in range(layers)])  2.06 us
  transfers between devices with their start and end apart: 9, of which 8 were waited for; matrix products, arithmetic and copies ran while one was open for 2% of the time, Pallas kernels for 5%

profile of v2, /device:TPU:0, one launch (start us, length us, event | category | flops | bytes accessed | tf_op | source)
XLA Modules:
  0.0 64.4 jit_solution(5860235102214765466)
XLA Ops:
  0.6 0.0 copy-start
  0.6 3.1 %shard_map.69 = (bf16[2,1024,128]{2,1,0:T(8,128)(2,1)S(1)}, bf16[2,1024,128]{2,1,0:T(8,128)(2,1)S(1)}) custom-call(bf16[8192,512]{1,0:T(8,128)(2,1)} %bitcast.22, bf16[8192,512]{1,0:T(8,128)(2,1)} %bitcast.23, bf16[128,512]{1,0:T(8,128)(2,1)} %bitcast.26), custom_call_target="tpu_custom_call" | custom-call | flops 536870912 | bytes 5242880 | tf_op jit(solution)/shard_map/pallas_call | solution.py:79
  3.8 3.0 %collective-permute-start = (bf16[2,1024,128]{2,1,0:T(8,128)(2,1)S(1)}, bf16[2,1024,128]{2,1,0:T(8,128)(2,1)S(1)}, u32[]{:S(2)}, u32[]{:S(2)}) collective-permute-start(bf16[2,1024,128]{2,1,0:T(8,128)(2,1)S(1)} %get-tuple-element.16), channel_id=1, source_target_pairs={{0,1},{1,0},{2,3},{3,2},{4,5},{5,4},{6,7},{7,6},{8,9},{9,8},{10,11... | collective-permute-start | bytes 1572872 | tf_op jit(solution)/shard_map/ppermute | solution.py:212
  6.8 1.5 %collective-permute-start.1 = (bf16[2,1024,128]{2,1,0:T(8,128)(2,1)S(1)}, bf16[2,1024,128]{2,1,0:T(8,128)(2,1)S(1)}, u32[]{:S(2)}, u32[]{:S(2)}) collective-permute-start(bf16[2,1024,128]{2,1,0:T(8,128)(2,1)S(1)} %get-tuple-element.17), channel_id=1, source_target_pairs={{0,2},{1,3},{2,0},{3,1},{4,6},{5,7},{6,4},{7,5},{8,10},{9,11},{10,... | collective-permute-start | bytes 1572872 | tf_op jit(solution)/shard_map/ppermute | solution.py:212
  8.3 3.4 %shard_map.68 = (bf16[2,1024,128]{2,1,0:T(8,128)(2,1)S(1)}, bf16[2,1024,128]{2,1,0:T(8,128)(2,1)S(1)}, f32[8,128]{1,0:T(8,128)S(1)}) custom-call(bf16[8192,512]{1,0:T(8,128)(2,1)} %bitcast.24, bf16[8192,512]{1,0:T(8,128)(2,1)} %bitcast.25, bf16[128,512]{1,0:T(8,128)(2,1)} %bitcast.27, bf16[2048,128]{1,0:T(8,128)(2,1)S(1)} %bitcast.14), custom_call_target="tpu_custom_call" | custom-call | flops 536870912 | bytes 5242880 | tf_op jit(solution)/shard_map/pallas_call | solution.py:79
  11.7 0.0 copy-start.1
  11.7 7.0 %collective-permute-done.refs_2_ = bf16[2,1024,128]{2,1,0:T(8,128)(2,1)S(1)} collective-permute-done((bf16[2,1024,128]{2,1,0:T(8,128)(2,1)S(1)}, bf16[2,1024,128]{2,1,0:T(8,128)(2,1)S(1)}, u32[]{:S(2)}, u32[]{:S(2)}) %collective-permute-start) | collective-permute-done | bytes 524320 | tf_op jit(solution)/shard_map/ppermute | solution.py:212
  18.7 1.5 %collective-permute-done.1.refs_3_ = bf16[2,1024,128]{2,1,0:T(8,128)(2,1)S(1)} collective-permute-done((bf16[2,1024,128]{2,1,0:T(8,128)(2,1)S(1)}, bf16[2,1024,128]{2,1,0:T(8,128)(2,1)S(1)}, u32[]{:S(2)}, u32[]{:S(2)}) %collective-permute-start.1) | collective-permute-done | bytes 524320 | tf_op jit(solution)/shard_map/ppermute | solution.py:212
  20.2 0.3 shard_map.70
  20.5 1.6 %collective-permute-start.2 = (bf16[1,1024,128]{2,1,0:T(8,128)(2,1)S(1)}, bf16[1,1024,128]{2,1,0:T(8,128)(2,1)S(1)}, u32[]{:S(2)}, u32[]{:S(2)}) collective-permute-start(bf16[1,1024,128]{2,1,0:T(8,128)(2,1)S(1)} %get-tuple-element.18), channel_id=1, source_target_pairs={{0,2},{1,3},{2,0},{3,1},{4,6},{5,7},{6,4},{7,5},{8,10},{9,11},{10,... | collective-permute-start | bytes 786440 | tf_op jit(solution)/shard_map/ppermute | solution.py:212
  22.0 0.5 collective-permute-start.3
  22.6 4.8 %collective-permute-done.2.refs_4_ = bf16[1,1024,128]{2,1,0:T(8,128)(2,1)S(1)} collective-permute-done((bf16[1,1024,128]{2,1,0:T(8,128)(2,1)S(1)}, bf16[1,1024,128]{2,1,0:T(8,128)(2,1)S(1)}, u32[]{:S(2)}, u32[]{:S(2)}) %collective-permute-start.2) | collective-permute-done | bytes 262176 | tf_op jit(solution)/shard_map/ppermute | solution.py:212
  27.4 1.2 %collective-permute-done.3.refs_5_ = bf16[1,1024,128]{2,1,0:T(8,128)(2,1)S(1)} collective-permute-done((bf16[1,1024,128]{2,1,0:T(8,128)(2,1)S(1)}, bf16[1,1024,128]{2,1,0:T(8,128)(2,1)S(1)}, u32[]{:S(2)}, u32[]{:S(2)}) %collective-permute-start.3) | collective-permute-done | bytes 262176 | tf_op jit(solution)/shard_map/ppermute | solution.py:212
  28.6 0.4 shard_map.71
  29.0 0.7 %collective-permute-start.6 = (f32[16,128]{1,0:T(8,128)S(1)}, f32[16,128]{1,0:T(8,128)S(1)}, u32[]{:S(2)}, u32[]{:S(2)}) collective-permute-start(f32[16,128]{1,0:T(8,128)S(1)} %get-tuple-element.22.refs_3_), channel_id=1, source_target_pairs={{0,3},{1,2},{2,1},{3,0},{4,7},{5,6},{6,5},{7,4},{8,11},{9,10},{10,... | collective-permute-start | bytes 24584 | tf_op jit(solution)/shard_map/ppermute | solution.py:212
  29.7 1.4 %collective-permute-start.5 = (f32[16,128]{1,0:T(8,128)S(1)}, f32[16,128]{1,0:T(8,128)S(1)}, u32[]{:S(2)}, u32[]{:S(2)}) collective-permute-start(f32[16,128]{1,0:T(8,128)S(1)} %get-tuple-element.22.refs_3_), channel_id=1, source_target_pairs={{0,2},{1,3},{2,0},{3,1},{4,6},{5,7},{6,4},{7,5},{8,10},{9,11},{10,... | collective-permute-start | bytes 24584 | tf_op jit(solution)/shard_map/ppermute | solution.py:212
  31.1 1.4 %collective-permute-start.4 = (f32[16,128]{1,0:T(8,128)S(1)}, f32[16,128]{1,0:T(8,128)S(1)}, u32[]{:S(2)}, u32[]{:S(2)}) collective-permute-start(f32[16,128]{1,0:T(8,128)S(1)} %get-tuple-element.22.refs_3_), channel_id=1, source_target_pairs={{0,1},{1,0},{2,3},{3,2},{4,5},{5,4},{6,7},{7,6},{8,9},{9,8},{10,11... | collective-permute-start | bytes 24584 | tf_op jit(solution)/shard_map/ppermute | solution.py:212
  32.6 1.1 %collective-permute-done.6.refs_6_ = f32[16,128]{1,0:T(8,128)S(1)} collective-permute-done((f32[16,128]{1,0:T(8,128)S(1)}, f32[16,128]{1,0:T(8,128)S(1)}, u32[]{:S(2)}, u32[]{:S(2)}) %collective-permute-start.6) | collective-permute-done | bytes 8224 | tf_op jit(solution)/shard_map/ppermute | solution.py:212
  33.6 0.0 collective-permute-done.5.refs_5_
  33.6 1.2 %collective-permute-done.4.refs_4_ = f32[16,128]{1,0:T(8,128)S(1)} collective-permute-done((f32[16,128]{1,0:T(8,128)S(1)}, f32[16,128]{1,0:T(8,128)S(1)}, u32[]{:S(2)}, u32[]{:S(2)}) %collective-permute-start.4) | collective-permute-done | bytes 8224 | tf_op jit(solution)/shard_map/ppermute | solution.py:212
  34.8 0.4 shard_map.72
  35.2 0.1 collective-permute-start.7
  35.3 1.5 %collective-permute-done.7.came_ref = bf16[1024,128]{1,0:T(8,128)(2,1)S(1)} collective-permute-done((bf16[1024,128]{1,0:T(8,128)(2,1)S(1)}, bf16[1024,128]{1,0:T(8,128)(2,1)S(1)}, u32[]{:S(2)}, u32[]{:S(2)}) %collective-permute-start.7) | collective-permute-done | bytes 262176 | tf_op jit(solution)/shard_map/ppermute | solution.py:215
  36.8 0.1 shard_map.73
  36.9 13.8 %all_to_all.17.terms_ref = bf16[4,256,128]{2,1,0:T(8,128)(2,1)S(1)} all-to-all(bf16[4,256,128]{2,1,0:T(8,128)(2,1)S(1)} %bitcast.20), channel_id=1, replica_groups={{0,8,16,24},{4,12,20,28},{1,9,17,25},{5,13,21,29},{2,10,18,26},{6,14,22..., dimensions={0} | all-to-all | bytes 524288 | tf_op jit(solution)/shard_map/all_to_all | solution.py:218
  50.7 11.0 %all_to_all.18 = bf16[4,256,128]{2,1,0:T(8,128)(2,1)S(1)} all-to-all(bf16[4,256,128]{2,1,0:T(8,128)(2,1)S(1)} %shard_map.74), channel_id=1, replica_groups={{0,8,16,24},{4,12,20,28},{1,9,17,25},{5,13,21,29},{2,10,18,26},{6,14,22..., dimensions={0} | all-to-all | bytes 524288 | tf_op jit(solution)/shard_map/all_to_all | solution.py:218
  61.7 0.1 shard_map.75
  61.8 0.1 collective-permute-start.8
  61.9 0.4 fusion.1
  62.2 0.6 copy.7
  62.8 0.5 collective-permute-done.8.mate_ref
  63.4 1.0 %shard_map.76 = bf16[2,1024,128]{2,1,0:T(8,128)(2,1)} custom-call(f32[2,1024,128]{2,1,0:T(8,128)S(1)} %get-tuple-element.23.branch_ref, bf16[2,1024,128]{2,1,0:T(8,128)(2,1)S(1)} %bitcast.21, bf16[1024,128]{1,0:T(8,128)(2,1)S(1)} %bitcast.19, bf16[1024,128]{1,0:T(8,128)(2,1)S(1)} %collective-permute-done.7.came_ref, ...), custom_call_target="tpu_custom_call" | custom-call | tf_op jit(solution)/shard_map/pallas_call | solution.py:266
  (6 shorter events, 0.1 us)
Async XLA Ops:
  0.6 7.7 %copy-start = (bf16[1,2048,128]{2,1,0:T(8,128)(2,1)S(1)}, bf16[1,2048,128]{2,1,0:T(8,128)(2,1)}, u32[]{:S(2)}) copy-start(bf16[1,2048,128]{2,1,0:T(8,128)(2,1)} %param.5) | copy-start | bytes 1572868
  3.8 14.9 %collective-permute-start = (bf16[2,1024,128]{2,1,0:T(8,128)(2,1)S(1)}, bf16[2,1024,128]{2,1,0:T(8,128)(2,1)S(1)}, u32[]{:S(2)}, u32[]{:S(2)}) collective-permute-start(bf16[2,1024,128]{2,1,0:T(8,128)(2,1)S(1)} %get-tuple-element.16), channel_id=1, source_target_pairs={{0,1},{1,0},{2,3},{3,2},{4,5},{5,4},{6,7},{7,6},{8,9},{9,8},{10,11... | collective-permute-start | bytes 1572872 | tf_op jit(solution)/shard_map/ppermute | solution.py:212
  6.8 13.4 %collective-permute-start.1 = (bf16[2,1024,128]{2,1,0:T(8,128)(2,1)S(1)}, bf16[2,1024,128]{2,1,0:T(8,128)(2,1)S(1)}, u32[]{:S(2)}, u32[]{:S(2)}) collective-permute-start(bf16[2,1024,128]{2,1,0:T(8,128)(2,1)S(1)} %get-tuple-element.17), channel_id=1, source_target_pairs={{0,2},{1,3},{2,0},{3,1},{4,6},{5,7},{6,4},{7,5},{8,10},{9,11},{10,... | collective-permute-start | bytes 1572872 | tf_op jit(solution)/shard_map/ppermute | solution.py:212
  8.3 20.3 %copy-start.2 = (f32[1,2048]{1,0:T(1,128)S(1)}, f32[1,2048]{1,0:T(1,128)}, u32[]{:S(2)}) copy-start(f32[1,2048]{1,0:T(1,128)} %refs_2_.1) | copy-start | bytes 24580
  11.7 51.7 %copy-start.1 = (bf16[2048,128]{1,0:T(8,128)(2,1)S(1)}, bf16[2048,128]{1,0:T(8,128)(2,1)}, u32[]{:S(2)}) copy-start(bf16[2048,128]{1,0:T(8,128)(2,1)} %param.9) | copy-start | bytes 1572868
  20.5 6.9 %collective-permute-start.2 = (bf16[1,1024,128]{2,1,0:T(8,128)(2,1)S(1)}, bf16[1,1024,128]{2,1,0:T(8,128)(2,1)S(1)}, u32[]{:S(2)}, u32[]{:S(2)}) collective-permute-start(bf16[1,1024,128]{2,1,0:T(8,128)(2,1)S(1)} %get-tuple-element.18), channel_id=1, source_target_pairs={{0,2},{1,3},{2,0},{3,1},{4,6},{5,7},{6,4},{7,5},{8,10},{9,11},{10,... | collective-permute-start | bytes 786440 | tf_op jit(solution)/shard_map/ppermute | solution.py:212
  22.0 6.6 %collective-permute-start.3 = (bf16[1,1024,128]{2,1,0:T(8,128)(2,1)S(1)}, bf16[1,1024,128]{2,1,0:T(8,128)(2,1)S(1)}, u32[]{:S(2)}, u32[]{:S(2)}) collective-permute-start(bf16[1,1024,128]{2,1,0:T(8,128)(2,1)S(1)} %get-tuple-element.19), channel_id=1, source_target_pairs={{0,1},{1,0},{2,3},{3,2},{4,5},{5,4},{6,7},{7,6},{8,9},{9,8},{10,11... | collective-permute-start | bytes 786440 | tf_op jit(solution)/shard_map/ppermute | solution.py:212
  29.0 4.6 %collective-permute-start.6 = (f32[16,128]{1,0:T(8,128)S(1)}, f32[16,128]{1,0:T(8,128)S(1)}, u32[]{:S(2)}, u32[]{:S(2)}) collective-permute-start(f32[16,128]{1,0:T(8,128)S(1)} %get-tuple-element.22.refs_3_), channel_id=1, source_target_pairs={{0,3},{1,2},{2,1},{3,0},{4,7},{5,6},{6,5},{7,4},{8,11},{9,10},{10,... | collective-permute-start | bytes 24584 | tf_op jit(solution)/shard_map/ppermute | solution.py:212
  29.7 3.9 %collective-permute-start.5 = (f32[16,128]{1,0:T(8,128)S(1)}, f32[16,128]{1,0:T(8,128)S(1)}, u32[]{:S(2)}, u32[]{:S(2)}) collective-permute-start(f32[16,128]{1,0:T(8,128)S(1)} %get-tuple-element.22.refs_3_), channel_id=1, source_target_pairs={{0,2},{1,3},{2,0},{3,1},{4,6},{5,7},{6,4},{7,5},{8,10},{9,11},{10,... | collective-permute-start | bytes 24584 | tf_op jit(solution)/shard_map/ppermute | solution.py:212
  31.1 3.7 %collective-permute-start.4 = (f32[16,128]{1,0:T(8,128)S(1)}, f32[16,128]{1,0:T(8,128)S(1)}, u32[]{:S(2)}, u32[]{:S(2)}) collective-permute-start(f32[16,128]{1,0:T(8,128)S(1)} %get-tuple-element.22.refs_3_), channel_id=1, source_target_pairs={{0,1},{1,0},{2,3},{3,2},{4,5},{5,4},{6,7},{7,6},{8,9},{9,8},{10,11... | collective-permute-start | bytes 24584 | tf_op jit(solution)/shard_map/ppermute | solution.py:212
  35.2 1.6 %collective-permute-start.7 = (bf16[1024,128]{1,0:T(8,128)(2,1)S(1)}, bf16[1024,128]{1,0:T(8,128)(2,1)S(1)}, u32[]{:S(2)}, u32[]{:S(2)}) collective-permute-start(bf16[1024,128]{1,0:T(8,128)(2,1)S(1)} %get-tuple-element.24), channel_id=1, source_target_pairs={{0,4},{4,0},{8,12},{12,8},{16,20},{20,16},{24,28},{28,24},{1,5},{5... | collective-permute-start | bytes 786440 | tf_op jit(solution)/shard_map/ppermute | solution.py:215
  61.8 1.6 %collective-permute-start.8 = (bf16[1024,128]{1,0:T(8,128)(2,1)S(1)}, bf16[1024,128]{1,0:T(8,128)(2,1)S(1)}, u32[]{:S(2)}, u32[]{:S(2)}) collective-permute-start(bf16[1024,128]{1,0:T(8,128)(2,1)S(1)} %shard_map.75), channel_id=1, source_target_pairs={{0,4},{4,0},{8,12},{12,8},{16,20},{20,16},{24,28},{28,24},{1,5},{5... | collective-permute-start | bytes 786440 | tf_op jit(solution)/shard_map/ppermute | solution.py:215

commit v3 on v2

--- a/solution.py
+++ b/solution.py
@@ -152,23 +152,40 @@
     other_out[...] = branch_out[1 - core].astype(other_out.dtype)
 
 
-def pair_kernel(branch_ref, came_ref, out_ref):
+def chip_of(distance):
+    return (lax.axis_index("section") >> 1) ^ distance
+
+
+def pair_kernel(branch_ref, came_ref, *outs):
     core = lax.axis_index("section") & 1
-    out_ref[...] = (branch_ref[core] + came_ref[...].astype(F32)).astype(out_ref.dtype)
-
-
-def later_kernel(terms_ref, later_out):
-    chips, sub, tokens = terms_ref.shape
-    total = jnp.zeros((sub, tokens), F32)
+    for k, out in enumerate(outs):
+        q = chip_of(k)
+        out[...] = (branch_ref[core, q] + came_ref[q].astype(F32)).astype(out.dtype)
+
+
+def later_kernel(*refs):
+    chips = len(refs) // 2
+    held = refs[-1]
+    for k in range(chips):
+        held[chip_of(k)] = refs[k][...].astype(F32)
+    total = jnp.zeros(held.shape[1:], F32)
     for z in range(chips - 1, -1, -1):
-        later_out[z] = total.astype(later_out.dtype)
-        total = total + terms_ref[z].astype(F32)
-
-
-def mate_kernel(later_ref, branch_ref, out_ref):
+        term = held[z]
+        held[z] = total
+        total = total + term
+    for k in range(chips):
+        out = refs[chips + k]
+        out[...] = held[chip_of(k)].astype(out.dtype)
+
+
+def mate_kernel(branch_ref, *refs):
+    later, (later_out, mate_out) = refs[:-2], refs[-2:]
     core = lax.axis_index("section") & 1
-    own = branch_ref[core] * core.astype(F32)
-    out_ref[...] = (later_ref[...].astype(F32) + own).astype(out_ref.dtype)
+    scale = core.astype(F32)
+    for k, part in enumerate(later):
+        q = chip_of(k)
+        later_out[q] = part[...]
+        mate_out[q] = (part[...].astype(F32) + branch_ref[core, q] * scale).astype(mate_out.dtype)
 
 
 def end_kernel(branch_ref, top_ref, later_ref, came_ref, mate_ref, out_ref):
@@ -214,8 +231,10 @@
     def swap(value):
         return lax.ppermute(value, "section", [(s, s ^ 1) for s in range(layers)])
 
-    def all_to_all(value, axis, groups):
-        return lax.all_to_all(value, axis, 0, 0, tiled=True, axis_index_groups=groups)
+    def across(value, distance):
+        if not distance:
+            return value
+        return lax.ppermute(value, "section", [(s, s ^ (2 * distance)) for s in range(layers)])
 
     units = count // 2
     sent = product(units, weight, grads, count)
@@ -252,14 +271,23 @@
         *sums,
     )
 
-    groups = [[2 * z + c for z in range(chips)] for c in range(2)]
+    shape = (chips, sub, tokens)
+    block, whole = pltpu.VMEM((sub, tokens), BF16), pltpu.VMEM(shape, BF16)
     pair = swap(other)
-    terms = all_to_all(call(pair_kernel, half, branch, pair), "section", groups)
-    later = call(
-        later_kernel, pltpu.VMEM((chips, sub, tokens), BF16), terms.reshape(chips, sub, tokens)
-    )
-    later = all_to_all(later.reshape(part, tokens), "section", groups)
-    mate = swap(call(mate_kernel, half, later, branch))
+    halves = branch.reshape(2, *shape)
+    terms = call(pair_kernel, [block] * chips, halves, pair.reshape(shape))
+    terms = [across(v, k) for k, v in enumerate(terms)]
+    later = pl.pallas_call(
+        later_kernel,
+        out_shape=[block] * chips,
+        in_specs=[WHOLE] * chips,
+        out_specs=[WHOLE] * chips,
+        scratch_shapes=[pltpu.VMEM(shape, F32)],
+        compiler_params=LIMIT,
+    )(*(near(v) for v in terms))
+    later = [across(v, k) for k, v in enumerate(later)]
+    later, mate = call(mate_kernel, [whole] * 2, halves, *later)
+    later, mate = later.reshape(part, tokens), swap(mate.reshape(part, tokens))
     values = inputs.reshape(2, part, tokens).astype(F32)
     gain_grad = jnp.sum(partial_value * values * upside[:1], axis=2).reshape(1, rows)
     arrays = (branch, top_grads.reshape(2, part, tokens), later, pair, mate)

time: 64.6 us -> 58.9 us (0.912)
  blocking collectives: 24.8 us -> 0 us
  waiting for transfers between devices: 18.8 us -> 29 us
  starting transfers between devices: 10.3 us -> 19.2 us
    all_to_all x2 -> x0, blocking collectives: 24.8 us -> none  [all_to_all(): lax.all_to_all(value, axis, 0, 0, tiled=True, axis_index_groups=groups)]
    ppermute x0 -> x6, waiting for transfers between devices: none -> 10.2 us  [across(): lax.ppermute(value, 'section', [(s, s ^ 2 * distance) for s in range(laye...]
    ppermute x0 -> x6, starting transfers between devices: none -> 8.9 us  [across(): lax.ppermute(value, 'section', [(s, s ^ 2 * distance) for s in range(laye...]
  transfers between devices with their start and end apart: 9 -> 15, of which waited for: 8 -> 13; matrix products, arithmetic and copies ran while one was open for 2% -> 2% of each run, Pallas kernels for 5% -> 6%
where the time goes in v3:
time: 58.9 us; the launch traced here: 58.8 us
  waiting for transfers between devices  29 us (49%)
  starting transfers between devices  19.2 us (33%)
  Pallas kernels  8.86 us (15%)
  between operations  0.73 us (1%)
  local copies, waits for them, and re-layouts  0.63 us (1%)
    ppermute x7, waiting for transfers between devices, exchange(): return lax.ppermute(value, 'tensor', [(i, i ^ mask) for i in range(count)])  16.7 us
    ppermute x7, starting transfers between devices, exchange(): return lax.ppermute(value, 'tensor', [(i, i ^ mask) for i in range(count)])  10.2 us
    ppermute x6, waiting for transfers between devices, across(): lax.ppermute(value, 'section', [(s, s ^ 2 * distance) for s in range(laye...  10.2 us
    ppermute x6, starting transfers between devices, across(): lax.ppermute(value, 'section', [(s, s ^ 2 * distance) for s in range(laye...  8.9 us
    pallas_call x2, Pallas kernels, product(): pl.pallas_call(keep_kernel if extra else multiply, out_shape=out_shape, g...  6.51 us
    ppermute x2, waiting for transfers between devices, swap(): return lax.ppermute(value, 'section', [(s, s ^ 1) for s in range(layers)])  2.06 us
    pallas_call x5, Pallas kernels, call(): pl.pallas_call(kernel, out_shape=out_shape, in_specs=[WHOLE] * len(arrays...  1.22 us
  transfers between devices with their start and end apart: 15, of which 13 were waited for; matrix products, arithmetic and copies ran while one was open for 2% of the time, Pallas kernels for 6%

profile of v3, /device:TPU:0, one launch (start us, length us, event | category | flops | bytes accessed | tf_op | source)
XLA Modules:
  0.0 58.8 jit_solution(16682864865873406813)
XLA Ops:
  0.6 3.1 %shard_map.69 = (bf16[2,1024,128]{2,1,0:T(8,128)(2,1)S(1)}, bf16[2,1024,128]{2,1,0:T(8,128)(2,1)S(1)}) custom-call(bf16[8192,512]{1,0:T(8,128)(2,1)} %bitcast.26, bf16[8192,512]{1,0:T(8,128)(2,1)} %bitcast.27, bf16[128,512]{1,0:T(8,128)(2,1)} %bitcast.30), custom_call_target="tpu_custom_call" | custom-call | flops 536870912 | bytes 5242880 | tf_op jit(solution)/shard_map/pallas_call | solution.py:79
  3.8 3.0 %collective-permute-start = (bf16[2,1024,128]{2,1,0:T(8,128)(2,1)S(1)}, bf16[2,1024,128]{2,1,0:T(8,128)(2,1)S(1)}, u32[]{:S(2)}, u32[]{:S(2)}) collective-permute-start(bf16[2,1024,128]{2,1,0:T(8,128)(2,1)S(1)} %get-tuple-element.26), channel_id=1, source_target_pairs={{0,1},{1,0},{2,3},{3,2},{4,5},{5,4},{6,7},{7,6},{8,9},{9,8},{10,11... | collective-permute-start | bytes 1572872 | tf_op jit(solution)/shard_map/ppermute | solution.py:229
  6.8 1.5 %collective-permute-start.1 = (bf16[2,1024,128]{2,1,0:T(8,128)(2,1)S(1)}, bf16[2,1024,128]{2,1,0:T(8,128)(2,1)S(1)}, u32[]{:S(2)}, u32[]{:S(2)}) collective-permute-start(bf16[2,1024,128]{2,1,0:T(8,128)(2,1)S(1)} %get-tuple-element.27), channel_id=1, source_target_pairs={{0,2},{1,3},{2,0},{3,1},{4,6},{5,7},{6,4},{7,5},{8,10},{9,11},{10,... | collective-permute-start | bytes 1572872 | tf_op jit(solution)/shard_map/ppermute | solution.py:229
  8.3 3.4 %shard_map.68 = (bf16[2,1024,128]{2,1,0:T(8,128)(2,1)S(1)}, bf16[2,1024,128]{2,1,0:T(8,128)(2,1)S(1)}, f32[8,128]{1,0:T(8,128)S(1)}) custom-call(bf16[8192,512]{1,0:T(8,128)(2,1)} %bitcast.28, bf16[8192,512]{1,0:T(8,128)(2,1)} %bitcast.29, bf16[128,512]{1,0:T(8,128)(2,1)} %bitcast.31, bf16[2048,128]{1,0:T(8,128)(2,1)S(1)} %bitcast.18), custom_call_target="tpu_custom_call" | custom-call | flops 536870912 | bytes 5242880 | tf_op jit(solution)/shard_map/pallas_call | solution.py:79
  11.7 7.0 %collective-permute-done.refs_2_ = bf16[2,1024,128]{2,1,0:T(8,128)(2,1)S(1)} collective-permute-done((bf16[2,1024,128]{2,1,0:T(8,128)(2,1)S(1)}, bf16[2,1024,128]{2,1,0:T(8,128)(2,1)S(1)}, u32[]{:S(2)}, u32[]{:S(2)}) %collective-permute-start) | collective-permute-done | bytes 524320 | tf_op jit(solution)/shard_map/ppermute | solution.py:229
  18.7 1.5 %collective-permute-done.1.refs_3_ = bf16[2,1024,128]{2,1,0:T(8,128)(2,1)S(1)} collective-permute-done((bf16[2,1024,128]{2,1,0:T(8,128)(2,1)S(1)}, bf16[2,1024,128]{2,1,0:T(8,128)(2,1)S(1)}, u32[]{:S(2)}, u32[]{:S(2)}) %collective-permute-start.1) | collective-permute-done | bytes 524320 | tf_op jit(solution)/shard_map/ppermute | solution.py:229
  20.2 0.3 shard_map.70
  20.5 1.6 %collective-permute-start.2 = (bf16[1,1024,128]{2,1,0:T(8,128)(2,1)S(1)}, bf16[1,1024,128]{2,1,0:T(8,128)(2,1)S(1)}, u32[]{:S(2)}, u32[]{:S(2)}) collective-permute-start(bf16[1,1024,128]{2,1,0:T(8,128)(2,1)S(1)} %get-tuple-element.28), channel_id=1, source_target_pairs={{0,2},{1,3},{2,0},{3,1},{4,6},{5,7},{6,4},{7,5},{8,10},{9,11},{10,... | collective-permute-start | bytes 786440 | tf_op jit(solution)/shard_map/ppermute | solution.py:229
  22.0 0.5 collective-permute-start.3
  22.6 4.8 %collective-permute-done.2.refs_4_ = bf16[1,1024,128]{2,1,0:T(8,128)(2,1)S(1)} collective-permute-done((bf16[1,1024,128]{2,1,0:T(8,128)(2,1)S(1)}, bf16[1,1024,128]{2,1,0:T(8,128)(2,1)S(1)}, u32[]{:S(2)}, u32[]{:S(2)}) %collective-permute-start.2) | collective-permute-done | bytes 262176 | tf_op jit(solution)/shard_map/ppermute | solution.py:229
  27.4 1.2 %collective-permute-done.3.refs_5_ = bf16[1,1024,128]{2,1,0:T(8,128)(2,1)S(1)} collective-permute-done((bf16[1,1024,128]{2,1,0:T(8,128)(2,1)S(1)}, bf16[1,1024,128]{2,1,0:T(8,128)(2,1)S(1)}, u32[]{:S(2)}, u32[]{:S(2)}) %collective-permute-start.3) | collective-permute-done | bytes 262176 | tf_op jit(solution)/shard_map/ppermute | solution.py:229
  28.6 0.4 shard_map.71
  29.0 0.7 %collective-permute-start.6 = (f32[16,128]{1,0:T(8,128)S(1)}, f32[16,128]{1,0:T(8,128)S(1)}, u32[]{:S(2)}, u32[]{:S(2)}) collective-permute-start(f32[16,128]{1,0:T(8,128)S(1)} %get-tuple-element.32.refs_3_), channel_id=1, source_target_pairs={{0,3},{1,2},{2,1},{3,0},{4,7},{5,6},{6,5},{7,4},{8,11},{9,10},{10,... | collective-permute-start | bytes 24584 | tf_op jit(solution)/shard_map/ppermute | solution.py:229
  29.7 1.4 %collective-permute-start.5 = (f32[16,128]{1,0:T(8,128)S(1)}, f32[16,128]{1,0:T(8,128)S(1)}, u32[]{:S(2)}, u32[]{:S(2)}) collective-permute-start(f32[16,128]{1,0:T(8,128)S(1)} %get-tuple-element.32.refs_3_), channel_id=1, source_target_pairs={{0,2},{1,3},{2,0},{3,1},{4,6},{5,7},{6,4},{7,5},{8,10},{9,11},{10,... | collective-permute-start | bytes 24584 | tf_op jit(solution)/shard_map/ppermute | solution.py:229
  31.1 1.4 %collective-permute-start.4 = (f32[16,128]{1,0:T(8,128)S(1)}, f32[16,128]{1,0:T(8,128)S(1)}, u32[]{:S(2)}, u32[]{:S(2)}) collective-permute-start(f32[16,128]{1,0:T(8,128)S(1)} %get-tuple-element.32.refs_3_), channel_id=1, source_target_pairs={{0,1},{1,0},{2,3},{3,2},{4,5},{5,4},{6,7},{7,6},{8,9},{9,8},{10,11... | collective-permute-start | bytes 24584 | tf_op jit(solution)/shard_map/ppermute | solution.py:229
  32.6 1.1 %collective-permute-done.6.refs_6_ = f32[16,128]{1,0:T(8,128)S(1)} collective-permute-done((f32[16,128]{1,0:T(8,128)S(1)}, f32[16,128]{1,0:T(8,128)S(1)}, u32[]{:S(2)}, u32[]{:S(2)}) %collective-permute-start.6) | collective-permute-done | bytes 8224 | tf_op jit(solution)/shard_map/ppermute | solution.py:229
  33.6 1.2 %collective-permute-done.4.refs_4_ = f32[16,128]{1,0:T(8,128)S(1)} collective-permute-done((f32[16,128]{1,0:T(8,128)S(1)}, f32[16,128]{1,0:T(8,128)S(1)}, u32[]{:S(2)}, u32[]{:S(2)}) %collective-permute-start.4) | collective-permute-done | bytes 8224 | tf_op jit(solution)/shard_map/ppermute | solution.py:229
  34.8 0.4 shard_map.72
  35.3 1.5 %collective-permute-done.7.came_ref = bf16[1024,128]{1,0:T(8,128)(2,1)S(1)} collective-permute-done((bf16[1024,128]{1,0:T(8,128)(2,1)S(1)}, bf16[1024,128]{1,0:T(8,128)(2,1)S(1)}, u32[]{:S(2)}, u32[]{:S(2)}) %collective-permute-start.7) | collective-permute-done | bytes 262176 | tf_op jit(solution)/shard_map/ppermute | solution.py:232
  36.9 1.6 %collective-permute-start.8 = (bf16[256,128]{1,0:T(8,128)(2,1)S(1)}, bf16[256,128]{1,0:T(8,128)(2,1)S(1)}, u32[]{:S(2)}, u32[]{:S(2)}) collective-permute-start(bf16[256,128]{1,0:T(8,128)(2,1)S(1)} %get-tuple-element.36), channel_id=1, source_target_pairs={{0,8},{4,12},{8,0},{12,4},{16,24},{20,28},{24,16},{28,20},{1,9},{5... | collective-permute-start | bytes 196616 | tf_op jit(solution)/shard_map/ppermute | solution.py:237
  38.5 2.6 %collective-permute-start.9 = (bf16[256,128]{1,0:T(8,128)(2,1)S(1)}, bf16[256,128]{1,0:T(8,128)(2,1)S(1)}, u32[]{:S(2)}, u32[]{:S(2)}) collective-permute-start(bf16[256,128]{1,0:T(8,128)(2,1)S(1)} %get-tuple-element.37), channel_id=1, source_target_pairs={{0,16},{4,20},{8,24},{12,28},{16,0},{20,4},{24,8},{28,12},{1,17},{... | collective-permute-start | bytes 196616 | tf_op jit(solution)/shard_map/ppermute | solution.py:237
  41.3 4.7 %collective-permute-done.9.refs_2_ = bf16[256,128]{1,0:T(8,128)(2,1)S(1)} collective-permute-done((bf16[256,128]{1,0:T(8,128)(2,1)S(1)}, bf16[256,128]{1,0:T(8,128)(2,1)S(1)}, u32[]{:S(2)}, u32[]{:S(2)}) %collective-permute-start.9) | collective-permute-done | bytes 65568 | tf_op jit(solution)/shard_map/ppermute | solution.py:237
  46.1 1.2 %collective-permute-done.10.refs_3_ = bf16[256,128]{1,0:T(8,128)(2,1)S(1)} collective-permute-done((bf16[256,128]{1,0:T(8,128)(2,1)S(1)}, bf16[256,128]{1,0:T(8,128)(2,1)S(1)}, u32[]{:S(2)}, u32[]{:S(2)}) %collective-permute-start.10) | collective-permute-done | bytes 65568 | tf_op jit(solution)/shard_map/ppermute | solution.py:237
  47.4 0.9 %collective-permute-start.11 = (bf16[256,128]{1,0:T(8,128)(2,1)S(1)}, bf16[256,128]{1,0:T(8,128)(2,1)S(1)}, u32[]{:S(2)}, u32[]{:S(2)}) collective-permute-start(bf16[256,128]{1,0:T(8,128)(2,1)S(1)} %get-tuple-element.40), channel_id=1, source_target_pairs={{0,8},{4,12},{8,0},{12,4},{16,24},{20,28},{24,16},{28,20},{1,9},{5... | collective-permute-start | bytes 196616 | tf_op jit(solution)/shard_map/ppermute | solution.py:237
  48.3 1.7 %collective-permute-start.12 = (bf16[256,128]{1,0:T(8,128)(2,1)S(1)}, bf16[256,128]{1,0:T(8,128)(2,1)S(1)}, u32[]{:S(2)}, u32[]{:S(2)}) collective-permute-start(bf16[256,128]{1,0:T(8,128)(2,1)S(1)} %get-tuple-element.41), channel_id=1, source_target_pairs={{0,16},{4,20},{8,24},{12,28},{16,0},{20,4},{24,8},{28,12},{1,17},{... | collective-permute-start | bytes 196616 | tf_op jit(solution)/shard_map/ppermute | solution.py:237
  50.0 1.8 %collective-permute-start.13 = (bf16[256,128]{1,0:T(8,128)(2,1)S(1)}, bf16[256,128]{1,0:T(8,128)(2,1)S(1)}, u32[]{:S(2)}, u32[]{:S(2)}) collective-permute-start(bf16[256,128]{1,0:T(8,128)(2,1)S(1)} %get-tuple-element.42), channel_id=1, source_target_pairs={{0,24},{4,28},{8,16},{12,20},{16,8},{20,12},{24,0},{28,4},{1,25},{... | collective-permute-start | bytes 196616 | tf_op jit(solution)/shard_map/ppermute | solution.py:237
  51.9 2.6 %collective-permute-done.12.refs_2_ = bf16[256,128]{1,0:T(8,128)(2,1)S(1)} collective-permute-done((bf16[256,128]{1,0:T(8,128)(2,1)S(1)}, bf16[256,128]{1,0:T(8,128)(2,1)S(1)}, u32[]{:S(2)}, u32[]{:S(2)}) %collective-permute-start.12) | collective-permute-done | bytes 65568 | tf_op jit(solution)/shard_map/ppermute | solution.py:237
  54.5 1.5 %collective-permute-done.13.refs_3_ = bf16[256,128]{1,0:T(8,128)(2,1)S(1)} collective-permute-done((bf16[256,128]{1,0:T(8,128)(2,1)S(1)}, bf16[256,128]{1,0:T(8,128)(2,1)S(1)}, u32[]{:S(2)}, u32[]{:S(2)}) %collective-permute-start.13) | collective-permute-done | bytes 65568 | tf_op jit(solution)/shard_map/ppermute | solution.py:237
  56.2 0.4 fusion.1
  56.6 0.6 %copy.7 = f32[1,1,2,1024]{3,1,2,0:T(1,128)} copy(f32[1,1,2,1024]{3,2,1,0:T(2,128)S(1)} %bitcast.33) | data formatting | bytes 16384
  57.2 0.5 collective-permute-done.14.mate_ref
  57.7 1.0 %shard_map.76 = bf16[2,1024,128]{2,1,0:T(8,128)(2,1)} custom-call(f32[2,1024,128]{2,1,0:T(8,128)S(1)} %get-tuple-element.33.branch_ref, bf16[2,1024,128]{2,1,0:T(8,128)(2,1)S(1)} %bitcast.23, bf16[1024,128]{1,0:T(8,128)(2,1)S(1)} %bitcast.24, bf16[1024,128]{1,0:T(8,128)(2,1)S(1)} %collective-permute-done.7.came_ref, ...), custom_call_target="tpu_custom_call" | custom-call | tf_op jit(solution)/shard_map/pallas_call | solution.py:294
  (16 shorter events, 0.8 us)
Async XLA Ops:
  0.6 7.7 %copy-start = (bf16[1,2048,128]{2,1,0:T(8,128)(2,1)S(1)}, bf16[1,2048,128]{2,1,0:T(8,128)(2,1)}, u32[]{:S(2)}) copy-start(bf16[1,2048,128]{2,1,0:T(8,128)(2,1)} %param.5) | copy-start | bytes 1572868
  3.8 14.9 %collective-permute-start = (bf16[2,1024,128]{2,1,0:T(8,128)(2,1)S(1)}, bf16[2,1024,128]{2,1,0:T(8,128)(2,1)S(1)}, u32[]{:S(2)}, u32[]{:S(2)}) collective-permute-start(bf16[2,1024,128]{2,1,0:T(8,128)(2,1)S(1)} %get-tuple-element.26), channel_id=1, source_target_pairs={{0,1},{1,0},{2,3},{3,2},{4,5},{5,4},{6,7},{7,6},{8,9},{9,8},{10,11... | collective-permute-start | bytes 1572872 | tf_op jit(solution)/shard_map/ppermute | solution.py:229
  6.8 13.4 %collective-permute-start.1 = (bf16[2,1024,128]{2,1,0:T(8,128)(2,1)S(1)}, bf16[2,1024,128]{2,1,0:T(8,128)(2,1)S(1)}, u32[]{:S(2)}, u32[]{:S(2)}) collective-permute-start(bf16[2,1024,128]{2,1,0:T(8,128)(2,1)S(1)} %get-tuple-element.27), channel_id=1, source_target_pairs={{0,2},{1,3},{2,0},{3,1},{4,6},{5,7},{6,4},{7,5},{8,10},{9,11},{10,... | collective-permute-start | bytes 1572872 | tf_op jit(solution)/shard_map/ppermute | solution.py:229
  8.3 20.3 %copy-start.2 = (f32[1,2048]{1,0:T(1,128)S(1)}, f32[1,2048]{1,0:T(1,128)}, u32[]{:S(2)}) copy-start(f32[1,2048]{1,0:T(1,128)} %refs_2_.1) | copy-start | bytes 24580
  11.7 46.0 %copy-start.1 = (bf16[2048,128]{1,0:T(8,128)(2,1)S(1)}, bf16[2048,128]{1,0:T(8,128)(2,1)}, u32[]{:S(2)}) copy-start(bf16[2048,128]{1,0:T(8,128)(2,1)} %param.9) | copy-start | bytes 1572868
  20.5 6.9 %collective-permute-start.2 = (bf16[1,1024,128]{2,1,0:T(8,128)(2,1)S(1)}, bf16[1,1024,128]{2,1,0:T(8,128)(2,1)S(1)}, u32[]{:S(2)}, u32[]{:S(2)}) collective-permute-start(bf16[1,1024,128]{2,1,0:T(8,128)(2,1)S(1)} %get-tuple-element.28), channel_id=1, source_target_pairs={{0,2},{1,3},{2,0},{3,1},{4,6},{5,7},{6,4},{7,5},{8,10},{9,11},{10,... | collective-permute-start | bytes 786440 | tf_op jit(solution)/shard_map/ppermute | solution.py:229
  22.0 6.6 %collective-permute-start.3 = (bf16[1,1024,128]{2,1,0:T(8,128)(2,1)S(1)}, bf16[1,1024,128]{2,1,0:T(8,128)(2,1)S(1)}, u32[]{:S(2)}, u32[]{:S(2)}) collective-permute-start(bf16[1,1024,128]{2,1,0:T(8,128)(2,1)S(1)} %get-tuple-element.29), channel_id=1, source_target_pairs={{0,1},{1,0},{2,3},{3,2},{4,5},{5,4},{6,7},{7,6},{8,9},{9,8},{10,11... | collective-permute-start | bytes 786440 | tf_op jit(solution)/shard_map/ppermute | solution.py:229
  29.0 4.6 %collective-permute-start.6 = (f32[16,128]{1,0:T(8,128)S(1)}, f32[16,128]{1,0:T(8,128)S(1)}, u32[]{:S(2)}, u32[]{:S(2)}) collective-permute-start(f32[16,128]{1,0:T(8,128)S(1)} %get-tuple-element.32.refs_3_), channel_id=1, source_target_pairs={{0,3},{1,2},{2,1},{3,0},{4,7},{5,6},{6,5},{7,4},{8,11},{9,10},{10,... | collective-permute-start | bytes 24584 | tf_op jit(solution)/shard_map/ppermute | solution.py:229
  29.7 3.9 %collective-permute-start.5 = (f32[16,128]{1,0:T(8,128)S(1)}, f32[16,128]{1,0:T(8,128)S(1)}, u32[]{:S(2)}, u32[]{:S(2)}) collective-permute-start(f32[16,128]{1,0:T(8,128)S(1)} %get-tuple-element.32.refs_3_), channel_id=1, source_target_pairs={{0,2},{1,3},{2,0},{3,1},{4,6},{5,7},{6,4},{7,5},{8,10},{9,11},{10,... | collective-permute-start | bytes 24584 | tf_op jit(solution)/shard_map/ppermute | solution.py:229
  31.1 3.7 %collective-permute-start.4 = (f32[16,128]{1,0:T(8,128)S(1)}, f32[16,128]{1,0:T(8,128)S(1)}, u32[]{:S(2)}, u32[]{:S(2)}) collective-permute-start(f32[16,128]{1,0:T(8,128)S(1)} %get-tuple-element.32.refs_3_), channel_id=1, source_target_pairs={{0,1},{1,0},{2,3},{3,2},{4,5},{5,4},{6,7},{7,6},{8,9},{9,8},{10,11... | collective-permute-start | bytes 24584 | tf_op jit(solution)/shard_map/ppermute | solution.py:229
  35.2 1.6 %collective-permute-start.7 = (bf16[1024,128]{1,0:T(8,128)(2,1)S(1)}, bf16[1024,128]{1,0:T(8,128)(2,1)S(1)}, u32[]{:S(2)}, u32[]{:S(2)}) collective-permute-start(bf16[1024,128]{1,0:T(8,128)(2,1)S(1)} %get-tuple-element.34), channel_id=1, source_target_pairs={{0,4},{4,0},{8,12},{12,8},{16,20},{20,16},{24,28},{28,24},{1,5},{5... | collective-permute-start | bytes 786440 | tf_op jit(solution)/shard_map/ppermute | solution.py:232
  36.9 4.5 %collective-permute-start.8 = (bf16[256,128]{1,0:T(8,128)(2,1)S(1)}, bf16[256,128]{1,0:T(8,128)(2,1)S(1)}, u32[]{:S(2)}, u32[]{:S(2)}) collective-permute-start(bf16[256,128]{1,0:T(8,128)(2,1)S(1)} %get-tuple-element.36), channel_id=1, source_target_pairs={{0,8},{4,12},{8,0},{12,4},{16,24},{20,28},{24,16},{28,20},{1,9},{5... | collective-permute-start | bytes 196616 | tf_op jit(solution)/shard_map/ppermute | solution.py:237
  38.5 7.5 %collective-permute-start.9 = (bf16[256,128]{1,0:T(8,128)(2,1)S(1)}, bf16[256,128]{1,0:T(8,128)(2,1)S(1)}, u32[]{:S(2)}, u32[]{:S(2)}) collective-permute-start(bf16[256,128]{1,0:T(8,128)(2,1)S(1)} %get-tuple-element.37), channel_id=1, source_target_pairs={{0,16},{4,20},{8,24},{12,28},{16,0},{20,4},{24,8},{28,12},{1,17},{... | collective-permute-start | bytes 196616 | tf_op jit(solution)/shard_map/ppermute | solution.py:237
  41.1 6.2 %collective-permute-start.10 = (bf16[256,128]{1,0:T(8,128)(2,1)S(1)}, bf16[256,128]{1,0:T(8,128)(2,1)S(1)}, u32[]{:S(2)}, u32[]{:S(2)}) collective-permute-start(bf16[256,128]{1,0:T(8,128)(2,1)S(1)} %get-tuple-element.38), channel_id=1, source_target_pairs={{0,24},{4,28},{8,16},{12,20},{16,8},{20,12},{24,0},{28,4},{1,25},{... | collective-permute-start | bytes 196616 | tf_op jit(solution)/shard_map/ppermute | solution.py:237
  47.4 4.6 %collective-permute-start.11 = (bf16[256,128]{1,0:T(8,128)(2,1)S(1)}, bf16[256,128]{1,0:T(8,128)(2,1)S(1)}, u32[]{:S(2)}, u32[]{:S(2)}) collective-permute-start(bf16[256,128]{1,0:T(8,128)(2,1)S(1)} %get-tuple-element.40), channel_id=1, source_target_pairs={{0,8},{4,12},{8,0},{12,4},{16,24},{20,28},{24,16},{28,20},{1,9},{5... | collective-permute-start | bytes 196616 | tf_op jit(solution)/shard_map/ppermute | solution.py:237
  48.3 6.2 %collective-permute-start.12 = (bf16[256,128]{1,0:T(8,128)(2,1)S(1)}, bf16[256,128]{1,0:T(8,128)(2,1)S(1)}, u32[]{:S(2)}, u32[]{:S(2)}) collective-permute-start(bf16[256,128]{1,0:T(8,128)(2,1)S(1)} %get-tuple-element.41), channel_id=1, source_target_pairs={{0,16},{4,20},{8,24},{12,28},{16,0},{20,4},{24,8},{28,12},{1,17},{... | collective-permute-start | bytes 196616 | tf_op jit(solution)/shard_map/ppermute | solution.py:237
  50.0 6.1 %collective-permute-start.13 = (bf16[256,128]{1,0:T(8,128)(2,1)S(1)}, bf16[256,128]{1,0:T(8,128)(2,1)S(1)}, u32[]{:S(2)}, u32[]{:S(2)}) collective-permute-start(bf16[256,128]{1,0:T(8,128)(2,1)S(1)} %get-tuple-element.42), channel_id=1, source_target_pairs={{0,24},{4,28},{8,16},{12,20},{16,8},{20,12},{24,0},{28,4},{1,25},{... | collective-permute-start | bytes 196616 | tf_op jit(solution)/shard_map/ppermute | solution.py:237
  56.1 1.6 %collective-permute-start.14 = (bf16[1024,128]{1,0:T(8,128)(2,1)S(1)}, bf16[1024,128]{1,0:T(8,128)(2,1)S(1)}, u32[]{:S(2)}, u32[]{:S(2)}) collective-permute-start(bf16[1024,128]{1,0:T(8,128)(2,1)S(1)} %bitcast.25), channel_id=1, source_target_pairs={{0,4},{4,0},{8,12},{12,8},{16,20},{20,16},{24,28},{28,24},{1,5},{5... | collective-permute-start | bytes 786440 | tf_op jit(solution)/shard_map/ppermute | solution.py:232

commit v4 on v3

--- a/solution.py
+++ b/solution.py
@@ -8,7 +8,7 @@
 epsilon = 1e-05
 F32 = jnp.float32
 BF16 = jnp.bfloat16
-BOTH = ("section", "tensor")
+PIECES = 2
 WHOLE = pl.BlockSpec(memory_space=pltpu.VMEM)
 LIMIT = pltpu.CompilerParams(vmem_limit_bytes=16 << 20)
 
@@ -42,32 +42,39 @@
         ).astype(out.dtype)
 
 
+def tile_of(part):
+    return min(part, 128)
+
+
+def wide(gains_ref, start, width, tokens):
+    return jnp.broadcast_to(gains_ref[:, start : start + width], (tokens, width)).T
+
+
 def keep_kernel(first_ref, second_ref, grads_ref, inputs_ref, first_out, second_out, squares_out):
     rows, tokens = inputs_ref.shape
-    width = min(rows, 128)
+    width = tile_of(rows)
 
     @pl.when(pl.program_id(0) == 0)
     def _():
-        def step(i, total):
-            at = pl.ds(pl.multiple_of(i * width, width), width)
-            value = inputs_ref[at].astype(F32)
-            return total + jnp.sum((value * value).reshape(width // 8, 8, tokens), axis=0)
-
-        squares_out[...] = lax.fori_loop(0, rows // width, step, jnp.zeros((8, tokens), F32))
+        total = jnp.zeros((8, tokens), F32)
+        for start in range(0, rows, width):
+            value = inputs_ref[pl.ds(start, width)].astype(F32)
+            total = total + jnp.sum((value * value).reshape(width // 8, 8, tokens), axis=0)
+        squares_out[...] = total
 
     multiply(first_ref, second_ref, grads_ref, first_out, second_out)
 
 
-def product(base, weight, grads, count, extra=()):
+def product(base, weight, grads, count, extra=(), pieces=1, piece=0):
     features, depth = weight.shape
     tokens = grads.shape[0]
-    part = features // count // 2
+    part = features // count // 2 // pieces
     units = count // 2
 
     def rows_of(stream):
         def at(i):
             block = lax.axis_index("tensor") ^ block_of(stream, i + base, count)
-            return (block * 2 + stream, 0)
+            return ((block * 2 + stream) * pieces + piece, 0)
 
         return at
 
@@ -96,58 +103,80 @@
     )(far(weight), far(weight), far(grads), *extra)
 
 
-def add_kernel(*refs):
+def terms_of(refs, pieces, stream, piece):
+    kept, came = refs[stream], refs[2 + 2 * piece + stream :: 2 * pieces]
+    return [(kept, piece * (kept.shape[1] // pieces))] + [(c, 0) for c in came]
+
+
+def add_kernel(piece, pieces, *refs):
     outs = refs[-2:]
     for h, out in enumerate(outs):
-        units = out.shape[0]
-        parts = refs[h : len(refs) - 2 : 2]
-        rows = min(out.shape[1], 64)
-
-        def step(i, _):
-            at = pl.ds(pl.multiple_of(i * rows, rows), rows)
-            for u in range(units):
-                total = sum(p[u + units, at].astype(F32) for p in parts)
-                out[u, at] = total.astype(out.dtype)
-            return 0
-
-        lax.fori_loop(0, out.shape[1] // rows, step, 0)
-
-
-def tile_of(part):
-    return min(part, 128)
-
-
-def wide(gains_ref, start, width, tokens):
-    return jnp.broadcast_to(gains_ref[:, start : start + width], (tokens, width)).T
-
-
-def sum_kernel(held, *refs):
-    blocks = refs[: 2 * held]
-    inputs_ref, gains_ref, squares_ref, partial_out, sums_out = refs[2 * held :]
-    part, tokens = blocks[0].shape[1:]
-    width = tile_of(part)
+        units, size, _ = out.shape
+        width = tile_of(size)
+        kept = refs[h]
+        parts = [(kept, piece * size)] + [(c, 0) for c in refs[2 + h : -2 : 2]]
+        for u in range(units):
+            for start in range(0, size, width):
+                total = sum(p[u + units, pl.ds(first + start, width)].astype(F32) for p, first in parts)
+                out[u, pl.ds(start, width)] = total.astype(out.dtype)
+
+
+def last_add_kernel(pieces, inputs_ref, gains_ref, *refs):
+    add_kernel(0, pieces, *refs[:-2], *(out.at[:1] for out in refs[-2:]))
+    rows, tokens = inputs_ref.shape
+    part = rows // 2
+    for h, out in enumerate(refs[-2:]):
+        size = out.shape[1]
+        width = tile_of(size)
+        for start in range(0, size, width):
+            row = (h + 1) * part - size + start
+            gained = inputs_ref[pl.ds(row, width)].astype(F32) * wide(gains_ref, row, width, tokens)
+            out[1, pl.ds(start, width)] = gained.astype(out.dtype)
+
+
+def inner_kernel(pieces, *refs):
+    held, (inputs_ref, gains_ref, squares_ref, sums_out) = refs[:-4], refs[-4:]
+    gained = held[-2:]
+    part = held[0].shape[1]
+    tokens = inputs_ref.shape[1]
+    size = part // pieces
+    width = tile_of(size)
     inner = jnp.zeros((8, tokens), F32)
-    for start in range(0, 2 * part, width):
-        h, at = start // part, pl.ds(start % part, width)
-        total = sum(b[0, at].astype(F32) for b in blocks[h::2])
-        partial_out[h, at] = total
-        product = total * wide(gains_ref, start, width, tokens) * inputs_ref[pl.ds(start, width)].astype(F32)
-        inner = inner + jnp.sum(product.reshape(width // 8, 8, tokens), axis=0)
+    for h in range(2):
+        for a in range(pieces):
+            parts = terms_of(held, pieces, h, a)
+            for start in range(0, size, width):
+                row = h * part + a * size + start
+                factor = wide(gains_ref, row, width, tokens) * inputs_ref[pl.ds(row, width)].astype(F32)
+                product = sum(p[0, pl.ds(first + start, width)].astype(F32) for p, first in parts) * factor
+                if a == pieces - 1:
+                    factor = gained[h][1, pl.ds(start, width)].astype(F32)
+                    total = sum(p[1, pl.ds(first + start, width)].astype(F32) for p, first in parts)
+                    product = product + total * factor
+                inner = inner + jnp.sum(product.reshape(width // 8, 8, tokens), axis=0)
     sums_out[...] = jnp.concatenate([squares_ref[...], inner])
 
 
-def branch_kernel(features, partial_ref, inputs_ref, gains_ref, *refs):
-    sums, (branch_out, other_out, upside_out) = refs[:-3], refs[-3:]
-    part, tokens = partial_ref.shape[1:]
-    width = tile_of(part)
+def branch_kernel(features, pieces, held, *refs):
+    blocks, (inputs_ref, gains_ref, *sums) = refs[:held], refs[held:-4]
+    partial_out, branch_out, other_out, upside_out = refs[-4:]
+    part, tokens = partial_out.shape[1:]
+    size = part // pieces
+    width = tile_of(size)
     both = jnp.sum(sum(s[...] for s in sums).reshape(2, 8, tokens), axis=1)
     upside = lax.rsqrt(both[:1] / features + epsilon)
     factor = both[1:] * (upside * upside * upside / features)
     upside_out[...] = jnp.broadcast_to(upside, upside_out.shape)
-    for start in range(0, 2 * part, width):
-        h, at = start // part, pl.ds(start % part, width)
-        weighted = partial_ref[h, at] * wide(gains_ref, start, width, tokens)
-        branch_out[h, at] = weighted * upside - inputs_ref[pl.ds(start, width)].astype(F32) * factor
+    for h in range(2):
+        for a in range(pieces):
+            parts = terms_of(blocks, pieces, h, a)
+            for start in range(0, size, width):
+                at = pl.ds(a * size + start, width)
+                row = h * part + a * size + start
+                total = sum(p[0, pl.ds(first + start, width)].astype(F32) for p, first in parts)
+                partial_out[h, at] = total
+                weighted = total * wide(gains_ref, row, width, tokens)
+                branch_out[h, at] = weighted * upside - inputs_ref[pl.ds(row, width)].astype(F32) * factor
     core = lax.axis_index("section") & 1
     other_out[...] = branch_out[1 - core].astype(other_out.dtype)
 
@@ -237,35 +266,46 @@
         return lax.ppermute(value, "section", [(s, s ^ (2 * distance)) for s in range(layers)])
 
     units = count // 2
-    sent = product(units, weight, grads, count)
-    came = [exchange(sent[h], mask_of(h, 0, count)) for h in range(2)]
+    sent = [product(units, weight, grads, count, (), PIECES, a) for a in range(PIECES)]
+    held = [[exchange(sent[a][h], mask_of(h, 0, count)) for h in range(2)] for a in range(PIECES)]
     *kept, squares = product(0, weight, grads, count, (inputs,))
 
-    held = [*kept, *came]
+    size = part // PIECES
     for step in range(1, steps):
         units //= 2
-        total = call(add_kernel, [pltpu.VMEM((units, part, tokens), BF16)] * 2, *held)
-        held += [exchange(total[h], mask_of(h, step, count)) for h in range(2)]
-    partial_value, sums = call(
-        lambda *refs: sum_kernel(len(held) // 2, *refs),
-        [pltpu.VMEM((2, part, tokens), F32), pltpu.VMEM((16, tokens), F32)],
-        *held,
+        for a in range(PIECES):
+            last = step == steps - 1 and a == 0
+            outs = [pltpu.VMEM((units + last, size, tokens), BF16)] * 2
+            if last:
+                kernel = lambda *refs: last_add_kernel(PIECES, *refs)
+                total = call(kernel, outs, inputs, norm_gains, *kept, *held[a])
+            else:
+                total = call(lambda *refs: add_kernel(a, PIECES, *refs), outs, *kept, *held[a])
+            held[a] = held[a] + [exchange(total[h], mask_of(h, step, count)) for h in range(2)]
+    arrived = [v for step in range(steps) for a in range(PIECES) for v in held[a][2 * step : 2 * step + 2]]
+    sums = call(
+        lambda *refs: inner_kernel(PIECES, *refs),
+        pltpu.VMEM((16, tokens), F32),
+        *kept,
+        *arrived[:-2],
         inputs,
         norm_gains,
         squares,
     )
-
     sums, low = [sums], 1
     while low < count:
         group = [low] if 2 * low >= count else [low, 2 * low, 3 * low]
         total = sum(sums)
         sums = [total] + [exchange(total, m) for m in group]
         low *= 4
+
     half = pltpu.VMEM((part, tokens), BF16)
-    branch, other, upside = call(
-        lambda *refs: branch_kernel(features, *refs),
-        [pltpu.VMEM((2, part, tokens), F32), half, pltpu.VMEM((8, tokens), F32)],
-        partial_value,
+    full = pltpu.VMEM((2, part, tokens), F32)
+    held = [*kept, *arrived]
+    partial_value, branch, other, upside = call(
+        lambda *refs: branch_kernel(features, PIECES, len(held), *refs),
+        [full, full, half, pltpu.VMEM((8, tokens), F32)],
+        *held,
         inputs,
         norm_gains,
         *sums,

time: 58.9 us -> 56.3 us (0.956)
  waiting for transfers between devices: 29 us -> 22.4 us
  starting transfers between devices: 19.2 us -> 22 us
  Pallas kernels: 8.86 us -> 10 us
    ppermute x7 -> x11, waiting for transfers between devices: 16.7 us -> 10.2 us  [exchange(): return lax.ppermute(value, 'tensor', [(i, i ^ mask) for i in range(count)])]
    ppermute x7 -> x11, starting transfers between devices: 10.2 us -> 13 us  [exchange(): return lax.ppermute(value, 'tensor', [(i, i ^ mask) for i in range(count)])]
    pallas_call x2 -> x3, Pallas kernels: 6.51 us -> 7.56 us  [product(): pl.pallas_call(keep_kernel if extra else multiply, out_shape=out_shape, g...]
    pallas_call x5 -> x6, Pallas kernels: 1.22 us -> 1.31 us  [call(): pl.pallas_call(kernel, out_shape=out_shape, in_specs=[WHOLE] * len(arrays...]
  transfers between devices with their start and end apart: 15 -> 19, of which waited for: 13 -> 14; matrix products, arithmetic and copies ran while one was open for 2% -> 2% of each run, Pallas kernels for 6% -> 11%
where the time goes in v4:
time: 56.3 us; the launch traced here: 56.2 us
  waiting for transfers between devices  22.4 us (40%)
  starting transfers between devices  22 us (39%)
  Pallas kernels  10 us (18%)
  between operations  0.74 us (1%)
  local copies, waits for them, and re-layouts  0.63 us (1%)
    ppermute x11, starting transfers between devices, exchange(): return lax.ppermute(value, 'tensor', [(i, i ^ mask) for i in range(count)])  13 us
    ppermute x11, waiting for transfers between devices, exchange(): return lax.ppermute(value, 'tensor', [(i, i ^ mask) for i in range(count)])  10.2 us
    ppermute x6, waiting for transfers between devices, across(): lax.ppermute(value, 'section', [(s, s ^ 2 * distance) for s in range(laye...  10.2 us
    ppermute x6, starting transfers between devices, across(): lax.ppermute(value, 'section', [(s, s ^ 2 * distance) for s in range(laye...  8.9 us
    pallas_call x3, Pallas kernels, product(): pl.pallas_call(keep_kernel if extra else multiply, out_shape=out_shape, g...  7.56 us
    ppermute x2, waiting for transfers between devices, swap(): return lax.ppermute(value, 'section', [(s, s ^ 1) for s in range(layers)])  2.05 us
    pallas_call x6, Pallas kernels, call(): pl.pallas_call(kernel, out_shape=out_shape, in_specs=[WHOLE] * len(arrays...  1.31 us
  transfers between devices with their start and end apart: 19, of which 14 were waited for; matrix products, arithmetic and copies ran while one was open for 2% of the time, Pallas kernels for 11%

profile of v4, /device:TPU:0, one launch (start us, length us, event | category | flops | bytes accessed | tf_op | source)
XLA Modules:
  0.0 56.2 jit_solution(17681193594610503673)
XLA Ops:
  0.6 2.2 %shard_map.69 = (bf16[2,512,128]{2,1,0:T(8,128)(2,1)S(1)}, bf16[2,512,128]{2,1,0:T(8,128)(2,1)S(1)}) custom-call(bf16[8192,512]{1,0:T(8,128)(2,1)} %bitcast.27, bf16[8192,512]{1,0:T(8,128)(2,1)} %bitcast.28, bf16[128,512]{1,0:T(8,128)(2,1)} %bitcast.33), custom_call_target="tpu_custom_call" | custom-call | flops 268435456 | bytes 2621440 | tf_op jit(solution)/shard_map/pallas_call | solution.py:86
  2.9 3.0 %collective-permute-start = (bf16[2,512,128]{2,1,0:T(8,128)(2,1)S(1)}, bf16[2,512,128]{2,1,0:T(8,128)(2,1)S(1)}, u32[]{:S(2)}, u32[]{:S(2)}) collective-permute-start(bf16[2,512,128]{2,1,0:T(8,128)(2,1)S(1)} %get-tuple-element.29), channel_id=1, source_target_pairs={{0,1},{1,0},{2,3},{3,2},{4,5},{5,4},{6,7},{7,6},{8,9},{9,8},{10,11... | collective-permute-start | bytes 786440 | tf_op jit(solution)/shard_map/ppermute | solution.py:258
  5.9 1.5 %collective-permute-start.1 = (bf16[2,512,128]{2,1,0:T(8,128)(2,1)S(1)}, bf16[2,512,128]{2,1,0:T(8,128)(2,1)S(1)}, u32[]{:S(2)}, u32[]{:S(2)}) collective-permute-start(bf16[2,512,128]{2,1,0:T(8,128)(2,1)S(1)} %get-tuple-element.30), channel_id=1, source_target_pairs={{0,2},{1,3},{2,0},{3,1},{4,6},{5,7},{6,4},{7,5},{8,10},{9,11},{10,... | collective-permute-start | bytes 786440 | tf_op jit(solution)/shard_map/ppermute | solution.py:258
  7.4 2.2 %shard_map.70 = (bf16[2,512,128]{2,1,0:T(8,128)(2,1)S(1)}, bf16[2,512,128]{2,1,0:T(8,128)(2,1)S(1)}) custom-call(bf16[8192,512]{1,0:T(8,128)(2,1)} %bitcast.29, bf16[8192,512]{1,0:T(8,128)(2,1)} %bitcast.30, bf16[128,512]{1,0:T(8,128)(2,1)} %bitcast.34), custom_call_target="tpu_custom_call" | custom-call | flops 268435456 | bytes 2621440 | tf_op jit(solution)/shard_map/pallas_call | solution.py:86
  9.6 0.6 %collective-permute-start.2 = (bf16[2,512,128]{2,1,0:T(8,128)(2,1)S(1)}, bf16[2,512,128]{2,1,0:T(8,128)(2,1)S(1)}, u32[]{:S(2)}, u32[]{:S(2)}) collective-permute-start(bf16[2,512,128]{2,1,0:T(8,128)(2,1)S(1)} %get-tuple-element.31), channel_id=1, source_target_pairs={{0,1},{1,0},{2,3},{3,2},{4,5},{5,4},{6,7},{7,6},{8,9},{9,8},{10,11... | collective-permute-start | bytes 786440 | tf_op jit(solution)/shard_map/ppermute | solution.py:258
  10.3 3.2 %shard_map.68 = (bf16[2,1024,128]{2,1,0:T(8,128)(2,1)S(1)}, bf16[2,1024,128]{2,1,0:T(8,128)(2,1)S(1)}, f32[8,128]{1,0:T(8,128)S(1)}) custom-call(bf16[8192,512]{1,0:T(8,128)(2,1)} %bitcast.31, bf16[8192,512]{1,0:T(8,128)(2,1)} %bitcast.32, bf16[128,512]{1,0:T(8,128)(2,1)} %bitcast.35, bf16[2048,128]{1,0:T(8,128)(2,1)S(1)} %bitcast.16), custom_call_target="tpu_custom_call" | custom-call | flops 536870912 | bytes 5242880 | tf_op jit(solution)/shard_map/pallas_call | solution.py:86
  13.5 1.6 %collective-permute-done.1.refs_5_.refs_3_ = bf16[2,512,128]{2,1,0:T(8,128)(2,1)S(1)} collective-permute-done((bf16[2,512,128]{2,1,0:T(8,128)(2,1)S(1)}, bf16[2,512,128]{2,1,0:T(8,128)(2,1)S(1)}, u32[]{:S(2)}, u32[]{:S(2)}) %collective-permute-start.1) | collective-permute-done | bytes 262176 | tf_op jit(solution)/shard_map/ppermute | solution.py:258
  15.3 1.6 %collective-permute-start.4 = (bf16[2,512,128]{2,1,0:T(8,128)(2,1)S(1)}, bf16[2,512,128]{2,1,0:T(8,128)(2,1)S(1)}, u32[]{:S(2)}, u32[]{:S(2)}) collective-permute-start(bf16[2,512,128]{2,1,0:T(8,128)(2,1)S(1)} %get-tuple-element.33), channel_id=1, source_target_pairs={{0,2},{1,3},{2,0},{3,1},{4,6},{5,7},{6,4},{7,5},{8,10},{9,11},{10,... | collective-permute-start | bytes 786440 | tf_op jit(solution)/shard_map/ppermute | solution.py:258
  16.9 0.5 collective-permute-start.5
  17.4 1.3 %collective-permute-done.2.refs_2_.refs_4_ = bf16[2,512,128]{2,1,0:T(8,128)(2,1)S(1)} collective-permute-done((bf16[2,512,128]{2,1,0:T(8,128)(2,1)S(1)}, bf16[2,512,128]{2,1,0:T(8,128)(2,1)S(1)}, u32[]{:S(2)}, u32[]{:S(2)}) %collective-permute-start.2) | collective-permute-done | bytes 262176 | tf_op jit(solution)/shard_map/ppermute | solution.py:258
  18.8 2.0 %collective-permute-done.3.refs_3_.refs_5_ = bf16[2,512,128]{2,1,0:T(8,128)(2,1)S(1)} collective-permute-done((bf16[2,512,128]{2,1,0:T(8,128)(2,1)S(1)}, bf16[2,512,128]{2,1,0:T(8,128)(2,1)S(1)}, u32[]{:S(2)}, u32[]{:S(2)}) %collective-permute-start.3) | collective-permute-done | bytes 262176 | tf_op jit(solution)/shard_map/ppermute | solution.py:258
  20.8 1.6 %collective-permute-start.6 = (bf16[1,512,128]{2,1,0:T(8,128)(2,1)S(1)}, bf16[1,512,128]{2,1,0:T(8,128)(2,1)S(1)}, u32[]{:S(2)}, u32[]{:S(2)}) collective-permute-start(bf16[1,512,128]{2,1,0:T(8,128)(2,1)S(1)} %get-tuple-element.35), channel_id=1, source_target_pairs={{0,2},{1,3},{2,0},{3,1},{4,6},{5,7},{6,4},{7,5},{8,10},{9,11},{10,... | collective-permute-start | bytes 393224 | tf_op jit(solution)/shard_map/ppermute | solution.py:258
  22.4 0.5 collective-permute-start.7
  22.9 3.4 %collective-permute-done.4.refs_6_ = bf16[2,512,128]{2,1,0:T(8,128)(2,1)S(1)} collective-permute-done((bf16[2,512,128]{2,1,0:T(8,128)(2,1)S(1)}, bf16[2,512,128]{2,1,0:T(8,128)(2,1)S(1)}, u32[]{:S(2)}, u32[]{:S(2)}) %collective-permute-start.4) | collective-permute-done | bytes 262176 | tf_op jit(solution)/shard_map/ppermute | solution.py:258
  26.7 1.6 %collective-permute-start.10 = (f32[16,128]{1,0:T(8,128)S(1)}, f32[16,128]{1,0:T(8,128)S(1)}, u32[]{:S(2)}, u32[]{:S(2)}) collective-permute-start(f32[16,128]{1,0:T(8,128)S(1)} %shard_map.73.refs_12_), channel_id=1, source_target_pairs={{0,3},{1,2},{2,1},{3,0},{4,7},{5,6},{6,5},{7,4},{8,11},{9,10},{10,... | collective-permute-start | bytes 24584 | tf_op jit(solution)/shard_map/ppermute | solution.py:258
  28.5 1.8 %collective-permute-start.8 = (f32[16,128]{1,0:T(8,128)S(1)}, f32[16,128]{1,0:T(8,128)S(1)}, u32[]{:S(2)}, u32[]{:S(2)}) collective-permute-start(f32[16,128]{1,0:T(8,128)S(1)} %shard_map.73.refs_12_), channel_id=1, source_target_pairs={{0,1},{1,0},{2,3},{3,2},{4,5},{5,4},{6,7},{7,6},{8,9},{9,8},{10,11... | collective-permute-start | bytes 24584 | tf_op jit(solution)/shard_map/ppermute | solution.py:258
  30.3 1.1 %collective-permute-done.10.refs_15_ = f32[16,128]{1,0:T(8,128)S(1)} collective-permute-done((f32[16,128]{1,0:T(8,128)S(1)}, f32[16,128]{1,0:T(8,128)S(1)}, u32[]{:S(2)}, u32[]{:S(2)}) %collective-permute-start.10) | collective-permute-done | bytes 8224 | tf_op jit(solution)/shard_map/ppermute | solution.py:258
  31.3 0.6 %collective-permute-done.9.refs_14_ = f32[16,128]{1,0:T(8,128)S(1)} collective-permute-done((f32[16,128]{1,0:T(8,128)S(1)}, f32[16,128]{1,0:T(8,128)S(1)}, u32[]{:S(2)}, u32[]{:S(2)}) %collective-permute-start.9) | collective-permute-done | bytes 8224 | tf_op jit(solution)/shard_map/ppermute | solution.py:258
  32.1 0.5 shard_map.74
  32.7 1.5 %collective-permute-done.11.came_ref = bf16[1024,128]{1,0:T(8,128)(2,1)S(1)} collective-permute-done((bf16[1024,128]{1,0:T(8,128)(2,1)S(1)}, bf16[1024,128]{1,0:T(8,128)(2,1)S(1)}, u32[]{:S(2)}, u32[]{:S(2)}) %collective-permute-start.11) | collective-permute-done | bytes 262176 | tf_op jit(solution)/shard_map/ppermute | solution.py:261
  34.3 1.6 %collective-permute-start.12 = (bf16[256,128]{1,0:T(8,128)(2,1)S(1)}, bf16[256,128]{1,0:T(8,128)(2,1)S(1)}, u32[]{:S(2)}, u32[]{:S(2)}) collective-permute-start(bf16[256,128]{1,0:T(8,128)(2,1)S(1)} %get-tuple-element.41), channel_id=1, source_target_pairs={{0,8},{4,12},{8,0},{12,4},{16,24},{20,28},{24,16},{28,20},{1,9},{5... | collective-permute-start | bytes 196616 | tf_op jit(solution)/shard_map/ppermute | solution.py:266
  35.9 2.6 %collective-permute-start.13 = (bf16[256,128]{1,0:T(8,128)(2,1)S(1)}, bf16[256,128]{1,0:T(8,128)(2,1)S(1)}, u32[]{:S(2)}, u32[]{:S(2)}) collective-permute-start(bf16[256,128]{1,0:T(8,128)(2,1)S(1)} %get-tuple-element.42), channel_id=1, source_target_pairs={{0,16},{4,20},{8,24},{12,28},{16,0},{20,4},{24,8},{28,12},{1,17},{... | collective-permute-start | bytes 196616 | tf_op jit(solution)/shard_map/ppermute | solution.py:266
  38.7 4.7 %collective-permute-done.13.refs_2_ = bf16[256,128]{1,0:T(8,128)(2,1)S(1)} collective-permute-done((bf16[256,128]{1,0:T(8,128)(2,1)S(1)}, bf16[256,128]{1,0:T(8,128)(2,1)S(1)}, u32[]{:S(2)}, u32[]{:S(2)}) %collective-permute-start.13) | collective-permute-done | bytes 65568 | tf_op jit(solution)/shard_map/ppermute | solution.py:266
  43.5 1.2 %collective-permute-done.14.refs_3_ = bf16[256,128]{1,0:T(8,128)(2,1)S(1)} collective-permute-done((bf16[256,128]{1,0:T(8,128)(2,1)S(1)}, bf16[256,128]{1,0:T(8,128)(2,1)S(1)}, u32[]{:S(2)}, u32[]{:S(2)}) %collective-permute-start.14) | collective-permute-done | bytes 65568 | tf_op jit(solution)/shard_map/ppermute | solution.py:266
  44.8 0.9 %collective-permute-start.15 = (bf16[256,128]{1,0:T(8,128)(2,1)S(1)}, bf16[256,128]{1,0:T(8,128)(2,1)S(1)}, u32[]{:S(2)}, u32[]{:S(2)}) collective-permute-start(bf16[256,128]{1,0:T(8,128)(2,1)S(1)} %get-tuple-element.45), channel_id=1, source_target_pairs={{0,8},{4,12},{8,0},{12,4},{16,24},{20,28},{24,16},{28,20},{1,9},{5... | collective-permute-start | bytes 196616 | tf_op jit(solution)/shard_map/ppermute | solution.py:266
  45.7 1.7 %collective-permute-start.16 = (bf16[256,128]{1,0:T(8,128)(2,1)S(1)}, bf16[256,128]{1,0:T(8,128)(2,1)S(1)}, u32[]{:S(2)}, u32[]{:S(2)}) collective-permute-start(bf16[256,128]{1,0:T(8,128)(2,1)S(1)} %get-tuple-element.46), channel_id=1, source_target_pairs={{0,16},{4,20},{8,24},{12,28},{16,0},{20,4},{24,8},{28,12},{1,17},{... | collective-permute-start | bytes 196616 | tf_op jit(solution)/shard_map/ppermute | solution.py:266
  47.4 1.8 %collective-permute-start.17 = (bf16[256,128]{1,0:T(8,128)(2,1)S(1)}, bf16[256,128]{1,0:T(8,128)(2,1)S(1)}, u32[]{:S(2)}, u32[]{:S(2)}) collective-permute-start(bf16[256,128]{1,0:T(8,128)(2,1)S(1)} %get-tuple-element.47), channel_id=1, source_target_pairs={{0,24},{4,28},{8,16},{12,20},{16,8},{20,12},{24,0},{28,4},{1,25},{... | collective-permute-start | bytes 196616 | tf_op jit(solution)/shard_map/ppermute | solution.py:266
  49.4 2.6 %collective-permute-done.16.refs_2_ = bf16[256,128]{1,0:T(8,128)(2,1)S(1)} collective-permute-done((bf16[256,128]{1,0:T(8,128)(2,1)S(1)}, bf16[256,128]{1,0:T(8,128)(2,1)S(1)}, u32[]{:S(2)}, u32[]{:S(2)}) %collective-permute-start.16) | collective-permute-done | bytes 65568 | tf_op jit(solution)/shard_map/ppermute | solution.py:266
  51.9 1.5 %collective-permute-done.17.refs_3_ = bf16[256,128]{1,0:T(8,128)(2,1)S(1)} collective-permute-done((bf16[256,128]{1,0:T(8,128)(2,1)S(1)}, bf16[256,128]{1,0:T(8,128)(2,1)S(1)}, u32[]{:S(2)}, u32[]{:S(2)}) %collective-permute-start.17) | collective-permute-done | bytes 65568 | tf_op jit(solution)/shard_map/ppermute | solution.py:266
  54.0 0.6 %copy.7 = f32[1,1,2,1024]{3,1,2,0:T(1,128)} copy(f32[1,1,2,1024]{3,2,1,0:T(2,128)S(1)} %bitcast.37) | data formatting | bytes 16384
  54.6 0.5 collective-permute-done.18.mate_ref
  55.2 1.0 %shard_map.78 = bf16[2,1024,128]{2,1,0:T(8,128)(2,1)} custom-call(f32[2,1024,128]{2,1,0:T(8,128)S(1)} %get-tuple-element.38.branch_ref, bf16[2,1024,128]{2,1,0:T(8,128)(2,1)S(1)} %bitcast.24, bf16[1024,128]{1,0:T(8,128)(2,1)S(1)} %bitcast.25, bf16[1024,128]{1,0:T(8,128)(2,1)S(1)} %collective-permute-done.11.came_ref, ...), custom_call_target="tpu_custom_call" | custom-call | tf_op jit(solution)/shard_map/pallas_call | solution.py:334
  (26 shorter events, 2.4 us)
Async XLA Ops:
  2.9 10.6 %collective-permute-start = (bf16[2,512,128]{2,1,0:T(8,128)(2,1)S(1)}, bf16[2,512,128]{2,1,0:T(8,128)(2,1)S(1)}, u32[]{:S(2)}, u32[]{:S(2)}) collective-permute-start(bf16[2,512,128]{2,1,0:T(8,128)(2,1)S(1)} %get-tuple-element.29), channel_id=1, source_target_pairs={{0,1},{1,0},{2,3},{3,2},{4,5},{5,4},{6,7},{7,6},{8,9},{9,8},{10,11... | collective-permute-start | bytes 786440 | tf_op jit(solution)/shard_map/ppermute | solution.py:258
  5.9 4.4 %copy-start = (bf16[1,2048,128]{2,1,0:T(8,128)(2,1)S(1)}, bf16[1,2048,128]{2,1,0:T(8,128)(2,1)}, u32[]{:S(2)}) copy-start(bf16[1,2048,128]{2,1,0:T(8,128)(2,1)} %param.5) | copy-start | bytes 1572868
  5.9 9.2 %collective-permute-start.1 = (bf16[2,512,128]{2,1,0:T(8,128)(2,1)S(1)}, bf16[2,512,128]{2,1,0:T(8,128)(2,1)S(1)}, u32[]{:S(2)}, u32[]{:S(2)}) collective-permute-start(bf16[2,512,128]{2,1,0:T(8,128)(2,1)S(1)} %get-tuple-element.30), channel_id=1, source_target_pairs={{0,2},{1,3},{2,0},{3,1},{4,6},{5,7},{6,4},{7,5},{8,10},{9,11},{10,... | collective-permute-start | bytes 786440 | tf_op jit(solution)/shard_map/ppermute | solution.py:258
  9.6 9.2 %collective-permute-start.2 = (bf16[2,512,128]{2,1,0:T(8,128)(2,1)S(1)}, bf16[2,512,128]{2,1,0:T(8,128)(2,1)S(1)}, u32[]{:S(2)}, u32[]{:S(2)}) collective-permute-start(bf16[2,512,128]{2,1,0:T(8,128)(2,1)S(1)} %get-tuple-element.31), channel_id=1, source_target_pairs={{0,1},{1,0},{2,3},{3,2},{4,5},{5,4},{6,7},{7,6},{8,9},{9,8},{10,11... | collective-permute-start | bytes 786440 | tf_op jit(solution)/shard_map/ppermute | solution.py:258
  10.2 10.6 %collective-permute-start.3 = (bf16[2,512,128]{2,1,0:T(8,128)(2,1)S(1)}, bf16[2,512,128]{2,1,0:T(8,128)(2,1)S(1)}, u32[]{:S(2)}, u32[]{:S(2)}) collective-permute-start(bf16[2,512,128]{2,1,0:T(8,128)(2,1)S(1)} %get-tuple-element.32), channel_id=1, source_target_pairs={{0,2},{1,3},{2,0},{3,1},{4,6},{5,7},{6,4},{7,5},{8,10},{9,11},{10,... | collective-permute-start | bytes 786440 | tf_op jit(solution)/shard_map/ppermute | solution.py:258
  10.3 4.8 %copy-start.2 = (f32[1,2048]{1,0:T(1,128)S(1)}, f32[1,2048]{1,0:T(1,128)}, u32[]{:S(2)}) copy-start(f32[1,2048]{1,0:T(1,128)} %refs_11_.1) | copy-start | bytes 24580
  13.4 41.7 %copy-start.1 = (bf16[2048,128]{1,0:T(8,128)(2,1)S(1)}, bf16[2048,128]{1,0:T(8,128)(2,1)}, u32[]{:S(2)}) copy-start(bf16[2048,128]{1,0:T(8,128)(2,1)} %param.9) | copy-start | bytes 1572868
  15.3 10.9 %collective-permute-start.4 = (bf16[2,512,128]{2,1,0:T(8,128)(2,1)S(1)}, bf16[2,512,128]{2,1,0:T(8,128)(2,1)S(1)}, u32[]{:S(2)}, u32[]{:S(2)}) collective-permute-start(bf16[2,512,128]{2,1,0:T(8,128)(2,1)S(1)} %get-tuple-element.33), channel_id=1, source_target_pairs={{0,2},{1,3},{2,0},{3,1},{4,6},{5,7},{6,4},{7,5},{8,10},{9,11},{10,... | collective-permute-start | bytes 786440 | tf_op jit(solution)/shard_map/ppermute | solution.py:258
  16.9 9.4 %collective-permute-start.5 = (bf16[2,512,128]{2,1,0:T(8,128)(2,1)S(1)}, bf16[2,512,128]{2,1,0:T(8,128)(2,1)S(1)}, u32[]{:S(2)}, u32[]{:S(2)}) collective-permute-start(bf16[2,512,128]{2,1,0:T(8,128)(2,1)S(1)} %get-tuple-element.34), channel_id=1, source_target_pairs={{0,1},{1,0},{2,3},{3,2},{4,5},{5,4},{6,7},{7,6},{8,9},{9,8},{10,11... | collective-permute-start | bytes 786440 | tf_op jit(solution)/shard_map/ppermute | solution.py:258
  20.8 9.5 %collective-permute-start.6 = (bf16[1,512,128]{2,1,0:T(8,128)(2,1)S(1)}, bf16[1,512,128]{2,1,0:T(8,128)(2,1)S(1)}, u32[]{:S(2)}, u32[]{:S(2)}) collective-permute-start(bf16[1,512,128]{2,1,0:T(8,128)(2,1)S(1)} %get-tuple-element.35), channel_id=1, source_target_pairs={{0,2},{1,3},{2,0},{3,1},{4,6},{5,7},{6,4},{7,5},{8,10},{9,11},{10,... | collective-permute-start | bytes 393224 | tf_op jit(solution)/shard_map/ppermute | solution.py:258
  22.4 7.9 %collective-permute-start.7 = (bf16[1,512,128]{2,1,0:T(8,128)(2,1)S(1)}, bf16[1,512,128]{2,1,0:T(8,128)(2,1)S(1)}, u32[]{:S(2)}, u32[]{:S(2)}) collective-permute-start(bf16[1,512,128]{2,1,0:T(8,128)(2,1)S(1)} %get-tuple-element.36), channel_id=1, source_target_pairs={{0,1},{1,0},{2,3},{3,2},{4,5},{5,4},{6,7},{7,6},{8,9},{9,8},{10,11... | collective-permute-start | bytes 393224 | tf_op jit(solution)/shard_map/ppermute | solution.py:258
  26.7 4.6 %collective-permute-start.10 = (f32[16,128]{1,0:T(8,128)S(1)}, f32[16,128]{1,0:T(8,128)S(1)}, u32[]{:S(2)}, u32[]{:S(2)}) collective-permute-start(f32[16,128]{1,0:T(8,128)S(1)} %shard_map.73.refs_12_), channel_id=1, source_target_pairs={{0,3},{1,2},{2,1},{3,0},{4,7},{5,6},{6,5},{7,4},{8,11},{9,10},{10,... | collective-permute-start | bytes 24584 | tf_op jit(solution)/shard_map/ppermute | solution.py:258
  28.2 3.7 %collective-permute-start.9 = (f32[16,128]{1,0:T(8,128)S(1)}, f32[16,128]{1,0:T(8,128)S(1)}, u32[]{:S(2)}, u32[]{:S(2)}) collective-permute-start(f32[16,128]{1,0:T(8,128)S(1)} %shard_map.73.refs_12_), channel_id=1, source_target_pairs={{0,2},{1,3},{2,0},{3,1},{4,6},{5,7},{6,4},{7,5},{8,10},{9,11},{10,... | collective-permute-start | bytes 24584 | tf_op jit(solution)/shard_map/ppermute | solution.py:258
  28.5 3.7 %collective-permute-start.8 = (f32[16,128]{1,0:T(8,128)S(1)}, f32[16,128]{1,0:T(8,128)S(1)}, u32[]{:S(2)}, u32[]{:S(2)}) collective-permute-start(f32[16,128]{1,0:T(8,128)S(1)} %shard_map.73.refs_12_), channel_id=1, source_target_pairs={{0,1},{1,0},{2,3},{3,2},{4,5},{5,4},{6,7},{7,6},{8,9},{9,8},{10,11... | collective-permute-start | bytes 24584 | tf_op jit(solution)/shard_map/ppermute | solution.py:258
  32.6 1.6 %collective-permute-start.11 = (bf16[1024,128]{1,0:T(8,128)(2,1)S(1)}, bf16[1024,128]{1,0:T(8,128)(2,1)S(1)}, u32[]{:S(2)}, u32[]{:S(2)}) collective-permute-start(bf16[1024,128]{1,0:T(8,128)(2,1)S(1)} %get-tuple-element.39), channel_id=1, source_target_pairs={{0,4},{4,0},{8,12},{12,8},{16,20},{20,16},{24,28},{28,24},{1,5},{5... | collective-permute-start | bytes 786440 | tf_op jit(solution)/shard_map/ppermute | solution.py:261
  34.3 4.5 %collective-permute-start.12 = (bf16[256,128]{1,0:T(8,128)(2,1)S(1)}, bf16[256,128]{1,0:T(8,128)(2,1)S(1)}, u32[]{:S(2)}, u32[]{:S(2)}) collective-permute-start(bf16[256,128]{1,0:T(8,128)(2,1)S(1)} %get-tuple-element.41), channel_id=1, source_target_pairs={{0,8},{4,12},{8,0},{12,4},{16,24},{20,28},{24,16},{28,20},{1,9},{5... | collective-permute-start | bytes 196616 | tf_op jit(solution)/shard_map/ppermute | solution.py:266
  35.9 7.5 %collective-permute-start.13 = (bf16[256,128]{1,0:T(8,128)(2,1)S(1)}, bf16[256,128]{1,0:T(8,128)(2,1)S(1)}, u32[]{:S(2)}, u32[]{:S(2)}) collective-permute-start(bf16[256,128]{1,0:T(8,128)(2,1)S(1)} %get-tuple-element.42), channel_id=1, source_target_pairs={{0,16},{4,20},{8,24},{12,28},{16,0},{20,4},{24,8},{28,12},{1,17},{... | collective-permute-start | bytes 196616 | tf_op jit(solution)/shard_map/ppermute | solution.py:266
  38.5 6.2 %collective-permute-start.14 = (bf16[256,128]{1,0:T(8,128)(2,1)S(1)}, bf16[256,128]{1,0:T(8,128)(2,1)S(1)}, u32[]{:S(2)}, u32[]{:S(2)}) collective-permute-start(bf16[256,128]{1,0:T(8,128)(2,1)S(1)} %get-tuple-element.43), channel_id=1, source_target_pairs={{0,24},{4,28},{8,16},{12,20},{16,8},{20,12},{24,0},{28,4},{1,25},{... | collective-permute-start | bytes 196616 | tf_op jit(solution)/shard_map/ppermute | solution.py:266
  44.8 4.6 %collective-permute-start.15 = (bf16[256,128]{1,0:T(8,128)(2,1)S(1)}, bf16[256,128]{1,0:T(8,128)(2,1)S(1)}, u32[]{:S(2)}, u32[]{:S(2)}) collective-permute-start(bf16[256,128]{1,0:T(8,128)(2,1)S(1)} %get-tuple-element.45), channel_id=1, source_target_pairs={{0,8},{4,12},{8,0},{12,4},{16,24},{20,28},{24,16},{28,20},{1,9},{5... | collective-permute-start | bytes 196616 | tf_op jit(solution)/shard_map/ppermute | solution.py:266
  45.7 6.2 %collective-permute-start.16 = (bf16[256,128]{1,0:T(8,128)(2,1)S(1)}, bf16[256,128]{1,0:T(8,128)(2,1)S(1)}, u32[]{:S(2)}, u32[]{:S(2)}) collective-permute-start(bf16[256,128]{1,0:T(8,128)(2,1)S(1)} %get-tuple-element.46), channel_id=1, source_target_pairs={{0,16},{4,20},{8,24},{12,28},{16,0},{20,4},{24,8},{28,12},{1,17},{... | collective-permute-start | bytes 196616 | tf_op jit(solution)/shard_map/ppermute | solution.py:266
  47.4 6.1 %collective-permute-start.17 = (bf16[256,128]{1,0:T(8,128)(2,1)S(1)}, bf16[256,128]{1,0:T(8,128)(2,1)S(1)}, u32[]{:S(2)}, u32[]{:S(2)}) collective-permute-start(bf16[256,128]{1,0:T(8,128)(2,1)S(1)} %get-tuple-element.47), channel_id=1, source_target_pairs={{0,24},{4,28},{8,16},{12,20},{16,8},{20,12},{24,0},{28,4},{1,25},{... | collective-permute-start | bytes 196616 | tf_op jit(solution)/shard_map/ppermute | solution.py:266
  53.6 1.6 %collective-permute-start.18 = (bf16[1024,128]{1,0:T(8,128)(2,1)S(1)}, bf16[1024,128]{1,0:T(8,128)(2,1)S(1)}, u32[]{:S(2)}, u32[]{:S(2)}) collective-permute-start(bf16[1024,128]{1,0:T(8,128)(2,1)S(1)} %bitcast.26), channel_id=1, source_target_pairs={{0,4},{4,0},{8,12},{12,8},{16,20},{20,16},{24,28},{28,24},{1,5},{5... | collective-permute-start | bytes 786440 | tf_op jit(solution)/shard_map/ppermute | solution.py:261

commit v5 on v4

--- a/solution.py
+++ b/solution.py
@@ -185,6 +185,10 @@
     return (lax.axis_index("section") >> 1) ^ distance
 
 
+def order_of(chips):
+    return sorted(range(chips), key=lambda k: (k % 2 == 0, -k))
+
+
 def pair_kernel(branch_ref, came_ref, *outs):
     core = lax.axis_index("section") & 1
     for k, out in enumerate(outs):
@@ -194,9 +198,9 @@
 
 def later_kernel(*refs):
     chips = len(refs) // 2
-    held = refs[-1]
+    held, order = refs[-1], order_of(chips)
     for k in range(chips):
-        held[chip_of(k)] = refs[k][...].astype(F32)
+        held[chip_of(k)] = refs[order.index(k)][...].astype(F32)
     total = jnp.zeros(held.shape[1:], F32)
     for z in range(chips - 1, -1, -1):
         term = held[z]
@@ -211,7 +215,7 @@
     later, (later_out, mate_out) = refs[:-2], refs[-2:]
     core = lax.axis_index("section") & 1
     scale = core.astype(F32)
-    for k, part in enumerate(later):
+    for k, part in zip(order_of(len(later)), later):
         q = chip_of(k)
         later_out[q] = part[...]
         mate_out[q] = (part[...].astype(F32) + branch_ref[core, q] * scale).astype(mate_out.dtype)
@@ -324,9 +328,9 @@
         out_specs=[WHOLE] * chips,
         scratch_shapes=[pltpu.VMEM(shape, F32)],
         compiler_params=LIMIT,
-    )(*(near(v) for v in terms))
+    )(*(near(terms[k]) for k in order_of(chips)))
     later = [across(v, k) for k, v in enumerate(later)]
-    later, mate = call(mate_kernel, [whole] * 2, halves, *later)
+    later, mate = call(mate_kernel, [whole] * 2, halves, *(later[k] for k in order_of(chips)))
     later, mate = later.reshape(part, tokens), swap(mate.reshape(part, tokens))
     values = inputs.reshape(2, part, tokens).astype(F32)
     gain_grad = jnp.sum(partial_value * values * upside[:1], axis=2).reshape(1, rows)

time: 56.3 us -> 54.7 us (0.972)
  waiting for transfers between devices: 22.4 us -> 20.8 us
    ppermute x6, waiting for transfers between devices: 10.2 us -> 8.55 us  [across(): lax.ppermute(value, 'section', [(s, s ^ 2 * distance) for s in range(laye...]
  transfers between devices with their start and end apart: 19 -> 19, of which waited for: 14 -> 15; matrix products, arithmetic and copies ran while one was open for 2% -> 2% of each run, Pallas kernels for 11% -> 11%
where the time goes in v5:
time: 54.7 us; the launch traced here: 54.6 us
  starting transfers between devices  22 us (40%)
  waiting for transfers between devices  20.8 us (38%)
  Pallas kernels  10 us (18%)
  between operations  0.74 us (1%)
  local copies, waits for them, and re-layouts  0.63 us (1%)
    ppermute x11, starting transfers between devices, exchange(): return lax.ppermute(value, 'tensor', [(i, i ^ mask) for i in range(count)])  13 us
    ppermute x11, waiting for transfers between devices, exchange(): return lax.ppermute(value, 'tensor', [(i, i ^ mask) for i in range(count)])  10.2 us
    ppermute x6, starting transfers between devices, across(): lax.ppermute(value, 'section', [(s, s ^ 2 * distance) for s in range(laye...  8.91 us
    ppermute x6, waiting for transfers between devices, across(): lax.ppermute(value, 'section', [(s, s ^ 2 * distance) for s in range(laye...  8.55 us
    pallas_call x3, Pallas kernels, product(): pl.pallas_call(keep_kernel if extra else multiply, out_shape=out_shape, g...  7.56 us
    ppermute x2, waiting for transfers between devices, swap(): return lax.ppermute(value, 'section', [(s, s ^ 1) for s in range(layers)])  2.05 us
    pallas_call x6, Pallas kernels, call(): pl.pallas_call(kernel, out_shape=out_shape, in_specs=[WHOLE] * len(arrays...  1.31 us
  transfers between devices with their start and end apart: 19, of which 15 were waited for; matrix products, arithmetic and copies ran while one was open for 2% of the time, Pallas kernels for 11%

profile of v5, /device:TPU:0, one launch (start us, length us, event | category | flops | bytes accessed | tf_op | source)
XLA Modules:
  0.0 54.6 jit_solution(17173948307131795991)
XLA Ops:
  0.6 2.2 %shard_map.69 = (bf16[2,512,128]{2,1,0:T(8,128)(2,1)S(1)}, bf16[2,512,128]{2,1,0:T(8,128)(2,1)S(1)}) custom-call(bf16[8192,512]{1,0:T(8,128)(2,1)} %bitcast.27, bf16[8192,512]{1,0:T(8,128)(2,1)} %bitcast.28, bf16[128,512]{1,0:T(8,128)(2,1)} %bitcast.33), custom_call_target="tpu_custom_call" | custom-call | flops 268435456 | bytes 2621440 | tf_op jit(solution)/shard_map/pallas_call | solution.py:86
  2.9 3.0 %collective-permute-start = (bf16[2,512,128]{2,1,0:T(8,128)(2,1)S(1)}, bf16[2,512,128]{2,1,0:T(8,128)(2,1)S(1)}, u32[]{:S(2)}, u32[]{:S(2)}) collective-permute-start(bf16[2,512,128]{2,1,0:T(8,128)(2,1)S(1)} %get-tuple-element.29), channel_id=1, source_target_pairs={{0,1},{1,0},{2,3},{3,2},{4,5},{5,4},{6,7},{7,6},{8,9},{9,8},{10,11... | collective-permute-start | bytes 786440 | tf_op jit(solution)/shard_map/ppermute | solution.py:262
  5.9 1.5 %collective-permute-start.1 = (bf16[2,512,128]{2,1,0:T(8,128)(2,1)S(1)}, bf16[2,512,128]{2,1,0:T(8,128)(2,1)S(1)}, u32[]{:S(2)}, u32[]{:S(2)}) collective-permute-start(bf16[2,512,128]{2,1,0:T(8,128)(2,1)S(1)} %get-tuple-element.30), channel_id=1, source_target_pairs={{0,2},{1,3},{2,0},{3,1},{4,6},{5,7},{6,4},{7,5},{8,10},{9,11},{10,... | collective-permute-start | bytes 786440 | tf_op jit(solution)/shard_map/ppermute | solution.py:262
  7.4 2.2 %shard_map.70 = (bf16[2,512,128]{2,1,0:T(8,128)(2,1)S(1)}, bf16[2,512,128]{2,1,0:T(8,128)(2,1)S(1)}) custom-call(bf16[8192,512]{1,0:T(8,128)(2,1)} %bitcast.29, bf16[8192,512]{1,0:T(8,128)(2,1)} %bitcast.30, bf16[128,512]{1,0:T(8,128)(2,1)} %bitcast.34), custom_call_target="tpu_custom_call" | custom-call | flops 268435456 | bytes 2621440 | tf_op jit(solution)/shard_map/pallas_call | solution.py:86
  9.6 0.6 %collective-permute-start.2 = (bf16[2,512,128]{2,1,0:T(8,128)(2,1)S(1)}, bf16[2,512,128]{2,1,0:T(8,128)(2,1)S(1)}, u32[]{:S(2)}, u32[]{:S(2)}) collective-permute-start(bf16[2,512,128]{2,1,0:T(8,128)(2,1)S(1)} %get-tuple-element.31), channel_id=1, source_target_pairs={{0,1},{1,0},{2,3},{3,2},{4,5},{5,4},{6,7},{7,6},{8,9},{9,8},{10,11... | collective-permute-start | bytes 786440 | tf_op jit(solution)/shard_map/ppermute | solution.py:262
  10.3 3.2 %shard_map.68 = (bf16[2,1024,128]{2,1,0:T(8,128)(2,1)S(1)}, bf16[2,1024,128]{2,1,0:T(8,128)(2,1)S(1)}, f32[8,128]{1,0:T(8,128)S(1)}) custom-call(bf16[8192,512]{1,0:T(8,128)(2,1)} %bitcast.31, bf16[8192,512]{1,0:T(8,128)(2,1)} %bitcast.32, bf16[128,512]{1,0:T(8,128)(2,1)} %bitcast.35, bf16[2048,128]{1,0:T(8,128)(2,1)S(1)} %bitcast.16), custom_call_target="tpu_custom_call" | custom-call | flops 536870912 | bytes 5242880 | tf_op jit(solution)/shard_map/pallas_call | solution.py:86
  13.5 1.6 %collective-permute-done.1.refs_5_.refs_3_ = bf16[2,512,128]{2,1,0:T(8,128)(2,1)S(1)} collective-permute-done((bf16[2,512,128]{2,1,0:T(8,128)(2,1)S(1)}, bf16[2,512,128]{2,1,0:T(8,128)(2,1)S(1)}, u32[]{:S(2)}, u32[]{:S(2)}) %collective-permute-start.1) | collective-permute-done | bytes 262176 | tf_op jit(solution)/shard_map/ppermute | solution.py:262
  15.3 1.6 %collective-permute-start.4 = (bf16[2,512,128]{2,1,0:T(8,128)(2,1)S(1)}, bf16[2,512,128]{2,1,0:T(8,128)(2,1)S(1)}, u32[]{:S(2)}, u32[]{:S(2)}) collective-permute-start(bf16[2,512,128]{2,1,0:T(8,128)(2,1)S(1)} %get-tuple-element.33), channel_id=1, source_target_pairs={{0,2},{1,3},{2,0},{3,1},{4,6},{5,7},{6,4},{7,5},{8,10},{9,11},{10,... | collective-permute-start | bytes 786440 | tf_op jit(solution)/shard_map/ppermute | solution.py:262
  16.9 0.5 collective-permute-start.5
  17.4 1.3 %collective-permute-done.2.refs_2_.refs_4_ = bf16[2,512,128]{2,1,0:T(8,128)(2,1)S(1)} collective-permute-done((bf16[2,512,128]{2,1,0:T(8,128)(2,1)S(1)}, bf16[2,512,128]{2,1,0:T(8,128)(2,1)S(1)}, u32[]{:S(2)}, u32[]{:S(2)}) %collective-permute-start.2) | collective-permute-done | bytes 262176 | tf_op jit(solution)/shard_map/ppermute | solution.py:262
  18.8 2.0 %collective-permute-done.3.refs_3_.refs_5_ = bf16[2,512,128]{2,1,0:T(8,128)(2,1)S(1)} collective-permute-done((bf16[2,512,128]{2,1,0:T(8,128)(2,1)S(1)}, bf16[2,512,128]{2,1,0:T(8,128)(2,1)S(1)}, u32[]{:S(2)}, u32[]{:S(2)}) %collective-permute-start.3) | collective-permute-done | bytes 262176 | tf_op jit(solution)/shard_map/ppermute | solution.py:262
  20.8 1.6 %collective-permute-start.6 = (bf16[1,512,128]{2,1,0:T(8,128)(2,1)S(1)}, bf16[1,512,128]{2,1,0:T(8,128)(2,1)S(1)}, u32[]{:S(2)}, u32[]{:S(2)}) collective-permute-start(bf16[1,512,128]{2,1,0:T(8,128)(2,1)S(1)} %get-tuple-element.35), channel_id=1, source_target_pairs={{0,2},{1,3},{2,0},{3,1},{4,6},{5,7},{6,4},{7,5},{8,10},{9,11},{10,... | collective-permute-start | bytes 393224 | tf_op jit(solution)/shard_map/ppermute | solution.py:262
  22.4 0.5 collective-permute-start.7
  22.9 3.4 %collective-permute-done.4.refs_6_ = bf16[2,512,128]{2,1,0:T(8,128)(2,1)S(1)} collective-permute-done((bf16[2,512,128]{2,1,0:T(8,128)(2,1)S(1)}, bf16[2,512,128]{2,1,0:T(8,128)(2,1)S(1)}, u32[]{:S(2)}, u32[]{:S(2)}) %collective-permute-start.4) | collective-permute-done | bytes 262176 | tf_op jit(solution)/shard_map/ppermute | solution.py:262
  26.7 1.6 %collective-permute-start.10 = (f32[16,128]{1,0:T(8,128)S(1)}, f32[16,128]{1,0:T(8,128)S(1)}, u32[]{:S(2)}, u32[]{:S(2)}) collective-permute-start(f32[16,128]{1,0:T(8,128)S(1)} %shard_map.73.refs_12_), channel_id=1, source_target_pairs={{0,3},{1,2},{2,1},{3,0},{4,7},{5,6},{6,5},{7,4},{8,11},{9,10},{10,... | collective-permute-start | bytes 24584 | tf_op jit(solution)/shard_map/ppermute | solution.py:262
  28.5 1.8 %collective-permute-start.8 = (f32[16,128]{1,0:T(8,128)S(1)}, f32[16,128]{1,0:T(8,128)S(1)}, u32[]{:S(2)}, u32[]{:S(2)}) collective-permute-start(f32[16,128]{1,0:T(8,128)S(1)} %shard_map.73.refs_12_), channel_id=1, source_target_pairs={{0,1},{1,0},{2,3},{3,2},{4,5},{5,4},{6,7},{7,6},{8,9},{9,8},{10,11... | collective-permute-start | bytes 24584 | tf_op jit(solution)/shard_map/ppermute | solution.py:262
  30.3 1.1 %collective-permute-done.10.refs_15_ = f32[16,128]{1,0:T(8,128)S(1)} collective-permute-done((f32[16,128]{1,0:T(8,128)S(1)}, f32[16,128]{1,0:T(8,128)S(1)}, u32[]{:S(2)}, u32[]{:S(2)}) %collective-permute-start.10) | collective-permute-done | bytes 8224 | tf_op jit(solution)/shard_map/ppermute | solution.py:262
  31.3 0.6 %collective-permute-done.9.refs_14_ = f32[16,128]{1,0:T(8,128)S(1)} collective-permute-done((f32[16,128]{1,0:T(8,128)S(1)}, f32[16,128]{1,0:T(8,128)S(1)}, u32[]{:S(2)}, u32[]{:S(2)}) %collective-permute-start.9) | collective-permute-done | bytes 8224 | tf_op jit(solution)/shard_map/ppermute | solution.py:262
  32.7 1.5 %collective-permute-done.11.came_ref = bf16[1024,128]{1,0:T(8,128)(2,1)S(1)} collective-permute-done((bf16[1024,128]{1,0:T(8,128)(2,1)S(1)}, bf16[1024,128]{1,0:T(8,128)(2,1)S(1)}, u32[]{:S(2)}, u32[]{:S(2)}) %collective-permute-start.11) | collective-permute-done | bytes 262176 | tf_op jit(solution)/shard_map/ppermute | solution.py:265
  34.3 3.7 %collective-permute-start.12 = (bf16[256,128]{1,0:T(8,128)(2,1)S(1)}, bf16[256,128]{1,0:T(8,128)(2,1)S(1)}, u32[]{:S(2)}, u32[]{:S(2)}) collective-permute-start(bf16[256,128]{1,0:T(8,128)(2,1)S(1)} %get-tuple-element.40), channel_id=1, source_target_pairs={{0,24},{4,28},{8,16},{12,20},{16,8},{20,12},{24,0},{28,4},{1,25},{... | collective-permute-start | bytes 196616 | tf_op jit(solution)/shard_map/ppermute | solution.py:270
  37.9 0.8 %collective-permute-start.14 = (bf16[256,128]{1,0:T(8,128)(2,1)S(1)}, bf16[256,128]{1,0:T(8,128)(2,1)S(1)}, u32[]{:S(2)}, u32[]{:S(2)}) collective-permute-start(bf16[256,128]{1,0:T(8,128)(2,1)S(1)} %get-tuple-element.42), channel_id=1, source_target_pairs={{0,16},{4,20},{8,24},{12,28},{16,0},{20,4},{24,8},{28,12},{1,17},{... | collective-permute-start | bytes 196616 | tf_op jit(solution)/shard_map/ppermute | solution.py:270
  38.7 2.4 %collective-permute-done.12.refs_0_ = bf16[256,128]{1,0:T(8,128)(2,1)S(1)} collective-permute-done((bf16[256,128]{1,0:T(8,128)(2,1)S(1)}, bf16[256,128]{1,0:T(8,128)(2,1)S(1)}, u32[]{:S(2)}, u32[]{:S(2)}) %collective-permute-start.12) | collective-permute-done | bytes 65568 | tf_op jit(solution)/shard_map/ppermute | solution.py:270
  41.1 1.9 %collective-permute-done.13.refs_1_ = bf16[256,128]{1,0:T(8,128)(2,1)S(1)} collective-permute-done((bf16[256,128]{1,0:T(8,128)(2,1)S(1)}, bf16[256,128]{1,0:T(8,128)(2,1)S(1)}, u32[]{:S(2)}, u32[]{:S(2)}) %collective-permute-start.13) | collective-permute-done | bytes 65568 | tf_op jit(solution)/shard_map/ppermute | solution.py:270
  43.0 0.8 %collective-permute-done.14.refs_2_ = bf16[256,128]{1,0:T(8,128)(2,1)S(1)} collective-permute-done((bf16[256,128]{1,0:T(8,128)(2,1)S(1)}, bf16[256,128]{1,0:T(8,128)(2,1)S(1)}, u32[]{:S(2)}, u32[]{:S(2)}) %collective-permute-start.14) | collective-permute-done | bytes 65568 | tf_op jit(solution)/shard_map/ppermute | solution.py:270
  43.9 2.2 %collective-permute-start.15 = (bf16[256,128]{1,0:T(8,128)(2,1)S(1)}, bf16[256,128]{1,0:T(8,128)(2,1)S(1)}, u32[]{:S(2)}, u32[]{:S(2)}) collective-permute-start(bf16[256,128]{1,0:T(8,128)(2,1)S(1)} %get-tuple-element.44), channel_id=1, source_target_pairs={{0,24},{4,28},{8,16},{12,20},{16,8},{20,12},{24,0},{28,4},{1,25},{... | collective-permute-start | bytes 196616 | tf_op jit(solution)/shard_map/ppermute | solution.py:270
  46.5 1.9 %collective-permute-start.17 = (bf16[256,128]{1,0:T(8,128)(2,1)S(1)}, bf16[256,128]{1,0:T(8,128)(2,1)S(1)}, u32[]{:S(2)}, u32[]{:S(2)}) collective-permute-start(bf16[256,128]{1,0:T(8,128)(2,1)S(1)} %get-tuple-element.46), channel_id=1, source_target_pairs={{0,16},{4,20},{8,24},{12,28},{16,0},{20,4},{24,8},{28,12},{1,17},{... | collective-permute-start | bytes 196616 | tf_op jit(solution)/shard_map/ppermute | solution.py:270
  48.4 1.9 %collective-permute-done.15.refs_0_ = bf16[256,128]{1,0:T(8,128)(2,1)S(1)} collective-permute-done((bf16[256,128]{1,0:T(8,128)(2,1)S(1)}, bf16[256,128]{1,0:T(8,128)(2,1)S(1)}, u32[]{:S(2)}, u32[]{:S(2)}) %collective-permute-start.15) | collective-permute-done | bytes 65568 | tf_op jit(solution)/shard_map/ppermute | solution.py:270
  50.3 0.9 %collective-permute-done.16.refs_1_ = bf16[256,128]{1,0:T(8,128)(2,1)S(1)} collective-permute-done((bf16[256,128]{1,0:T(8,128)(2,1)S(1)}, bf16[256,128]{1,0:T(8,128)(2,1)S(1)}, u32[]{:S(2)}, u32[]{:S(2)}) %collective-permute-start.16) | collective-permute-done | bytes 65568 | tf_op jit(solution)/shard_map/ppermute | solution.py:270
  51.2 0.6 %collective-permute-done.17.refs_2_ = bf16[256,128]{1,0:T(8,128)(2,1)S(1)} collective-permute-done((bf16[256,128]{1,0:T(8,128)(2,1)S(1)}, bf16[256,128]{1,0:T(8,128)(2,1)S(1)}, u32[]{:S(2)}, u32[]{:S(2)}) %collective-permute-start.17) | collective-permute-done | bytes 65568 | tf_op jit(solution)/shard_map/ppermute | solution.py:270
  52.4 0.6 %copy.7 = f32[1,1,2,1024]{3,1,2,0:T(1,128)} copy(f32[1,1,2,1024]{3,2,1,0:T(2,128)S(1)} %bitcast.37) | data formatting | bytes 16384
  53.0 0.5 collective-permute-done.18.mate_ref
  53.5 1.0 %shard_map.78 = bf16[2,1024,128]{2,1,0:T(8,128)(2,1)} custom-call(f32[2,1024,128]{2,1,0:T(8,128)S(1)} %get-tuple-element.38.branch_ref, bf16[2,1024,128]{2,1,0:T(8,128)(2,1)S(1)} %bitcast.24, bf16[1024,128]{1,0:T(8,128)(2,1)S(1)} %bitcast.25, bf16[1024,128]{1,0:T(8,128)(2,1)S(1)} %collective-permute-done.11.came_ref, ...), custom_call_target="tpu_custom_call" | custom-call | tf_op jit(solution)/shard_map/pallas_call | solution.py:338
  (26 shorter events, 2.9 us)
Async XLA Ops:
  2.9 10.6 %collective-permute-start = (bf16[2,512,128]{2,1,0:T(8,128)(2,1)S(1)}, bf16[2,512,128]{2,1,0:T(8,128)(2,1)S(1)}, u32[]{:S(2)}, u32[]{:S(2)}) collective-permute-start(bf16[2,512,128]{2,1,0:T(8,128)(2,1)S(1)} %get-tuple-element.29), channel_id=1, source_target_pairs={{0,1},{1,0},{2,3},{3,2},{4,5},{5,4},{6,7},{7,6},{8,9},{9,8},{10,11... | collective-permute-start | bytes 786440 | tf_op jit(solution)/shard_map/ppermute | solution.py:262
  5.9 4.4 %copy-start = (bf16[1,2048,128]{2,1,0:T(8,128)(2,1)S(1)}, bf16[1,2048,128]{2,1,0:T(8,128)(2,1)}, u32[]{:S(2)}) copy-start(bf16[1,2048,128]{2,1,0:T(8,128)(2,1)} %param.5) | copy-start | bytes 1572868
  5.9 9.2 %collective-permute-start.1 = (bf16[2,512,128]{2,1,0:T(8,128)(2,1)S(1)}, bf16[2,512,128]{2,1,0:T(8,128)(2,1)S(1)}, u32[]{:S(2)}, u32[]{:S(2)}) collective-permute-start(bf16[2,512,128]{2,1,0:T(8,128)(2,1)S(1)} %get-tuple-element.30), channel_id=1, source_target_pairs={{0,2},{1,3},{2,0},{3,1},{4,6},{5,7},{6,4},{7,5},{8,10},{9,11},{10,... | collective-permute-start | bytes 786440 | tf_op jit(solution)/shard_map/ppermute | solution.py:262
  9.6 9.2 %collective-permute-start.2 = (bf16[2,512,128]{2,1,0:T(8,128)(2,1)S(1)}, bf16[2,512,128]{2,1,0:T(8,128)(2,1)S(1)}, u32[]{:S(2)}, u32[]{:S(2)}) collective-permute-start(bf16[2,512,128]{2,1,0:T(8,128)(2,1)S(1)} %get-tuple-element.31), channel_id=1, source_target_pairs={{0,1},{1,0},{2,3},{3,2},{4,5},{5,4},{6,7},{7,6},{8,9},{9,8},{10,11... | collective-permute-start | bytes 786440 | tf_op jit(solution)/shard_map/ppermute | solution.py:262
  10.2 10.6 %collective-permute-start.3 = (bf16[2,512,128]{2,1,0:T(8,128)(2,1)S(1)}, bf16[2,512,128]{2,1,0:T(8,128)(2,1)S(1)}, u32[]{:S(2)}, u32[]{:S(2)}) collective-permute-start(bf16[2,512,128]{2,1,0:T(8,128)(2,1)S(1)} %get-tuple-element.32), channel_id=1, source_target_pairs={{0,2},{1,3},{2,0},{3,1},{4,6},{5,7},{6,4},{7,5},{8,10},{9,11},{10,... | collective-permute-start | bytes 786440 | tf_op jit(solution)/shard_map/ppermute | solution.py:262
  10.3 4.8 %copy-start.2 = (f32[1,2048]{1,0:T(1,128)S(1)}, f32[1,2048]{1,0:T(1,128)}, u32[]{:S(2)}) copy-start(f32[1,2048]{1,0:T(1,128)} %refs_11_.1) | copy-start | bytes 24580
  13.4 40.1 %copy-start.1 = (bf16[2048,128]{1,0:T(8,128)(2,1)S(1)}, bf16[2048,128]{1,0:T(8,128)(2,1)}, u32[]{:S(2)}) copy-start(bf16[2048,128]{1,0:T(8,128)(2,1)} %param.9) | copy-start | bytes 1572868
  15.3 10.9 %collective-permute-start.4 = (bf16[2,512,128]{2,1,0:T(8,128)(2,1)S(1)}, bf16[2,512,128]{2,1,0:T(8,128)(2,1)S(1)}, u32[]{:S(2)}, u32[]{:S(2)}) collective-permute-start(bf16[2,512,128]{2,1,0:T(8,128)(2,1)S(1)} %get-tuple-element.33), channel_id=1, source_target_pairs={{0,2},{1,3},{2,0},{3,1},{4,6},{5,7},{6,4},{7,5},{8,10},{9,11},{10,... | collective-permute-start | bytes 786440 | tf_op jit(solution)/shard_map/ppermute | solution.py:262
  16.9 9.4 %collective-permute-start.5 = (bf16[2,512,128]{2,1,0:T(8,128)(2,1)S(1)}, bf16[2,512,128]{2,1,0:T(8,128)(2,1)S(1)}, u32[]{:S(2)}, u32[]{:S(2)}) collective-permute-start(bf16[2,512,128]{2,1,0:T(8,128)(2,1)S(1)} %get-tuple-element.34), channel_id=1, source_target_pairs={{0,1},{1,0},{2,3},{3,2},{4,5},{5,4},{6,7},{7,6},{8,9},{9,8},{10,11... | collective-permute-start | bytes 786440 | tf_op jit(solution)/shard_map/ppermute | solution.py:262
  20.8 9.5 %collective-permute-start.6 = (bf16[1,512,128]{2,1,0:T(8,128)(2,1)S(1)}, bf16[1,512,128]{2,1,0:T(8,128)(2,1)S(1)}, u32[]{:S(2)}, u32[]{:S(2)}) collective-permute-start(bf16[1,512,128]{2,1,0:T(8,128)(2,1)S(1)} %get-tuple-element.35), channel_id=1, source_target_pairs={{0,2},{1,3},{2,0},{3,1},{4,6},{5,7},{6,4},{7,5},{8,10},{9,11},{10,... | collective-permute-start | bytes 393224 | tf_op jit(solution)/shard_map/ppermute | solution.py:262
  22.4 7.9 %collective-permute-start.7 = (bf16[1,512,128]{2,1,0:T(8,128)(2,1)S(1)}, bf16[1,512,128]{2,1,0:T(8,128)(2,1)S(1)}, u32[]{:S(2)}, u32[]{:S(2)}) collective-permute-start(bf16[1,512,128]{2,1,0:T(8,128)(2,1)S(1)} %get-tuple-element.36), channel_id=1, source_target_pairs={{0,1},{1,0},{2,3},{3,2},{4,5},{5,4},{6,7},{7,6},{8,9},{9,8},{10,11... | collective-permute-start | bytes 393224 | tf_op jit(solution)/shard_map/ppermute | solution.py:262
  26.7 4.6 %collective-permute-start.10 = (f32[16,128]{1,0:T(8,128)S(1)}, f32[16,128]{1,0:T(8,128)S(1)}, u32[]{:S(2)}, u32[]{:S(2)}) collective-permute-start(f32[16,128]{1,0:T(8,128)S(1)} %shard_map.73.refs_12_), channel_id=1, source_target_pairs={{0,3},{1,2},{2,1},{3,0},{4,7},{5,6},{6,5},{7,4},{8,11},{9,10},{10,... | collective-permute-start | bytes 24584 | tf_op jit(solution)/shard_map/ppermute | solution.py:262
  28.2 3.7 %collective-permute-start.9 = (f32[16,128]{1,0:T(8,128)S(1)}, f32[16,128]{1,0:T(8,128)S(1)}, u32[]{:S(2)}, u32[]{:S(2)}) collective-permute-start(f32[16,128]{1,0:T(8,128)S(1)} %shard_map.73.refs_12_), channel_id=1, source_target_pairs={{0,2},{1,3},{2,0},{3,1},{4,6},{5,7},{6,4},{7,5},{8,10},{9,11},{10,... | collective-permute-start | bytes 24584 | tf_op jit(solution)/shard_map/ppermute | solution.py:262
  28.5 3.7 %collective-permute-start.8 = (f32[16,128]{1,0:T(8,128)S(1)}, f32[16,128]{1,0:T(8,128)S(1)}, u32[]{:S(2)}, u32[]{:S(2)}) collective-permute-start(f32[16,128]{1,0:T(8,128)S(1)} %shard_map.73.refs_12_), channel_id=1, source_target_pairs={{0,1},{1,0},{2,3},{3,2},{4,5},{5,4},{6,7},{7,6},{8,9},{9,8},{10,11... | collective-permute-start | bytes 24584 | tf_op jit(solution)/shard_map/ppermute | solution.py:262
  32.6 1.6 %collective-permute-start.11 = (bf16[1024,128]{1,0:T(8,128)(2,1)S(1)}, bf16[1024,128]{1,0:T(8,128)(2,1)S(1)}, u32[]{:S(2)}, u32[]{:S(2)}) collective-permute-start(bf16[1024,128]{1,0:T(8,128)(2,1)S(1)} %get-tuple-element.39), channel_id=1, source_target_pairs={{0,4},{4,0},{8,12},{12,8},{16,20},{20,16},{24,28},{28,24},{1,5},{5... | collective-permute-start | bytes 786440 | tf_op jit(solution)/shard_map/ppermute | solution.py:265
  34.3 6.9 %collective-permute-start.12 = (bf16[256,128]{1,0:T(8,128)(2,1)S(1)}, bf16[256,128]{1,0:T(8,128)(2,1)S(1)}, u32[]{:S(2)}, u32[]{:S(2)}) collective-permute-start(bf16[256,128]{1,0:T(8,128)(2,1)S(1)} %get-tuple-element.40), channel_id=1, source_target_pairs={{0,24},{4,28},{8,16},{12,20},{16,8},{20,12},{24,0},{28,4},{1,25},{... | collective-permute-start | bytes 196616 | tf_op jit(solution)/shard_map/ppermute | solution.py:270
  37.9 5.1 %collective-permute-start.13 = (bf16[256,128]{1,0:T(8,128)(2,1)S(1)}, bf16[256,128]{1,0:T(8,128)(2,1)S(1)}, u32[]{:S(2)}, u32[]{:S(2)}) collective-permute-start(bf16[256,128]{1,0:T(8,128)(2,1)S(1)} %get-tuple-element.41), channel_id=1, source_target_pairs={{0,8},{4,12},{8,0},{12,4},{16,24},{20,28},{24,16},{28,20},{1,9},{5... | collective-permute-start | bytes 196616 | tf_op jit(solution)/shard_map/ppermute | solution.py:270
  37.9 5.9 %collective-permute-start.14 = (bf16[256,128]{1,0:T(8,128)(2,1)S(1)}, bf16[256,128]{1,0:T(8,128)(2,1)S(1)}, u32[]{:S(2)}, u32[]{:S(2)}) collective-permute-start(bf16[256,128]{1,0:T(8,128)(2,1)S(1)} %get-tuple-element.42), channel_id=1, source_target_pairs={{0,16},{4,20},{8,24},{12,28},{16,0},{20,4},{24,8},{28,12},{1,17},{... | collective-permute-start | bytes 196616 | tf_op jit(solution)/shard_map/ppermute | solution.py:270
  43.9 6.4 %collective-permute-start.15 = (bf16[256,128]{1,0:T(8,128)(2,1)S(1)}, bf16[256,128]{1,0:T(8,128)(2,1)S(1)}, u32[]{:S(2)}, u32[]{:S(2)}) collective-permute-start(bf16[256,128]{1,0:T(8,128)(2,1)S(1)} %get-tuple-element.44), channel_id=1, source_target_pairs={{0,24},{4,28},{8,16},{12,20},{16,8},{20,12},{24,0},{28,4},{1,25},{... | collective-permute-start | bytes 196616 | tf_op jit(solution)/shard_map/ppermute | solution.py:270
  46.2 5.1 %collective-permute-start.16 = (bf16[256,128]{1,0:T(8,128)(2,1)S(1)}, bf16[256,128]{1,0:T(8,128)(2,1)S(1)}, u32[]{:S(2)}, u32[]{:S(2)}) collective-permute-start(bf16[256,128]{1,0:T(8,128)(2,1)S(1)} %get-tuple-element.45), channel_id=1, source_target_pairs={{0,8},{4,12},{8,0},{12,4},{16,24},{20,28},{24,16},{28,20},{1,9},{5... | collective-permute-start | bytes 196616 | tf_op jit(solution)/shard_map/ppermute | solution.py:270
  46.5 5.3 %collective-permute-start.17 = (bf16[256,128]{1,0:T(8,128)(2,1)S(1)}, bf16[256,128]{1,0:T(8,128)(2,1)S(1)}, u32[]{:S(2)}, u32[]{:S(2)}) collective-permute-start(bf16[256,128]{1,0:T(8,128)(2,1)S(1)} %get-tuple-element.46), channel_id=1, source_target_pairs={{0,16},{4,20},{8,24},{12,28},{16,0},{20,4},{24,8},{28,12},{1,17},{... | collective-permute-start | bytes 196616 | tf_op jit(solution)/shard_map/ppermute | solution.py:270
  51.9 1.6 %collective-permute-start.18 = (bf16[1024,128]{1,0:T(8,128)(2,1)S(1)}, bf16[1024,128]{1,0:T(8,128)(2,1)S(1)}, u32[]{:S(2)}, u32[]{:S(2)}) collective-permute-start(bf16[1024,128]{1,0:T(8,128)(2,1)S(1)} %bitcast.26), channel_id=1, source_target_pairs={{0,4},{4,0},{8,12},{12,8},{16,20},{20,16},{24,28},{28,24},{1,5},{5... | collective-permute-start | bytes 786440 | tf_op jit(solution)/shard_map/ppermute | solution.py:265

commit v6 on v5

--- a/solution.py
+++ b/solution.py
@@ -157,16 +157,11 @@
     sums_out[...] = jnp.concatenate([squares_ref[...], inner])
 
 
-def branch_kernel(features, pieces, held, *refs):
-    blocks, (inputs_ref, gains_ref, *sums) = refs[:held], refs[held:-4]
-    partial_out, branch_out, other_out, upside_out = refs[-4:]
+def weigh_kernel(pieces, held, *refs):
+    blocks, (gains_ref, partial_out, weighted_out) = refs[:held], refs[held:]
     part, tokens = partial_out.shape[1:]
     size = part // pieces
     width = tile_of(size)
-    both = jnp.sum(sum(s[...] for s in sums).reshape(2, 8, tokens), axis=1)
-    upside = lax.rsqrt(both[:1] / features + epsilon)
-    factor = both[1:] * (upside * upside * upside / features)
-    upside_out[...] = jnp.broadcast_to(upside, upside_out.shape)
     for h in range(2):
         for a in range(pieces):
             parts = terms_of(blocks, pieces, h, a)
@@ -175,8 +170,21 @@
                 row = h * part + a * size + start
                 total = sum(p[0, pl.ds(first + start, width)].astype(F32) for p, first in parts)
                 partial_out[h, at] = total
-                weighted = total * wide(gains_ref, row, width, tokens)
-                branch_out[h, at] = weighted * upside - inputs_ref[pl.ds(row, width)].astype(F32) * factor
+                weighted_out[h, at] = total * wide(gains_ref, row, width, tokens)
+
+
+def branch_kernel(features, weighted_ref, inputs_ref, *refs):
+    sums, (branch_out, other_out, upside_out) = refs[:-3], refs[-3:]
+    _, part, tokens = branch_out.shape
+    width = tile_of(part)
+    both = jnp.sum(sum(s[...] for s in sums).reshape(2, 8, tokens), axis=1)
+    upside = lax.rsqrt(both[:1] / features + epsilon)
+    factor = both[1:] * (upside * upside * upside / features)
+    upside_out[...] = jnp.broadcast_to(upside, upside_out.shape)
+    for start in range(0, 2 * part, width):
+        h, at = start // part, pl.ds(start % part, width)
+        value = inputs_ref[pl.ds(start, width)].astype(F32)
+        branch_out[h, at] = weighted_ref[h, at] * upside - value * factor
     core = lax.axis_index("section") & 1
     other_out[...] = branch_out[1 - core].astype(other_out.dtype)
 
@@ -196,8 +204,18 @@
         out[...] = (branch_ref[core, q] + came_ref[q].astype(F32)).astype(out.dtype)
 
 
+def gain_grad_kernel(partial_ref, inputs_ref, upside_ref, out_ref, done_ref):
+    done_ref[...] = upside_ref[...]
+    _, part, tokens = partial_ref.shape
+    width = tile_of(part)
+    for start in range(0, 2 * part, width):
+        product = partial_ref[start // part, pl.ds(start % part, width)] * upside_ref[:1]
+        product = product * inputs_ref[pl.ds(start, width)].astype(F32)
+        out_ref[:, start : start + width] = jnp.sum(product.T, axis=0, keepdims=True)
+
+
 def later_kernel(*refs):
-    chips = len(refs) // 2
+    chips = len(refs) // 2 - 1
     held, order = refs[-1], order_of(chips)
     for k in range(chips):
         held[chip_of(k)] = refs[order.index(k)][...].astype(F32)
@@ -207,7 +225,7 @@
         held[z] = total
         total = total + term
     for k in range(chips):
-        out = refs[chips + k]
+        out = refs[chips + 1 + k]
         out[...] = held[chip_of(k)].astype(out.dtype)
 
 
@@ -221,28 +239,28 @@
         mate_out[q] = (part[...].astype(F32) + branch_ref[core, q] * scale).astype(mate_out.dtype)
 
 
-def end_kernel(branch_ref, top_ref, later_ref, came_ref, mate_ref, out_ref):
+def first_end_kernel(branch_ref, top_ref, later_ref, came_ref, out_ref):
     core = lax.axis_index("section") & 1
-    half = core ^ pl.program_id(0)
-    own = branch_ref[half] + top_ref[half].astype(F32)
-
-    @pl.when(pl.program_id(0) == 0)
-    def _():
-        pair = came_ref[...].astype(F32) * (1 - core).astype(F32)
-        out_ref[0] = (own + later_ref[...].astype(F32) + pair).astype(out_ref.dtype)
-
-    @pl.when(pl.program_id(0) == 1)
-    def _():
-        out_ref[0] = (own + mate_ref[...].astype(F32)).astype(out_ref.dtype)
-
-
-def call(kernel, out_shape, *arrays):
+    pair = came_ref[...].astype(F32) * (1 - core).astype(F32)
+    total = branch_ref[core] + top_ref[core].astype(F32) + later_ref[...].astype(F32) + pair
+    out_ref[0] = total.astype(out_ref.dtype)
+
+
+def second_end_kernel(branch_ref, top_ref, mate_ref, result_ref, out_ref):
+    del result_ref
+    other = 1 - (lax.axis_index("section") & 1)
+    total = branch_ref[other] + top_ref[other].astype(F32) + mate_ref[...].astype(F32)
+    out_ref[0] = total.astype(out_ref.dtype)
+
+
+def call(kernel, out_shape, *arrays, cost=None):
     return pl.pallas_call(
         kernel,
         out_shape=out_shape,
         in_specs=[WHOLE] * len(arrays),
         out_specs=jax.tree.map(lambda _: WHOLE, out_shape),
         compiler_params=LIMIT,
+        cost_estimate=cost,
     )(*(near(a) for a in arrays))
 
 
@@ -298,7 +316,7 @@
     )
     sums, low = [sums], 1
     while low < count:
-        group = [low] if 2 * low >= count else [low, 2 * low, 3 * low]
+        group = [low] if 2 * low >= count else [3 * low, 2 * low, low]
         total = sum(sums)
         sums = [total] + [exchange(total, m) for m in group]
         low *= 4
@@ -306,12 +324,18 @@
     half = pltpu.VMEM((part, tokens), BF16)
     full = pltpu.VMEM((2, part, tokens), F32)
     held = [*kept, *arrived]
-    partial_value, branch, other, upside = call(
-        lambda *refs: branch_kernel(features, PIECES, len(held), *refs),
-        [full, full, half, pltpu.VMEM((8, tokens), F32)],
+    partial_value, weighted = call(
+        lambda *refs: weigh_kernel(PIECES, len(held), *refs),
+        [full, full],
         *held,
+        norm_gains,
+        cost=pl.CostEstimate(flops=1 << 32, bytes_accessed=1 << 20, transcendentals=0),
+    )
+    branch, other, upside = call(
+        lambda *refs: branch_kernel(features, *refs),
+        [full, half, pltpu.VMEM((8, tokens), F32)],
+        weighted,
         inputs,
-        norm_gains,
         *sums,
     )
 
@@ -321,30 +345,39 @@
     halves = branch.reshape(2, *shape)
     terms = call(pair_kernel, [block] * chips, halves, pair.reshape(shape))
     terms = [across(v, k) for k, v in enumerate(terms)]
+    gain_grad, done = call(
+        gain_grad_kernel,
+        [jax.ShapeDtypeStruct((1, rows), F32), pltpu.VMEM((8, tokens), F32)],
+        partial_value,
+        inputs,
+        upside,
+    )
     later = pl.pallas_call(
         later_kernel,
         out_shape=[block] * chips,
-        in_specs=[WHOLE] * chips,
+        in_specs=[WHOLE] * chips + [pl.BlockSpec(memory_space=pl.ANY)],
         out_specs=[WHOLE] * chips,
         scratch_shapes=[pltpu.VMEM(shape, F32)],
         compiler_params=LIMIT,
-    )(*(near(terms[k]) for k in order_of(chips)))
+    )(*(near(terms[k]) for k in order_of(chips)), done)
     later = [across(v, k) for k, v in enumerate(later)]
     later, mate = call(mate_kernel, [whole] * 2, halves, *(later[k] for k in order_of(chips)))
     later, mate = later.reshape(part, tokens), swap(mate.reshape(part, tokens))
-    values = inputs.reshape(2, part, tokens).astype(F32)
-    gain_grad = jnp.sum(partial_value * values * upside[:1], axis=2).reshape(1, rows)
-    arrays = (branch, top_grads.reshape(2, part, tokens), later, pair, mate)
-    result = pl.pallas_call(
-        end_kernel,
-        out_shape=jax.ShapeDtypeStruct((2, part, tokens), BF16),
-        grid=(2,),
-        in_specs=[WHOLE] * len(arrays),
-        out_specs=pl.BlockSpec(
-            (1, part, tokens), lambda i: ((lax.axis_index("section") & 1) ^ i, 0, 0)
-        ),
-        compiler_params=LIMIT,
-    )(*(near(a) for a in arrays))
+    top = near(top_grads.reshape(2, part, tokens))
+
+    def end(kernel, half, arrays, into):
+        return pl.pallas_call(
+            kernel,
+            out_shape=jax.ShapeDtypeStruct((2, part, tokens), BF16),
+            grid=(1,),
+            in_specs=[WHOLE] * len(arrays) + [pl.BlockSpec(memory_space=pl.ANY)] * len(into),
+            out_specs=pl.BlockSpec((1, part, tokens), lambda i: (half(lax.axis_index("section") & 1), 0, 0)),
+            input_output_aliases={len(arrays): 0} if into else {},
+            compiler_params=LIMIT,
+        )(*(near(a) for a in arrays), *into)
+
+    result = end(first_end_kernel, lambda core: core, (branch, top, later, pair), ())
+    result = end(second_end_kernel, lambda core: 1 - core, (branch, top, mate), (result,))
     return (result.reshape(1, rows, tokens), gain_grad)
 
 

time: 54.7 us -> 54.2 us (level)
  Pallas kernels: 10 us -> 11.7 us
  waiting for transfers between devices: 20.8 us -> 19.6 us
  local copies, waits for them, and re-layouts: 0.63 us -> 0.01 us
    pallas_call x6 -> x8, Pallas kernels: 1.31 us -> 2.34 us  [call(): pl.pallas_call(kernel, out_shape=out_shape, in_specs=[WHOLE] * len(arrays...]
    ppermute x6, waiting for transfers between devices: 8.55 us -> 7.6 us  [across(): lax.ppermute(value, 'section', [(s, s ^ 2 * distance) for s in range(laye...]
    pallas_call x1 -> x2, Pallas kernels: 1.02 us -> 1.66 us  [end(): pl.pallas_call(kernel, out_shape=jax.ShapeDtypeStruct((2, part, tokens),...]
    unnamed x7 -> x6, local copies, waits for them, and re-layouts: 0.62 us -> 0.01 us
  transfers between devices with their start and end apart: 19 -> 19, of which waited for: 15 -> 15; matrix products, arithmetic and copies ran while one was open for 2% -> 0% of each run, Pallas kernels for 11% -> 15%
where the time goes in v6:
time: 54.2 us; the launch traced here: 54.1 us
  starting transfers between devices  22 us (41%)
  waiting for transfers between devices  19.6 us (36%)
  Pallas kernels  11.7 us (22%)
  between operations  0.75 us (1%)
    ppermute x11, starting transfers between devices, exchange(): return lax.ppermute(value, 'tensor', [(i, i ^ mask) for i in range(count)])  13 us
    ppermute x11, waiting for transfers between devices, exchange(): return lax.ppermute(value, 'tensor', [(i, i ^ mask) for i in range(count)])  9.83 us
    ppermute x6, starting transfers between devices, across(): lax.ppermute(value, 'section', [(s, s ^ 2 * distance) for s in range(laye...  8.91 us
    ppermute x6, waiting for transfers between devices, across(): lax.ppermute(value, 'section', [(s, s ^ 2 * distance) for s in range(laye...  7.6 us
    pallas_call x3, Pallas kernels, product(): pl.pallas_call(keep_kernel if extra else multiply, out_shape=out_shape, g...  7.56 us
    pallas_call x8, Pallas kernels, call(): pl.pallas_call(kernel, out_shape=out_shape, in_specs=[WHOLE] * len(arrays...  2.34 us
    ppermute x2, waiting for transfers between devices, swap(): return lax.ppermute(value, 'section', [(s, s ^ 1) for s in range(layers)])  2.18 us
    pallas_call x2, Pallas kernels, end(): pl.pallas_call(kernel, out_shape=jax.ShapeDtypeStruct((2, part, tokens),...  1.66 us
  transfers between devices with their start and end apart: 19, of which 15 were waited for; matrix products, arithmetic and copies ran while one was open for 0% of the time, Pallas kernels for 15%

profile of v6, /device:TPU:0, one launch (start us, length us, event | category | flops | bytes accessed | tf_op | source)
XLA Modules:
  0.0 54.1 jit_solution(16202843158695961184)
XLA Ops:
  0.6 2.2 %shard_map.69 = (bf16[2,512,128]{2,1,0:T(8,128)(2,1)S(1)}, bf16[2,512,128]{2,1,0:T(8,128)(2,1)S(1)}) custom-call(bf16[8192,512]{1,0:T(8,128)(2,1)} %bitcast.21, bf16[8192,512]{1,0:T(8,128)(2,1)} %bitcast.22, bf16[128,512]{1,0:T(8,128)(2,1)} %bitcast.28), custom_call_target="tpu_custom_call" | custom-call | flops 268435456 | bytes 2621440 | tf_op jit(solution)/shard_map/pallas_call | solution.py:86
  2.9 3.0 %collective-permute-start = (bf16[2,512,128]{2,1,0:T(8,128)(2,1)S(1)}, bf16[2,512,128]{2,1,0:T(8,128)(2,1)S(1)}, u32[]{:S(2)}, u32[]{:S(2)}) collective-permute-start(bf16[2,512,128]{2,1,0:T(8,128)(2,1)S(1)} %get-tuple-element.32), channel_id=1, source_target_pairs={{0,1},{1,0},{2,3},{3,2},{4,5},{5,4},{6,7},{7,6},{8,9},{9,8},{10,11... | collective-permute-start | bytes 786440 | tf_op jit(solution)/shard_map/ppermute | solution.py:280
  5.9 1.5 %collective-permute-start.1 = (bf16[2,512,128]{2,1,0:T(8,128)(2,1)S(1)}, bf16[2,512,128]{2,1,0:T(8,128)(2,1)S(1)}, u32[]{:S(2)}, u32[]{:S(2)}) collective-permute-start(bf16[2,512,128]{2,1,0:T(8,128)(2,1)S(1)} %get-tuple-element.33), channel_id=1, source_target_pairs={{0,2},{1,3},{2,0},{3,1},{4,6},{5,7},{6,4},{7,5},{8,10},{9,11},{10,... | collective-permute-start | bytes 786440 | tf_op jit(solution)/shard_map/ppermute | solution.py:280
  7.4 2.2 %shard_map.70 = (bf16[2,512,128]{2,1,0:T(8,128)(2,1)S(1)}, bf16[2,512,128]{2,1,0:T(8,128)(2,1)S(1)}) custom-call(bf16[8192,512]{1,0:T(8,128)(2,1)} %bitcast.23, bf16[8192,512]{1,0:T(8,128)(2,1)} %bitcast.24, bf16[128,512]{1,0:T(8,128)(2,1)} %bitcast.29), custom_call_target="tpu_custom_call" | custom-call | flops 268435456 | bytes 2621440 | tf_op jit(solution)/shard_map/pallas_call | solution.py:86
  9.6 0.6 %collective-permute-start.2 = (bf16[2,512,128]{2,1,0:T(8,128)(2,1)S(1)}, bf16[2,512,128]{2,1,0:T(8,128)(2,1)S(1)}, u32[]{:S(2)}, u32[]{:S(2)}) collective-permute-start(bf16[2,512,128]{2,1,0:T(8,128)(2,1)S(1)} %get-tuple-element.34), channel_id=1, source_target_pairs={{0,1},{1,0},{2,3},{3,2},{4,5},{5,4},{6,7},{7,6},{8,9},{9,8},{10,11... | collective-permute-start | bytes 786440 | tf_op jit(solution)/shard_map/ppermute | solution.py:280
  10.3 3.2 %shard_map.68 = (bf16[2,1024,128]{2,1,0:T(8,128)(2,1)S(1)}, bf16[2,1024,128]{2,1,0:T(8,128)(2,1)S(1)}, f32[8,128]{1,0:T(8,128)S(1)}) custom-call(bf16[8192,512]{1,0:T(8,128)(2,1)} %bitcast.25, bf16[8192,512]{1,0:T(8,128)(2,1)} %bitcast.26, bf16[128,512]{1,0:T(8,128)(2,1)} %bitcast.30, bf16[2048,128]{1,0:T(8,128)(2,1)S(1)} %bitcast.11), custom_call_target="tpu_custom_call" | custom-call | flops 536870912 | bytes 5242880 | tf_op jit(solution)/shard_map/pallas_call | solution.py:86
  13.5 1.7 %collective-permute-done.1.refs_5_.refs_3_ = bf16[2,512,128]{2,1,0:T(8,128)(2,1)S(1)} collective-permute-done((bf16[2,512,128]{2,1,0:T(8,128)(2,1)S(1)}, bf16[2,512,128]{2,1,0:T(8,128)(2,1)S(1)}, u32[]{:S(2)}, u32[]{:S(2)}) %collective-permute-start.1) | collective-permute-done | bytes 262176 | tf_op jit(solution)/shard_map/ppermute | solution.py:280
  15.3 1.6 %collective-permute-start.4 = (bf16[2,512,128]{2,1,0:T(8,128)(2,1)S(1)}, bf16[2,512,128]{2,1,0:T(8,128)(2,1)S(1)}, u32[]{:S(2)}, u32[]{:S(2)}) collective-permute-start(bf16[2,512,128]{2,1,0:T(8,128)(2,1)S(1)} %get-tuple-element.36), channel_id=1, source_target_pairs={{0,2},{1,3},{2,0},{3,1},{4,6},{5,7},{6,4},{7,5},{8,10},{9,11},{10,... | collective-permute-start | bytes 786440 | tf_op jit(solution)/shard_map/ppermute | solution.py:280
  16.9 0.5 collective-permute-start.5
  17.4 1.3 %collective-permute-done.2.refs_2_.refs_4_ = bf16[2,512,128]{2,1,0:T(8,128)(2,1)S(1)} collective-permute-done((bf16[2,512,128]{2,1,0:T(8,128)(2,1)S(1)}, bf16[2,512,128]{2,1,0:T(8,128)(2,1)S(1)}, u32[]{:S(2)}, u32[]{:S(2)}) %collective-permute-start.2) | collective-permute-done | bytes 262176 | tf_op jit(solution)/shard_map/ppermute | solution.py:280
  18.8 1.9 %collective-permute-done.3.refs_3_.refs_5_ = bf16[2,512,128]{2,1,0:T(8,128)(2,1)S(1)} collective-permute-done((bf16[2,512,128]{2,1,0:T(8,128)(2,1)S(1)}, bf16[2,512,128]{2,1,0:T(8,128)(2,1)S(1)}, u32[]{:S(2)}, u32[]{:S(2)}) %collective-permute-start.3) | collective-permute-done | bytes 262176 | tf_op jit(solution)/shard_map/ppermute | solution.py:280
  20.8 1.6 %collective-permute-start.6 = (bf16[1,512,128]{2,1,0:T(8,128)(2,1)S(1)}, bf16[1,512,128]{2,1,0:T(8,128)(2,1)S(1)}, u32[]{:S(2)}, u32[]{:S(2)}) collective-permute-start(bf16[1,512,128]{2,1,0:T(8,128)(2,1)S(1)} %get-tuple-element.38), channel_id=1, source_target_pairs={{0,2},{1,3},{2,0},{3,1},{4,6},{5,7},{6,4},{7,5},{8,10},{9,11},{10,... | collective-permute-start | bytes 393224 | tf_op jit(solution)/shard_map/ppermute | solution.py:280
  22.9 3.4 %collective-permute-done.4.refs_6_ = bf16[2,512,128]{2,1,0:T(8,128)(2,1)S(1)} collective-permute-done((bf16[2,512,128]{2,1,0:T(8,128)(2,1)S(1)}, bf16[2,512,128]{2,1,0:T(8,128)(2,1)S(1)}, u32[]{:S(2)}, u32[]{:S(2)}) %collective-permute-start.4) | collective-permute-done | bytes 262176 | tf_op jit(solution)/shard_map/ppermute | solution.py:280
  26.7 1.6 %collective-permute-start.8 = (f32[16,128]{1,0:T(8,128)S(1)}, f32[16,128]{1,0:T(8,128)S(1)}, u32[]{:S(2)}, u32[]{:S(2)}) collective-permute-start(f32[16,128]{1,0:T(8,128)S(1)} %shard_map.74.refs_2_), channel_id=1, source_target_pairs={{0,3},{1,2},{2,1},{3,0},{4,7},{5,6},{6,5},{7,4},{8,11},{9,10},{10,... | collective-permute-start | bytes 24584 | tf_op jit(solution)/shard_map/ppermute | solution.py:280
  28.5 1.8 %collective-permute-start.10 = (f32[16,128]{1,0:T(8,128)S(1)}, f32[16,128]{1,0:T(8,128)S(1)}, u32[]{:S(2)}, u32[]{:S(2)}) collective-permute-start(f32[16,128]{1,0:T(8,128)S(1)} %shard_map.74.refs_2_), channel_id=1, source_target_pairs={{0,1},{1,0},{2,3},{3,2},{4,5},{5,4},{6,7},{7,6},{8,9},{9,8},{10,11... | collective-permute-start | bytes 24584 | tf_op jit(solution)/shard_map/ppermute | solution.py:280
  30.6 0.7 %collective-permute-done.8.refs_3_ = f32[16,128]{1,0:T(8,128)S(1)} collective-permute-done((f32[16,128]{1,0:T(8,128)S(1)}, f32[16,128]{1,0:T(8,128)S(1)}, u32[]{:S(2)}, u32[]{:S(2)}) %collective-permute-start.8) | collective-permute-done | bytes 8224 | tf_op jit(solution)/shard_map/ppermute | solution.py:280
  31.3 0.6 %collective-permute-done.9.refs_4_ = f32[16,128]{1,0:T(8,128)S(1)} collective-permute-done((f32[16,128]{1,0:T(8,128)S(1)}, f32[16,128]{1,0:T(8,128)S(1)}, u32[]{:S(2)}, u32[]{:S(2)}) %collective-permute-start.9) | collective-permute-done | bytes 8224 | tf_op jit(solution)/shard_map/ppermute | solution.py:280
  32.4 1.5 %collective-permute-done.11.came_ref = bf16[1024,128]{1,0:T(8,128)(2,1)S(1)} collective-permute-done((bf16[1024,128]{1,0:T(8,128)(2,1)S(1)}, bf16[1024,128]{1,0:T(8,128)(2,1)S(1)}, u32[]{:S(2)}, u32[]{:S(2)}) %collective-permute-start.11) | collective-permute-done | bytes 262176 | tf_op jit(solution)/shard_map/ppermute | solution.py:283
  34.0 3.7 %collective-permute-start.12 = (bf16[256,128]{1,0:T(8,128)(2,1)S(1)}, bf16[256,128]{1,0:T(8,128)(2,1)S(1)}, u32[]{:S(2)}, u32[]{:S(2)}) collective-permute-start(bf16[256,128]{1,0:T(8,128)(2,1)S(1)} %get-tuple-element.44), channel_id=1, source_target_pairs={{0,24},{4,28},{8,16},{12,20},{16,8},{20,12},{24,0},{28,4},{1,25},{... | collective-permute-start | bytes 196616 | tf_op jit(solution)/shard_map/ppermute | solution.py:288
  37.7 0.8 %collective-permute-start.14 = (bf16[256,128]{1,0:T(8,128)(2,1)S(1)}, bf16[256,128]{1,0:T(8,128)(2,1)S(1)}, u32[]{:S(2)}, u32[]{:S(2)}) collective-permute-start(bf16[256,128]{1,0:T(8,128)(2,1)S(1)} %get-tuple-element.46), channel_id=1, source_target_pairs={{0,16},{4,20},{8,24},{12,28},{16,0},{20,4},{24,8},{28,12},{1,17},{... | collective-permute-start | bytes 196616 | tf_op jit(solution)/shard_map/ppermute | solution.py:288
  38.5 0.9 %shard_map.77 = (f32[1,2048]{1,0:T(1,128)}, f32[8,128]{1,0:T(8,128)S(1)}) custom-call(f32[2,1024,128]{2,1,0:T(8,128)S(1)} %get-tuple-element.48.partial_ref, bf16[2048,128]{1,0:T(8,128)(2,1)S(1)} %bitcast.15, f32[8,128]{1,0:T(8,128)S(1)} %get-tuple-element.49.upside_ref), custom_call_target="tpu_custom_call" | custom-call | tf_op jit(solution)/shard_map/pallas_call | solution.py:257
  39.4 1.5 %collective-permute-done.12.refs_0_ = bf16[256,128]{1,0:T(8,128)(2,1)S(1)} collective-permute-done((bf16[256,128]{1,0:T(8,128)(2,1)S(1)}, bf16[256,128]{1,0:T(8,128)(2,1)S(1)}, u32[]{:S(2)}, u32[]{:S(2)}) %collective-permute-start.12) | collective-permute-done | bytes 65568 | tf_op jit(solution)/shard_map/ppermute | solution.py:288
  40.9 1.9 %collective-permute-done.13.refs_1_ = bf16[256,128]{1,0:T(8,128)(2,1)S(1)} collective-permute-done((bf16[256,128]{1,0:T(8,128)(2,1)S(1)}, bf16[256,128]{1,0:T(8,128)(2,1)S(1)}, u32[]{:S(2)}, u32[]{:S(2)}) %collective-permute-start.13) | collective-permute-done | bytes 65568 | tf_op jit(solution)/shard_map/ppermute | solution.py:288
  42.8 0.8 %collective-permute-done.14.refs_2_ = bf16[256,128]{1,0:T(8,128)(2,1)S(1)} collective-permute-done((bf16[256,128]{1,0:T(8,128)(2,1)S(1)}, bf16[256,128]{1,0:T(8,128)(2,1)S(1)}, u32[]{:S(2)}, u32[]{:S(2)}) %collective-permute-start.14) | collective-permute-done | bytes 65568 | tf_op jit(solution)/shard_map/ppermute | solution.py:288
  43.7 2.2 %collective-permute-start.15 = (bf16[256,128]{1,0:T(8,128)(2,1)S(1)}, bf16[256,128]{1,0:T(8,128)(2,1)S(1)}, u32[]{:S(2)}, u32[]{:S(2)}) collective-permute-start(bf16[256,128]{1,0:T(8,128)(2,1)S(1)} %get-tuple-element.51), channel_id=1, source_target_pairs={{0,24},{4,28},{8,16},{12,20},{16,8},{20,12},{24,0},{28,4},{1,25},{... | collective-permute-start | bytes 196616 | tf_op jit(solution)/shard_map/ppermute | solution.py:288
  46.3 1.9 %collective-permute-start.17 = (bf16[256,128]{1,0:T(8,128)(2,1)S(1)}, bf16[256,128]{1,0:T(8,128)(2,1)S(1)}, u32[]{:S(2)}, u32[]{:S(2)}) collective-permute-start(bf16[256,128]{1,0:T(8,128)(2,1)S(1)} %get-tuple-element.53), channel_id=1, source_target_pairs={{0,16},{4,20},{8,24},{12,28},{16,0},{20,4},{24,8},{28,12},{1,17},{... | collective-permute-start | bytes 196616 | tf_op jit(solution)/shard_map/ppermute | solution.py:288
  48.1 1.9 %collective-permute-done.15.refs_0_ = bf16[256,128]{1,0:T(8,128)(2,1)S(1)} collective-permute-done((bf16[256,128]{1,0:T(8,128)(2,1)S(1)}, bf16[256,128]{1,0:T(8,128)(2,1)S(1)}, u32[]{:S(2)}, u32[]{:S(2)}) %collective-permute-start.15) | collective-permute-done | bytes 65568 | tf_op jit(solution)/shard_map/ppermute | solution.py:288
  50.1 0.9 %collective-permute-done.16.refs_1_ = bf16[256,128]{1,0:T(8,128)(2,1)S(1)} collective-permute-done((bf16[256,128]{1,0:T(8,128)(2,1)S(1)}, bf16[256,128]{1,0:T(8,128)(2,1)S(1)}, u32[]{:S(2)}, u32[]{:S(2)}) %collective-permute-start.16) | collective-permute-done | bytes 65568 | tf_op jit(solution)/shard_map/ppermute | solution.py:288
  51.0 0.6 %collective-permute-done.17.refs_2_ = bf16[256,128]{1,0:T(8,128)(2,1)S(1)} collective-permute-done((bf16[256,128]{1,0:T(8,128)(2,1)S(1)}, bf16[256,128]{1,0:T(8,128)(2,1)S(1)}, u32[]{:S(2)}, u32[]{:S(2)}) %collective-permute-start.17) | collective-permute-done | bytes 65568 | tf_op jit(solution)/shard_map/ppermute | solution.py:288
  51.8 0.9 %shard_map.80.result_ref = bf16[2,1024,128]{2,1,0:T(8,128)(2,1)} custom-call(f32[2,1024,128]{2,1,0:T(8,128)S(1)} %get-tuple-element.42.branch_ref, bf16[2,1024,128]{2,1,0:T(8,128)(2,1)S(1)} %bitcast.16, bf16[1024,128]{1,0:T(8,128)(2,1)S(1)} %bitcast.19, bf16[1024,128]{1,0:T(8,128)(2,1)S(1)} %collective-permute-done.11.came_ref), custom_call_target="tpu_custom_call" | custom-call | tf_op jit(solution)/shard_map/pallas_call | solution.py:369
  52.6 0.7 %collective-permute-done.18.mate_ref = bf16[1024,128]{1,0:T(8,128)(2,1)S(1)} collective-permute-done((bf16[1024,128]{1,0:T(8,128)(2,1)S(1)}, bf16[1024,128]{1,0:T(8,128)(2,1)S(1)}, u32[]{:S(2)}, u32[]{:S(2)}) %collective-permute-start.18) | collective-permute-done | bytes 262176 | tf_op jit(solution)/shard_map/ppermute | solution.py:283
  53.3 0.8 %shard_map.81 = bf16[2,1024,128]{2,1,0:T(8,128)(2,1)} custom-call(f32[2,1024,128]{2,1,0:T(8,128)S(1)} %get-tuple-element.42.branch_ref, bf16[2,1024,128]{2,1,0:T(8,128)(2,1)S(1)} %bitcast.17, bf16[1024,128]{1,0:T(8,128)(2,1)S(1)} %collective-permute-done.18.mate_ref, bf16[2,1024,128]{2,1,0:T(8,128)(2,1)} %shard_map.80.result_ref), custom_call_target="tpu_custom_call", output_to_operand_aliasing={{}: (3, {})} | custom-call | tf_op jit(solution)/shard_map/pallas_call | solution.py:369
  (26 shorter events, 3.2 us)
Async XLA Ops:
  2.9 10.6 %collective-permute-start = (bf16[2,512,128]{2,1,0:T(8,128)(2,1)S(1)}, bf16[2,512,128]{2,1,0:T(8,128)(2,1)S(1)}, u32[]{:S(2)}, u32[]{:S(2)}) collective-permute-start(bf16[2,512,128]{2,1,0:T(8,128)(2,1)S(1)} %get-tuple-element.32), channel_id=1, source_target_pairs={{0,1},{1,0},{2,3},{3,2},{4,5},{5,4},{6,7},{7,6},{8,9},{9,8},{10,11... | collective-permute-start | bytes 786440 | tf_op jit(solution)/shard_map/ppermute | solution.py:280
  5.9 4.4 %copy-start = (bf16[1,2048,128]{2,1,0:T(8,128)(2,1)S(1)}, bf16[1,2048,128]{2,1,0:T(8,128)(2,1)}, u32[]{:S(2)}) copy-start(bf16[1,2048,128]{2,1,0:T(8,128)(2,1)} %param.5) | copy-start | bytes 1572868
  5.9 9.2 %collective-permute-start.1 = (bf16[2,512,128]{2,1,0:T(8,128)(2,1)S(1)}, bf16[2,512,128]{2,1,0:T(8,128)(2,1)S(1)}, u32[]{:S(2)}, u32[]{:S(2)}) collective-permute-start(bf16[2,512,128]{2,1,0:T(8,128)(2,1)S(1)} %get-tuple-element.33), channel_id=1, source_target_pairs={{0,2},{1,3},{2,0},{3,1},{4,6},{5,7},{6,4},{7,5},{8,10},{9,11},{10,... | collective-permute-start | bytes 786440 | tf_op jit(solution)/shard_map/ppermute | solution.py:280
  9.6 9.2 %collective-permute-start.2 = (bf16[2,512,128]{2,1,0:T(8,128)(2,1)S(1)}, bf16[2,512,128]{2,1,0:T(8,128)(2,1)S(1)}, u32[]{:S(2)}, u32[]{:S(2)}) collective-permute-start(bf16[2,512,128]{2,1,0:T(8,128)(2,1)S(1)} %get-tuple-element.34), channel_id=1, source_target_pairs={{0,1},{1,0},{2,3},{3,2},{4,5},{5,4},{6,7},{7,6},{8,9},{9,8},{10,11... | collective-permute-start | bytes 786440 | tf_op jit(solution)/shard_map/ppermute | solution.py:280
  10.2 10.6 %collective-permute-start.3 = (bf16[2,512,128]{2,1,0:T(8,128)(2,1)S(1)}, bf16[2,512,128]{2,1,0:T(8,128)(2,1)S(1)}, u32[]{:S(2)}, u32[]{:S(2)}) collective-permute-start(bf16[2,512,128]{2,1,0:T(8,128)(2,1)S(1)} %get-tuple-element.35), channel_id=1, source_target_pairs={{0,2},{1,3},{2,0},{3,1},{4,6},{5,7},{6,4},{7,5},{8,10},{9,11},{10,... | collective-permute-start | bytes 786440 | tf_op jit(solution)/shard_map/ppermute | solution.py:280
  10.3 4.8 %copy-start.2 = (f32[1,2048]{1,0:T(1,128)S(1)}, f32[1,2048]{1,0:T(1,128)}, u32[]{:S(2)}) copy-start(f32[1,2048]{1,0:T(1,128)} %refs_9_.1) | copy-start | bytes 24580
  15.3 10.9 %collective-permute-start.4 = (bf16[2,512,128]{2,1,0:T(8,128)(2,1)S(1)}, bf16[2,512,128]{2,1,0:T(8,128)(2,1)S(1)}, u32[]{:S(2)}, u32[]{:S(2)}) collective-permute-start(bf16[2,512,128]{2,1,0:T(8,128)(2,1)S(1)} %get-tuple-element.36), channel_id=1, source_target_pairs={{0,2},{1,3},{2,0},{3,1},{4,6},{5,7},{6,4},{7,5},{8,10},{9,11},{10,... | collective-permute-start | bytes 786440 | tf_op jit(solution)/shard_map/ppermute | solution.py:280
  16.9 9.4 %collective-permute-start.5 = (bf16[2,512,128]{2,1,0:T(8,128)(2,1)S(1)}, bf16[2,512,128]{2,1,0:T(8,128)(2,1)S(1)}, u32[]{:S(2)}, u32[]{:S(2)}) collective-permute-start(bf16[2,512,128]{2,1,0:T(8,128)(2,1)S(1)} %get-tuple-element.37), channel_id=1, source_target_pairs={{0,1},{1,0},{2,3},{3,2},{4,5},{5,4},{6,7},{7,6},{8,9},{9,8},{10,11... | collective-permute-start | bytes 786440 | tf_op jit(solution)/shard_map/ppermute | solution.py:280
  20.8 9.5 %collective-permute-start.6 = (bf16[1,512,128]{2,1,0:T(8,128)(2,1)S(1)}, bf16[1,512,128]{2,1,0:T(8,128)(2,1)S(1)}, u32[]{:S(2)}, u32[]{:S(2)}) collective-permute-start(bf16[1,512,128]{2,1,0:T(8,128)(2,1)S(1)} %get-tuple-element.38), channel_id=1, source_target_pairs={{0,2},{1,3},{2,0},{3,1},{4,6},{5,7},{6,4},{7,5},{8,10},{9,11},{10,... | collective-permute-start | bytes 393224 | tf_op jit(solution)/shard_map/ppermute | solution.py:280
  22.4 7.9 %collective-permute-start.7 = (bf16[1,512,128]{2,1,0:T(8,128)(2,1)S(1)}, bf16[1,512,128]{2,1,0:T(8,128)(2,1)S(1)}, u32[]{:S(2)}, u32[]{:S(2)}) collective-permute-start(bf16[1,512,128]{2,1,0:T(8,128)(2,1)S(1)} %get-tuple-element.39), channel_id=1, source_target_pairs={{0,1},{1,0},{2,3},{3,2},{4,5},{5,4},{6,7},{7,6},{8,9},{9,8},{10,11... | collective-permute-start | bytes 393224 | tf_op jit(solution)/shard_map/ppermute | solution.py:280
  26.7 25.1 %copy-start.1 = (bf16[2048,128]{1,0:T(8,128)(2,1)S(1)}, bf16[2048,128]{1,0:T(8,128)(2,1)}, u32[]{:S(2)}) copy-start(bf16[2048,128]{1,0:T(8,128)(2,1)} %param.9) | copy-start | bytes 1572868
  26.7 4.6 %collective-permute-start.8 = (f32[16,128]{1,0:T(8,128)S(1)}, f32[16,128]{1,0:T(8,128)S(1)}, u32[]{:S(2)}, u32[]{:S(2)}) collective-permute-start(f32[16,128]{1,0:T(8,128)S(1)} %shard_map.74.refs_2_), channel_id=1, source_target_pairs={{0,3},{1,2},{2,1},{3,0},{4,7},{5,6},{6,5},{7,4},{8,11},{9,10},{10,... | collective-permute-start | bytes 24584 | tf_op jit(solution)/shard_map/ppermute | solution.py:280
  28.3 3.7 %collective-permute-start.9 = (f32[16,128]{1,0:T(8,128)S(1)}, f32[16,128]{1,0:T(8,128)S(1)}, u32[]{:S(2)}, u32[]{:S(2)}) collective-permute-start(f32[16,128]{1,0:T(8,128)S(1)} %shard_map.74.refs_2_), channel_id=1, source_target_pairs={{0,2},{1,3},{2,0},{3,1},{4,6},{5,7},{6,4},{7,5},{8,10},{9,11},{10,... | collective-permute-start | bytes 24584 | tf_op jit(solution)/shard_map/ppermute | solution.py:280
  28.5 3.7 %collective-permute-start.10 = (f32[16,128]{1,0:T(8,128)S(1)}, f32[16,128]{1,0:T(8,128)S(1)}, u32[]{:S(2)}, u32[]{:S(2)}) collective-permute-start(f32[16,128]{1,0:T(8,128)S(1)} %shard_map.74.refs_2_), channel_id=1, source_target_pairs={{0,1},{1,0},{2,3},{3,2},{4,5},{5,4},{6,7},{7,6},{8,9},{9,8},{10,11... | collective-permute-start | bytes 24584 | tf_op jit(solution)/shard_map/ppermute | solution.py:280
  32.3 1.6 %collective-permute-start.11 = (bf16[1024,128]{1,0:T(8,128)(2,1)S(1)}, bf16[1024,128]{1,0:T(8,128)(2,1)S(1)}, u32[]{:S(2)}, u32[]{:S(2)}) collective-permute-start(bf16[1024,128]{1,0:T(8,128)(2,1)S(1)} %get-tuple-element.43), channel_id=1, source_target_pairs={{0,4},{4,0},{8,12},{12,8},{16,20},{20,16},{24,28},{28,24},{1,5},{5... | collective-permute-start | bytes 786440 | tf_op jit(solution)/shard_map/ppermute | solution.py:283
  34.0 6.9 %collective-permute-start.12 = (bf16[256,128]{1,0:T(8,128)(2,1)S(1)}, bf16[256,128]{1,0:T(8,128)(2,1)S(1)}, u32[]{:S(2)}, u32[]{:S(2)}) collective-permute-start(bf16[256,128]{1,0:T(8,128)(2,1)S(1)} %get-tuple-element.44), channel_id=1, source_target_pairs={{0,24},{4,28},{8,16},{12,20},{16,8},{20,12},{24,0},{28,4},{1,25},{... | collective-permute-start | bytes 196616 | tf_op jit(solution)/shard_map/ppermute | solution.py:288
  37.7 5.1 %collective-permute-start.13 = (bf16[256,128]{1,0:T(8,128)(2,1)S(1)}, bf16[256,128]{1,0:T(8,128)(2,1)S(1)}, u32[]{:S(2)}, u32[]{:S(2)}) collective-permute-start(bf16[256,128]{1,0:T(8,128)(2,1)S(1)} %get-tuple-element.45), channel_id=1, source_target_pairs={{0,8},{4,12},{8,0},{12,4},{16,24},{20,28},{24,16},{28,20},{1,9},{5... | collective-permute-start | bytes 196616 | tf_op jit(solution)/shard_map/ppermute | solution.py:288
  37.7 5.9 %collective-permute-start.14 = (bf16[256,128]{1,0:T(8,128)(2,1)S(1)}, bf16[256,128]{1,0:T(8,128)(2,1)S(1)}, u32[]{:S(2)}, u32[]{:S(2)}) collective-permute-start(bf16[256,128]{1,0:T(8,128)(2,1)S(1)} %get-tuple-element.46), channel_id=1, source_target_pairs={{0,16},{4,20},{8,24},{12,28},{16,0},{20,4},{24,8},{28,12},{1,17},{... | collective-permute-start | bytes 196616 | tf_op jit(solution)/shard_map/ppermute | solution.py:288
  43.7 6.4 %collective-permute-start.15 = (bf16[256,128]{1,0:T(8,128)(2,1)S(1)}, bf16[256,128]{1,0:T(8,128)(2,1)S(1)}, u32[]{:S(2)}, u32[]{:S(2)}) collective-permute-start(bf16[256,128]{1,0:T(8,128)(2,1)S(1)} %get-tuple-element.51), channel_id=1, source_target_pairs={{0,24},{4,28},{8,16},{12,20},{16,8},{20,12},{24,0},{28,4},{1,25},{... | collective-permute-start | bytes 196616 | tf_op jit(solution)/shard_map/ppermute | solution.py:288
  45.9 5.1 %collective-permute-start.16 = (bf16[256,128]{1,0:T(8,128)(2,1)S(1)}, bf16[256,128]{1,0:T(8,128)(2,1)S(1)}, u32[]{:S(2)}, u32[]{:S(2)}) collective-permute-start(bf16[256,128]{1,0:T(8,128)(2,1)S(1)} %get-tuple-element.52), channel_id=1, source_target_pairs={{0,8},{4,12},{8,0},{12,4},{16,24},{20,28},{24,16},{28,20},{1,9},{5... | collective-permute-start | bytes 196616 | tf_op jit(solution)/shard_map/ppermute | solution.py:288
  46.3 5.3 %collective-permute-start.17 = (bf16[256,128]{1,0:T(8,128)(2,1)S(1)}, bf16[256,128]{1,0:T(8,128)(2,1)S(1)}, u32[]{:S(2)}, u32[]{:S(2)}) collective-permute-start(bf16[256,128]{1,0:T(8,128)(2,1)S(1)} %get-tuple-element.53), channel_id=1, source_target_pairs={{0,16},{4,20},{8,24},{12,28},{16,0},{20,4},{24,8},{28,12},{1,17},{... | collective-permute-start | bytes 196616 | tf_op jit(solution)/shard_map/ppermute | solution.py:288
  51.7 1.6 %collective-permute-start.18 = (bf16[1024,128]{1,0:T(8,128)(2,1)S(1)}, bf16[1024,128]{1,0:T(8,128)(2,1)S(1)}, u32[]{:S(2)}, u32[]{:S(2)}) collective-permute-start(bf16[1024,128]{1,0:T(8,128)(2,1)S(1)} %bitcast.20), channel_id=1, source_target_pairs={{0,4},{4,0},{8,12},{12,8},{16,20},{20,16},{24,28},{28,24},{1,5},{5... | collective-permute-start | bytes 786440 | tf_op jit(solution)/shard_map/ppermute | solution.py:283

commit v7 on v6

--- a/solution.py
+++ b/solution.py
@@ -134,9 +134,8 @@
             out[1, pl.ds(start, width)] = gained.astype(out.dtype)
 
 
-def inner_kernel(pieces, *refs):
-    held, (inputs_ref, gains_ref, squares_ref, sums_out) = refs[:-4], refs[-4:]
-    gained = held[-2:]
+def early_kernel(pieces, *refs):
+    held, (inputs_ref, gains_ref, inner_out, pairs_out, gained_out) = refs[:-5], refs[-5:]
     part = held[0].shape[1]
     tokens = inputs_ref.shape[1]
     size = part // pieces
@@ -149,11 +148,27 @@
                 row = h * part + a * size + start
                 factor = wide(gains_ref, row, width, tokens) * inputs_ref[pl.ds(row, width)].astype(F32)
                 product = sum(p[0, pl.ds(first + start, width)].astype(F32) for p, first in parts) * factor
+                inner = inner + jnp.sum(product.reshape(width // 8, 8, tokens), axis=0)
                 if a == pieces - 1:
-                    factor = gained[h][1, pl.ds(start, width)].astype(F32)
                     total = sum(p[1, pl.ds(first + start, width)].astype(F32) for p, first in parts)
-                    product = product + total * factor
-                inner = inner + jnp.sum(product.reshape(width // 8, 8, tokens), axis=0)
+                    pairs_out[h, pl.ds(start, width)] = total
+                else:
+                    gained_out[h, pl.ds(a * size + start, width)] = factor
+    inner_out[...] = inner
+
+
+def inner_kernel(pieces, inner_ref, pairs_ref, gained_ref, squares_ref, *refs):
+    came, sums_out = refs[:-1], refs[-1]
+    _, size, tokens = pairs_ref.shape
+    width = tile_of(size)
+    inner = inner_ref[...]
+    for h in range(2):
+        for start in range(0, size, width):
+            at = pl.ds(start, width)
+            product = pairs_ref[h, at] * came[h][1, at].astype(F32)
+            for a in range(pieces - 1):
+                product = product + gained_ref[h, pl.ds(a * size + start, width)] * came[2 * a + h][0, at].astype(F32)
+            inner = inner + jnp.sum(product.reshape(width // 8, 8, tokens), axis=0)
     sums_out[...] = jnp.concatenate([squares_ref[...], inner])
 
 
@@ -305,18 +320,30 @@
                 total = call(lambda *refs: add_kernel(a, PIECES, *refs), outs, *kept, *held[a])
             held[a] = held[a] + [exchange(total[h], mask_of(h, step, count)) for h in range(2)]
     arrived = [v for step in range(steps) for a in range(PIECES) for v in held[a][2 * step : 2 * step + 2]]
+    done = 2 * PIECES * (steps - 1)
+    early = call(
+        lambda *refs: early_kernel(PIECES, *refs),
+        [
+            pltpu.VMEM((8, tokens), F32),
+            pltpu.VMEM((2, size, tokens), F32),
+            pltpu.VMEM((2, part - size, tokens), F32),
+        ],
+        *kept,
+        *arrived[:done],
+        inputs,
+        norm_gains,
+        cost=pl.CostEstimate(flops=1 << 32, bytes_accessed=1 << 20, transcendentals=0),
+    )
     sums = call(
         lambda *refs: inner_kernel(PIECES, *refs),
         pltpu.VMEM((16, tokens), F32),
-        *kept,
-        *arrived[:-2],
-        inputs,
-        norm_gains,
+        *early,
         squares,
+        *arrived[done:-2],
     )
     sums, low = [sums], 1
     while low < count:
-        group = [low] if 2 * low >= count else [3 * low, 2 * low, low]
+        group = [low] if 2 * low >= count else [2 * low, 1 * low, 3 * low]
         total = sum(sums)
         sums = [total] + [exchange(total, m) for m in group]
         low *= 4

time: 54.2 us -> 53.9 us (level)
    pallas_call x8 -> x9, Pallas kernels: 2.34 us -> 2.37 us  [call(): pl.pallas_call(kernel, out_shape=out_shape, in_specs=[WHOLE] * len(arrays...]
where the time goes in v7:
time: 53.9 us; the launch traced here: 53.8 us
  starting transfers between devices  22 us (41%)
  waiting for transfers between devices  19.2 us (36%)
  Pallas kernels  11.7 us (22%)
  between operations  0.76 us (1%)
    ppermute x11, starting transfers between devices, exchange(): return lax.ppermute(value, 'tensor', [(i, i ^ mask) for i in range(count)])  13 us
    ppermute x11, waiting for transfers between devices, exchange(): return lax.ppermute(value, 'tensor', [(i, i ^ mask) for i in range(count)])  9.47 us
    ppermute x6, starting transfers between devices, across(): lax.ppermute(value, 'section', [(s, s ^ 2 * distance) for s in range(laye...  8.91 us
    ppermute x6, waiting for transfers between devices, across(): lax.ppermute(value, 'section', [(s, s ^ 2 * distance) for s in range(laye...  7.6 us
    pallas_call x3, Pallas kernels, product(): pl.pallas_call(keep_kernel if extra else multiply, out_shape=out_shape, g...  7.56 us
    pallas_call x9, Pallas kernels, call(): pl.pallas_call(kernel, out_shape=out_shape, in_specs=[WHOLE] * len(arrays...  2.37 us
    ppermute x2, waiting for transfers between devices, swap(): return lax.ppermute(value, 'section', [(s, s ^ 1) for s in range(layers)])  2.18 us
    pallas_call x2, Pallas kernels, end(): pl.pallas_call(kernel, out_shape=jax.ShapeDtypeStruct((2, part, tokens),...  1.66 us
  transfers between devices with their start and end apart: 19, of which 15 were waited for; matrix products, arithmetic and copies ran while one was open for 0% of the time, Pallas kernels for 15%

profile of v7, /device:TPU:0, one launch (start us, length us, event | category | flops | bytes accessed | tf_op | source)
XLA Modules:
  0.0 53.8 jit_solution(15535000838996194728)
XLA Ops:
  0.6 2.2 %shard_map.69 = (bf16[2,512,128]{2,1,0:T(8,128)(2,1)S(1)}, bf16[2,512,128]{2,1,0:T(8,128)(2,1)S(1)}) custom-call(bf16[8192,512]{1,0:T(8,128)(2,1)} %bitcast.21, bf16[8192,512]{1,0:T(8,128)(2,1)} %bitcast.22, bf16[128,512]{1,0:T(8,128)(2,1)} %bitcast.28), custom_call_target="tpu_custom_call" | custom-call | flops 268435456 | bytes 2621440 | tf_op jit(solution)/shard_map/pallas_call | solution.py:86
  2.9 3.0 %collective-permute-start = (bf16[2,512,128]{2,1,0:T(8,128)(2,1)S(1)}, bf16[2,512,128]{2,1,0:T(8,128)(2,1)S(1)}, u32[]{:S(2)}, u32[]{:S(2)}) collective-permute-start(bf16[2,512,128]{2,1,0:T(8,128)(2,1)S(1)} %get-tuple-element.35), channel_id=1, source_target_pairs={{0,1},{1,0},{2,3},{3,2},{4,5},{5,4},{6,7},{7,6},{8,9},{9,8},{10,11... | collective-permute-start | bytes 786440 | tf_op jit(solution)/shard_map/ppermute | solution.py:295
  5.9 1.5 %collective-permute-start.1 = (bf16[2,512,128]{2,1,0:T(8,128)(2,1)S(1)}, bf16[2,512,128]{2,1,0:T(8,128)(2,1)S(1)}, u32[]{:S(2)}, u32[]{:S(2)}) collective-permute-start(bf16[2,512,128]{2,1,0:T(8,128)(2,1)S(1)} %get-tuple-element.36), channel_id=1, source_target_pairs={{0,2},{1,3},{2,0},{3,1},{4,6},{5,7},{6,4},{7,5},{8,10},{9,11},{10,... | collective-permute-start | bytes 786440 | tf_op jit(solution)/shard_map/ppermute | solution.py:295
  7.4 2.2 %shard_map.70 = (bf16[2,512,128]{2,1,0:T(8,128)(2,1)S(1)}, bf16[2,512,128]{2,1,0:T(8,128)(2,1)S(1)}) custom-call(bf16[8192,512]{1,0:T(8,128)(2,1)} %bitcast.23, bf16[8192,512]{1,0:T(8,128)(2,1)} %bitcast.24, bf16[128,512]{1,0:T(8,128)(2,1)} %bitcast.29), custom_call_target="tpu_custom_call" | custom-call | flops 268435456 | bytes 2621440 | tf_op jit(solution)/shard_map/pallas_call | solution.py:86
  9.6 0.6 %collective-permute-start.2 = (bf16[2,512,128]{2,1,0:T(8,128)(2,1)S(1)}, bf16[2,512,128]{2,1,0:T(8,128)(2,1)S(1)}, u32[]{:S(2)}, u32[]{:S(2)}) collective-permute-start(bf16[2,512,128]{2,1,0:T(8,128)(2,1)S(1)} %get-tuple-element.37), channel_id=1, source_target_pairs={{0,1},{1,0},{2,3},{3,2},{4,5},{5,4},{6,7},{7,6},{8,9},{9,8},{10,11... | collective-permute-start | bytes 786440 | tf_op jit(solution)/shard_map/ppermute | solution.py:295
  10.3 3.2 %shard_map.68 = (bf16[2,1024,128]{2,1,0:T(8,128)(2,1)S(1)}, bf16[2,1024,128]{2,1,0:T(8,128)(2,1)S(1)}, f32[8,128]{1,0:T(8,128)S(1)}) custom-call(bf16[8192,512]{1,0:T(8,128)(2,1)} %bitcast.25, bf16[8192,512]{1,0:T(8,128)(2,1)} %bitcast.26, bf16[128,512]{1,0:T(8,128)(2,1)} %bitcast.30, bf16[2048,128]{1,0:T(8,128)(2,1)S(1)} %bitcast.11), custom_call_target="tpu_custom_call" | custom-call | flops 536870912 | bytes 5242880 | tf_op jit(solution)/shard_map/pallas_call | solution.py:86
  13.5 1.7 %collective-permute-done.1.refs_5_.refs_3_ = bf16[2,512,128]{2,1,0:T(8,128)(2,1)S(1)} collective-permute-done((bf16[2,512,128]{2,1,0:T(8,128)(2,1)S(1)}, bf16[2,512,128]{2,1,0:T(8,128)(2,1)S(1)}, u32[]{:S(2)}, u32[]{:S(2)}) %collective-permute-start.1) | collective-permute-done | bytes 262176 | tf_op jit(solution)/shard_map/ppermute | solution.py:295
  15.3 1.6 %collective-permute-start.4 = (bf16[2,512,128]{2,1,0:T(8,128)(2,1)S(1)}, bf16[2,512,128]{2,1,0:T(8,128)(2,1)S(1)}, u32[]{:S(2)}, u32[]{:S(2)}) collective-permute-start(bf16[2,512,128]{2,1,0:T(8,128)(2,1)S(1)} %get-tuple-element.39), channel_id=1, source_target_pairs={{0,2},{1,3},{2,0},{3,1},{4,6},{5,7},{6,4},{7,5},{8,10},{9,11},{10,... | collective-permute-start | bytes 786440 | tf_op jit(solution)/shard_map/ppermute | solution.py:295
  16.9 0.5 collective-permute-start.5
  17.4 1.3 %collective-permute-done.2.refs_2_.refs_4_ = bf16[2,512,128]{2,1,0:T(8,128)(2,1)S(1)} collective-permute-done((bf16[2,512,128]{2,1,0:T(8,128)(2,1)S(1)}, bf16[2,512,128]{2,1,0:T(8,128)(2,1)S(1)}, u32[]{:S(2)}, u32[]{:S(2)}) %collective-permute-start.2) | collective-permute-done | bytes 262176 | tf_op jit(solution)/shard_map/ppermute | solution.py:295
  18.8 1.9 %collective-permute-done.3.refs_3_.refs_5_ = bf16[2,512,128]{2,1,0:T(8,128)(2,1)S(1)} collective-permute-done((bf16[2,512,128]{2,1,0:T(8,128)(2,1)S(1)}, bf16[2,512,128]{2,1,0:T(8,128)(2,1)S(1)}, u32[]{:S(2)}, u32[]{:S(2)}) %collective-permute-start.3) | collective-permute-done | bytes 262176 | tf_op jit(solution)/shard_map/ppermute | solution.py:295
  20.8 1.6 %collective-permute-start.6 = (bf16[1,512,128]{2,1,0:T(8,128)(2,1)S(1)}, bf16[1,512,128]{2,1,0:T(8,128)(2,1)S(1)}, u32[]{:S(2)}, u32[]{:S(2)}) collective-permute-start(bf16[1,512,128]{2,1,0:T(8,128)(2,1)S(1)} %get-tuple-element.41), channel_id=1, source_target_pairs={{0,2},{1,3},{2,0},{3,1},{4,6},{5,7},{6,4},{7,5},{8,10},{9,11},{10,... | collective-permute-start | bytes 393224 | tf_op jit(solution)/shard_map/ppermute | solution.py:295
  23.3 3.0 %collective-permute-done.4.refs_6_.refs_4_ = bf16[2,512,128]{2,1,0:T(8,128)(2,1)S(1)} collective-permute-done((bf16[2,512,128]{2,1,0:T(8,128)(2,1)S(1)}, bf16[2,512,128]{2,1,0:T(8,128)(2,1)S(1)}, u32[]{:S(2)}, u32[]{:S(2)}) %collective-permute-start.4) | collective-permute-done | bytes 262176 | tf_op jit(solution)/shard_map/ppermute | solution.py:295
  26.4 1.6 %collective-permute-start.10 = (f32[16,128]{1,0:T(8,128)S(1)}, f32[16,128]{1,0:T(8,128)S(1)}, u32[]{:S(2)}, u32[]{:S(2)}) collective-permute-start(f32[16,128]{1,0:T(8,128)S(1)} %shard_map.75.refs_2_), channel_id=1, source_target_pairs={{0,3},{1,2},{2,1},{3,0},{4,7},{5,6},{6,5},{7,4},{8,11},{9,10},{10,... | collective-permute-start | bytes 24584 | tf_op jit(solution)/shard_map/ppermute | solution.py:295
  28.2 1.8 %collective-permute-start.9 = (f32[16,128]{1,0:T(8,128)S(1)}, f32[16,128]{1,0:T(8,128)S(1)}, u32[]{:S(2)}, u32[]{:S(2)}) collective-permute-start(f32[16,128]{1,0:T(8,128)S(1)} %shard_map.75.refs_2_), channel_id=1, source_target_pairs={{0,1},{1,0},{2,3},{3,2},{4,5},{5,4},{6,7},{7,6},{8,9},{9,8},{10,11... | collective-permute-start | bytes 24584 | tf_op jit(solution)/shard_map/ppermute | solution.py:295
  30.3 0.7 %collective-permute-done.10.refs_5_ = f32[16,128]{1,0:T(8,128)S(1)} collective-permute-done((f32[16,128]{1,0:T(8,128)S(1)}, f32[16,128]{1,0:T(8,128)S(1)}, u32[]{:S(2)}, u32[]{:S(2)}) %collective-permute-start.10) | collective-permute-done | bytes 8224 | tf_op jit(solution)/shard_map/ppermute | solution.py:295
  31.0 0.6 %collective-permute-done.8.refs_3_ = f32[16,128]{1,0:T(8,128)S(1)} collective-permute-done((f32[16,128]{1,0:T(8,128)S(1)}, f32[16,128]{1,0:T(8,128)S(1)}, u32[]{:S(2)}, u32[]{:S(2)}) %collective-permute-start.8) | collective-permute-done | bytes 8224 | tf_op jit(solution)/shard_map/ppermute | solution.py:295
  32.1 1.5 %collective-permute-done.11.came_ref = bf16[1024,128]{1,0:T(8,128)(2,1)S(1)} collective-permute-done((bf16[1024,128]{1,0:T(8,128)(2,1)S(1)}, bf16[1024,128]{1,0:T(8,128)(2,1)S(1)}, u32[]{:S(2)}, u32[]{:S(2)}) %collective-permute-start.11) | collective-permute-done | bytes 262176 | tf_op jit(solution)/shard_map/ppermute | solution.py:298
  33.7 3.7 %collective-permute-start.12 = (bf16[256,128]{1,0:T(8,128)(2,1)S(1)}, bf16[256,128]{1,0:T(8,128)(2,1)S(1)}, u32[]{:S(2)}, u32[]{:S(2)}) collective-permute-start(bf16[256,128]{1,0:T(8,128)(2,1)S(1)} %get-tuple-element.50), channel_id=1, source_target_pairs={{0,24},{4,28},{8,16},{12,20},{16,8},{20,12},{24,0},{28,4},{1,25},{... | collective-permute-start | bytes 196616 | tf_op jit(solution)/shard_map/ppermute | solution.py:303
  37.4 0.8 %collective-permute-start.14 = (bf16[256,128]{1,0:T(8,128)(2,1)S(1)}, bf16[256,128]{1,0:T(8,128)(2,1)S(1)}, u32[]{:S(2)}, u32[]{:S(2)}) collective-permute-start(bf16[256,128]{1,0:T(8,128)(2,1)S(1)} %get-tuple-element.52), channel_id=1, source_target_pairs={{0,16},{4,20},{8,24},{12,28},{16,0},{20,4},{24,8},{28,12},{1,17},{... | collective-permute-start | bytes 196616 | tf_op jit(solution)/shard_map/ppermute | solution.py:303
  38.1 0.9 %shard_map.78 = (f32[1,2048]{1,0:T(1,128)}, f32[8,128]{1,0:T(8,128)S(1)}) custom-call(f32[2,1024,128]{2,1,0:T(8,128)S(1)} %get-tuple-element.54.partial_ref, bf16[2048,128]{1,0:T(8,128)(2,1)S(1)} %bitcast.15, f32[8,128]{1,0:T(8,128)S(1)} %get-tuple-element.55.upside_ref), custom_call_target="tpu_custom_call" | custom-call | tf_op jit(solution)/shard_map/pallas_call | solution.py:272
  39.1 1.5 %collective-permute-done.12.refs_0_ = bf16[256,128]{1,0:T(8,128)(2,1)S(1)} collective-permute-done((bf16[256,128]{1,0:T(8,128)(2,1)S(1)}, bf16[256,128]{1,0:T(8,128)(2,1)S(1)}, u32[]{:S(2)}, u32[]{:S(2)}) %collective-permute-start.12) | collective-permute-done | bytes 65568 | tf_op jit(solution)/shard_map/ppermute | solution.py:303
  40.6 1.9 %collective-permute-done.13.refs_1_ = bf16[256,128]{1,0:T(8,128)(2,1)S(1)} collective-permute-done((bf16[256,128]{1,0:T(8,128)(2,1)S(1)}, bf16[256,128]{1,0:T(8,128)(2,1)S(1)}, u32[]{:S(2)}, u32[]{:S(2)}) %collective-permute-start.13) | collective-permute-done | bytes 65568 | tf_op jit(solution)/shard_map/ppermute | solution.py:303
  42.4 0.8 %collective-permute-done.14.refs_2_ = bf16[256,128]{1,0:T(8,128)(2,1)S(1)} collective-permute-done((bf16[256,128]{1,0:T(8,128)(2,1)S(1)}, bf16[256,128]{1,0:T(8,128)(2,1)S(1)}, u32[]{:S(2)}, u32[]{:S(2)}) %collective-permute-start.14) | collective-permute-done | bytes 65568 | tf_op jit(solution)/shard_map/ppermute | solution.py:303
  43.3 2.2 %collective-permute-start.15 = (bf16[256,128]{1,0:T(8,128)(2,1)S(1)}, bf16[256,128]{1,0:T(8,128)(2,1)S(1)}, u32[]{:S(2)}, u32[]{:S(2)}) collective-permute-start(bf16[256,128]{1,0:T(8,128)(2,1)S(1)} %get-tuple-element.57), channel_id=1, source_target_pairs={{0,24},{4,28},{8,16},{12,20},{16,8},{20,12},{24,0},{28,4},{1,25},{... | collective-permute-start | bytes 196616 | tf_op jit(solution)/shard_map/ppermute | solution.py:303
  45.9 1.9 %collective-permute-start.17 = (bf16[256,128]{1,0:T(8,128)(2,1)S(1)}, bf16[256,128]{1,0:T(8,128)(2,1)S(1)}, u32[]{:S(2)}, u32[]{:S(2)}) collective-permute-start(bf16[256,128]{1,0:T(8,128)(2,1)S(1)} %get-tuple-element.59), channel_id=1, source_target_pairs={{0,16},{4,20},{8,24},{12,28},{16,0},{20,4},{24,8},{28,12},{1,17},{... | collective-permute-start | bytes 196616 | tf_op jit(solution)/shard_map/ppermute | solution.py:303
  47.8 1.9 %collective-permute-done.15.refs_0_ = bf16[256,128]{1,0:T(8,128)(2,1)S(1)} collective-permute-done((bf16[256,128]{1,0:T(8,128)(2,1)S(1)}, bf16[256,128]{1,0:T(8,128)(2,1)S(1)}, u32[]{:S(2)}, u32[]{:S(2)}) %collective-permute-start.15) | collective-permute-done | bytes 65568 | tf_op jit(solution)/shard_map/ppermute | solution.py:303
  49.7 0.9 %collective-permute-done.16.refs_1_ = bf16[256,128]{1,0:T(8,128)(2,1)S(1)} collective-permute-done((bf16[256,128]{1,0:T(8,128)(2,1)S(1)}, bf16[256,128]{1,0:T(8,128)(2,1)S(1)}, u32[]{:S(2)}, u32[]{:S(2)}) %collective-permute-start.16) | collective-permute-done | bytes 65568 | tf_op jit(solution)/shard_map/ppermute | solution.py:303
  50.7 0.6 %collective-permute-done.17.refs_2_ = bf16[256,128]{1,0:T(8,128)(2,1)S(1)} collective-permute-done((bf16[256,128]{1,0:T(8,128)(2,1)S(1)}, bf16[256,128]{1,0:T(8,128)(2,1)S(1)}, u32[]{:S(2)}, u32[]{:S(2)}) %collective-permute-start.17) | collective-permute-done | bytes 65568 | tf_op jit(solution)/shard_map/ppermute | solution.py:303
  51.4 0.9 %shard_map.81.result_ref = bf16[2,1024,128]{2,1,0:T(8,128)(2,1)} custom-call(f32[2,1024,128]{2,1,0:T(8,128)S(1)} %get-tuple-element.48.branch_ref, bf16[2,1024,128]{2,1,0:T(8,128)(2,1)S(1)} %bitcast.16, bf16[1024,128]{1,0:T(8,128)(2,1)S(1)} %bitcast.19, bf16[1024,128]{1,0:T(8,128)(2,1)S(1)} %collective-permute-done.11.came_ref), custom_call_target="tpu_custom_call" | custom-call | tf_op jit(solution)/shard_map/pallas_call | solution.py:396
  52.3 0.7 %collective-permute-done.18.mate_ref = bf16[1024,128]{1,0:T(8,128)(2,1)S(1)} collective-permute-done((bf16[1024,128]{1,0:T(8,128)(2,1)S(1)}, bf16[1024,128]{1,0:T(8,128)(2,1)S(1)}, u32[]{:S(2)}, u32[]{:S(2)}) %collective-permute-start.18) | collective-permute-done | bytes 262176 | tf_op jit(solution)/shard_map/ppermute | solution.py:298
  52.9 0.8 %shard_map.82 = bf16[2,1024,128]{2,1,0:T(8,128)(2,1)} custom-call(f32[2,1024,128]{2,1,0:T(8,128)S(1)} %get-tuple-element.48.branch_ref, bf16[2,1024,128]{2,1,0:T(8,128)(2,1)S(1)} %bitcast.17, bf16[1024,128]{1,0:T(8,128)(2,1)S(1)} %collective-permute-done.18.mate_ref, bf16[2,1024,128]{2,1,0:T(8,128)(2,1)} %shard_map.81.result_ref), custom_call_target="tpu_custom_call", output_to_operand_aliasing={{}: (3, {})} | custom-call | tf_op jit(solution)/shard_map/pallas_call | solution.py:396
  (27 shorter events, 3.2 us)
Async XLA Ops:
  2.9 10.6 %collective-permute-start = (bf16[2,512,128]{2,1,0:T(8,128)(2,1)S(1)}, bf16[2,512,128]{2,1,0:T(8,128)(2,1)S(1)}, u32[]{:S(2)}, u32[]{:S(2)}) collective-permute-start(bf16[2,512,128]{2,1,0:T(8,128)(2,1)S(1)} %get-tuple-element.35), channel_id=1, source_target_pairs={{0,1},{1,0},{2,3},{3,2},{4,5},{5,4},{6,7},{7,6},{8,9},{9,8},{10,11... | collective-permute-start | bytes 786440 | tf_op jit(solution)/shard_map/ppermute | solution.py:295
  5.9 4.4 %copy-start = (bf16[1,2048,128]{2,1,0:T(8,128)(2,1)S(1)}, bf16[1,2048,128]{2,1,0:T(8,128)(2,1)}, u32[]{:S(2)}) copy-start(bf16[1,2048,128]{2,1,0:T(8,128)(2,1)} %param.5) | copy-start | bytes 1572868
  5.9 9.2 %collective-permute-start.1 = (bf16[2,512,128]{2,1,0:T(8,128)(2,1)S(1)}, bf16[2,512,128]{2,1,0:T(8,128)(2,1)S(1)}, u32[]{:S(2)}, u32[]{:S(2)}) collective-permute-start(bf16[2,512,128]{2,1,0:T(8,128)(2,1)S(1)} %get-tuple-element.36), channel_id=1, source_target_pairs={{0,2},{1,3},{2,0},{3,1},{4,6},{5,7},{6,4},{7,5},{8,10},{9,11},{10,... | collective-permute-start | bytes 786440 | tf_op jit(solution)/shard_map/ppermute | solution.py:295
  9.6 9.2 %collective-permute-start.2 = (bf16[2,512,128]{2,1,0:T(8,128)(2,1)S(1)}, bf16[2,512,128]{2,1,0:T(8,128)(2,1)S(1)}, u32[]{:S(2)}, u32[]{:S(2)}) collective-permute-start(bf16[2,512,128]{2,1,0:T(8,128)(2,1)S(1)} %get-tuple-element.37), channel_id=1, source_target_pairs={{0,1},{1,0},{2,3},{3,2},{4,5},{5,4},{6,7},{7,6},{8,9},{9,8},{10,11... | collective-permute-start | bytes 786440 | tf_op jit(solution)/shard_map/ppermute | solution.py:295
  10.2 10.6 %collective-permute-start.3 = (bf16[2,512,128]{2,1,0:T(8,128)(2,1)S(1)}, bf16[2,512,128]{2,1,0:T(8,128)(2,1)S(1)}, u32[]{:S(2)}, u32[]{:S(2)}) collective-permute-start(bf16[2,512,128]{2,1,0:T(8,128)(2,1)S(1)} %get-tuple-element.38), channel_id=1, source_target_pairs={{0,2},{1,3},{2,0},{3,1},{4,6},{5,7},{6,4},{7,5},{8,10},{9,11},{10,... | collective-permute-start | bytes 786440 | tf_op jit(solution)/shard_map/ppermute | solution.py:295
  10.3 4.8 %copy-start.2 = (f32[1,2048]{1,0:T(1,128)S(1)}, f32[1,2048]{1,0:T(1,128)}, u32[]{:S(2)}) copy-start(f32[1,2048]{1,0:T(1,128)} %refs_7_.1) | copy-start | bytes 24580
  15.3 10.9 %collective-permute-start.4 = (bf16[2,512,128]{2,1,0:T(8,128)(2,1)S(1)}, bf16[2,512,128]{2,1,0:T(8,128)(2,1)S(1)}, u32[]{:S(2)}, u32[]{:S(2)}) collective-permute-start(bf16[2,512,128]{2,1,0:T(8,128)(2,1)S(1)} %get-tuple-element.39), channel_id=1, source_target_pairs={{0,2},{1,3},{2,0},{3,1},{4,6},{5,7},{6,4},{7,5},{8,10},{9,11},{10,... | collective-permute-start | bytes 786440 | tf_op jit(solution)/shard_map/ppermute | solution.py:295
  16.9 9.4 %collective-permute-start.5 = (bf16[2,512,128]{2,1,0:T(8,128)(2,1)S(1)}, bf16[2,512,128]{2,1,0:T(8,128)(2,1)S(1)}, u32[]{:S(2)}, u32[]{:S(2)}) collective-permute-start(bf16[2,512,128]{2,1,0:T(8,128)(2,1)S(1)} %get-tuple-element.40), channel_id=1, source_target_pairs={{0,1},{1,0},{2,3},{3,2},{4,5},{5,4},{6,7},{7,6},{8,9},{9,8},{10,11... | collective-permute-start | bytes 786440 | tf_op jit(solution)/shard_map/ppermute | solution.py:295
  20.8 9.2 %collective-permute-start.6 = (bf16[1,512,128]{2,1,0:T(8,128)(2,1)S(1)}, bf16[1,512,128]{2,1,0:T(8,128)(2,1)S(1)}, u32[]{:S(2)}, u32[]{:S(2)}) collective-permute-start(bf16[1,512,128]{2,1,0:T(8,128)(2,1)S(1)} %get-tuple-element.41), channel_id=1, source_target_pairs={{0,2},{1,3},{2,0},{3,1},{4,6},{5,7},{6,4},{7,5},{8,10},{9,11},{10,... | collective-permute-start | bytes 393224 | tf_op jit(solution)/shard_map/ppermute | solution.py:295
  22.4 7.6 %collective-permute-start.7 = (bf16[1,512,128]{2,1,0:T(8,128)(2,1)S(1)}, bf16[1,512,128]{2,1,0:T(8,128)(2,1)S(1)}, u32[]{:S(2)}, u32[]{:S(2)}) collective-permute-start(bf16[1,512,128]{2,1,0:T(8,128)(2,1)S(1)} %get-tuple-element.42), channel_id=1, source_target_pairs={{0,1},{1,0},{2,3},{3,2},{4,5},{5,4},{6,7},{7,6},{8,9},{9,8},{10,11... | collective-permute-start | bytes 393224 | tf_op jit(solution)/shard_map/ppermute | solution.py:295
  26.4 25.1 %copy-start.1 = (bf16[2048,128]{1,0:T(8,128)(2,1)S(1)}, bf16[2048,128]{1,0:T(8,128)(2,1)}, u32[]{:S(2)}) copy-start(bf16[2048,128]{1,0:T(8,128)(2,1)} %param.9) | copy-start | bytes 1572868
  26.4 4.6 %collective-permute-start.10 = (f32[16,128]{1,0:T(8,128)S(1)}, f32[16,128]{1,0:T(8,128)S(1)}, u32[]{:S(2)}, u32[]{:S(2)}) collective-permute-start(f32[16,128]{1,0:T(8,128)S(1)} %shard_map.75.refs_2_), channel_id=1, source_target_pairs={{0,3},{1,2},{2,1},{3,0},{4,7},{5,6},{6,5},{7,4},{8,11},{9,10},{10,... | collective-permute-start | bytes 24584 | tf_op jit(solution)/shard_map/ppermute | solution.py:295
  27.9 3.7 %collective-permute-start.8 = (f32[16,128]{1,0:T(8,128)S(1)}, f32[16,128]{1,0:T(8,128)S(1)}, u32[]{:S(2)}, u32[]{:S(2)}) collective-permute-start(f32[16,128]{1,0:T(8,128)S(1)} %shard_map.75.refs_2_), channel_id=1, source_target_pairs={{0,2},{1,3},{2,0},{3,1},{4,6},{5,7},{6,4},{7,5},{8,10},{9,11},{10,... | collective-permute-start | bytes 24584 | tf_op jit(solution)/shard_map/ppermute | solution.py:295
  28.2 3.7 %collective-permute-start.9 = (f32[16,128]{1,0:T(8,128)S(1)}, f32[16,128]{1,0:T(8,128)S(1)}, u32[]{:S(2)}, u32[]{:S(2)}) collective-permute-start(f32[16,128]{1,0:T(8,128)S(1)} %shard_map.75.refs_2_), channel_id=1, source_target_pairs={{0,1},{1,0},{2,3},{3,2},{4,5},{5,4},{6,7},{7,6},{8,9},{9,8},{10,11... | collective-permute-start | bytes 24584 | tf_op jit(solution)/shard_map/ppermute | solution.py:295
  32.0 1.6 %collective-permute-start.11 = (bf16[1024,128]{1,0:T(8,128)(2,1)S(1)}, bf16[1024,128]{1,0:T(8,128)(2,1)S(1)}, u32[]{:S(2)}, u32[]{:S(2)}) collective-permute-start(bf16[1024,128]{1,0:T(8,128)(2,1)S(1)} %get-tuple-element.49), channel_id=1, source_target_pairs={{0,4},{4,0},{8,12},{12,8},{16,20},{20,16},{24,28},{28,24},{1,5},{5... | collective-permute-start | bytes 786440 | tf_op jit(solution)/shard_map/ppermute | solution.py:298
  33.7 6.9 %collective-permute-start.12 = (bf16[256,128]{1,0:T(8,128)(2,1)S(1)}, bf16[256,128]{1,0:T(8,128)(2,1)S(1)}, u32[]{:S(2)}, u32[]{:S(2)}) collective-permute-start(bf16[256,128]{1,0:T(8,128)(2,1)S(1)} %get-tuple-element.50), channel_id=1, source_target_pairs={{0,24},{4,28},{8,16},{12,20},{16,8},{20,12},{24,0},{28,4},{1,25},{... | collective-permute-start | bytes 196616 | tf_op jit(solution)/shard_map/ppermute | solution.py:303
  37.4 5.1 %collective-permute-start.13 = (bf16[256,128]{1,0:T(8,128)(2,1)S(1)}, bf16[256,128]{1,0:T(8,128)(2,1)S(1)}, u32[]{:S(2)}, u32[]{:S(2)}) collective-permute-start(bf16[256,128]{1,0:T(8,128)(2,1)S(1)} %get-tuple-element.51), channel_id=1, source_target_pairs={{0,8},{4,12},{8,0},{12,4},{16,24},{20,28},{24,16},{28,20},{1,9},{5... | collective-permute-start | bytes 196616 | tf_op jit(solution)/shard_map/ppermute | solution.py:303
  37.4 5.9 %collective-permute-start.14 = (bf16[256,128]{1,0:T(8,128)(2,1)S(1)}, bf16[256,128]{1,0:T(8,128)(2,1)S(1)}, u32[]{:S(2)}, u32[]{:S(2)}) collective-permute-start(bf16[256,128]{1,0:T(8,128)(2,1)S(1)} %get-tuple-element.52), channel_id=1, source_target_pairs={{0,16},{4,20},{8,24},{12,28},{16,0},{20,4},{24,8},{28,12},{1,17},{... | collective-permute-start | bytes 196616 | tf_op jit(solution)/shard_map/ppermute | solution.py:303
  43.3 6.4 %collective-permute-start.15 = (bf16[256,128]{1,0:T(8,128)(2,1)S(1)}, bf16[256,128]{1,0:T(8,128)(2,1)S(1)}, u32[]{:S(2)}, u32[]{:S(2)}) collective-permute-start(bf16[256,128]{1,0:T(8,128)(2,1)S(1)} %get-tuple-element.57), channel_id=1, source_target_pairs={{0,24},{4,28},{8,16},{12,20},{16,8},{20,12},{24,0},{28,4},{1,25},{... | collective-permute-start | bytes 196616 | tf_op jit(solution)/shard_map/ppermute | solution.py:303
  45.6 5.1 %collective-permute-start.16 = (bf16[256,128]{1,0:T(8,128)(2,1)S(1)}, bf16[256,128]{1,0:T(8,128)(2,1)S(1)}, u32[]{:S(2)}, u32[]{:S(2)}) collective-permute-start(bf16[256,128]{1,0:T(8,128)(2,1)S(1)} %get-tuple-element.58), channel_id=1, source_target_pairs={{0,8},{4,12},{8,0},{12,4},{16,24},{20,28},{24,16},{28,20},{1,9},{5... | collective-permute-start | bytes 196616 | tf_op jit(solution)/shard_map/ppermute | solution.py:303
  45.9 5.3 %collective-permute-start.17 = (bf16[256,128]{1,0:T(8,128)(2,1)S(1)}, bf16[256,128]{1,0:T(8,128)(2,1)S(1)}, u32[]{:S(2)}, u32[]{:S(2)}) collective-permute-start(bf16[256,128]{1,0:T(8,128)(2,1)S(1)} %get-tuple-element.59), channel_id=1, source_target_pairs={{0,16},{4,20},{8,24},{12,28},{16,0},{20,4},{24,8},{28,12},{1,17},{... | collective-permute-start | bytes 196616 | tf_op jit(solution)/shard_map/ppermute | solution.py:303
  51.3 1.6 %collective-permute-start.18 = (bf16[1024,128]{1,0:T(8,128)(2,1)S(1)}, bf16[1024,128]{1,0:T(8,128)(2,1)S(1)}, u32[]{:S(2)}, u32[]{:S(2)}) collective-permute-start(bf16[1024,128]{1,0:T(8,128)(2,1)S(1)} %bitcast.20), channel_id=1, source_target_pairs={{0,4},{4,0},{8,12},{12,8},{16,20},{20,16},{24,28},{28,24},{1,5},{5... | collective-permute-start | bytes 786440 | tf_op jit(solution)/shard_map/ppermute | solution.py:298

commit v8 on v7

--- a/solution.py
+++ b/solution.py
@@ -244,14 +244,15 @@
         out[...] = held[chip_of(k)].astype(out.dtype)
 
 
-def mate_kernel(branch_ref, *refs):
+def mate_kernel(branch_ref, top_ref, came_ref, *refs):
     later, (later_out, mate_out) = refs[:-2], refs[-2:]
     core = lax.axis_index("section") & 1
     scale = core.astype(F32)
     for k, part in zip(order_of(len(later)), later):
         q = chip_of(k)
         later_out[q] = part[...]
-        mate_out[q] = (part[...].astype(F32) + branch_ref[core, q] * scale).astype(mate_out.dtype)
+        rest = top_ref[core, q].astype(F32) + came_ref[q].astype(F32) + branch_ref[core, q] * scale
+        mate_out[q] = (part[...].astype(F32) + rest).astype(mate_out.dtype)
 
 
 def first_end_kernel(branch_ref, top_ref, later_ref, came_ref, out_ref):
@@ -261,11 +262,12 @@
     out_ref[0] = total.astype(out_ref.dtype)
 
 
-def second_end_kernel(branch_ref, top_ref, mate_ref, result_ref, out_ref):
+def second_end_kernel(mate_ref, result_ref, out_ref, done):
     del result_ref
     other = 1 - (lax.axis_index("section") & 1)
-    total = branch_ref[other] + top_ref[other].astype(F32) + mate_ref[...].astype(F32)
-    out_ref[0] = total.astype(out_ref.dtype)
+    copy = pltpu.make_async_copy(mate_ref, out_ref.at[other], done)
+    copy.start()
+    copy.wait()
 
 
 def call(kernel, out_shape, *arrays, cost=None):
@@ -388,23 +390,34 @@
         compiler_params=LIMIT,
     )(*(near(terms[k]) for k in order_of(chips)), done)
     later = [across(v, k) for k, v in enumerate(later)]
-    later, mate = call(mate_kernel, [whole] * 2, halves, *(later[k] for k in order_of(chips)))
+    top = top_grads.reshape(2, part, tokens)
+    later, mate = call(
+        mate_kernel,
+        [whole] * 2,
+        halves,
+        top.reshape(2, *shape),
+        pair.reshape(shape),
+        *(later[k] for k in order_of(chips)),
+    )
     later, mate = later.reshape(part, tokens), swap(mate.reshape(part, tokens))
-    top = near(top_grads.reshape(2, part, tokens))
-
-    def end(kernel, half, arrays, into):
-        return pl.pallas_call(
-            kernel,
-            out_shape=jax.ShapeDtypeStruct((2, part, tokens), BF16),
-            grid=(1,),
-            in_specs=[WHOLE] * len(arrays) + [pl.BlockSpec(memory_space=pl.ANY)] * len(into),
-            out_specs=pl.BlockSpec((1, part, tokens), lambda i: (half(lax.axis_index("section") & 1), 0, 0)),
-            input_output_aliases={len(arrays): 0} if into else {},
-            compiler_params=LIMIT,
-        )(*(near(a) for a in arrays), *into)
-
-    result = end(first_end_kernel, lambda core: core, (branch, top, later, pair), ())
-    result = end(second_end_kernel, lambda core: 1 - core, (branch, top, mate), (result,))
+    arrays = (branch, top, later, pair)
+    result = pl.pallas_call(
+        first_end_kernel,
+        out_shape=jax.ShapeDtypeStruct((2, part, tokens), BF16),
+        grid=(1,),
+        in_specs=[WHOLE] * len(arrays),
+        out_specs=pl.BlockSpec((1, part, tokens), lambda i: (lax.axis_index("section") & 1, 0, 0)),
+        compiler_params=LIMIT,
+    )(*(near(a) for a in arrays))
+    result = pl.pallas_call(
+        second_end_kernel,
+        out_shape=jax.ShapeDtypeStruct((2, part, tokens), BF16),
+        in_specs=[WHOLE, pl.BlockSpec(memory_space=pl.ANY)],
+        out_specs=pl.BlockSpec(memory_space=pl.ANY),
+        scratch_shapes=[pltpu.SemaphoreType.DMA],
+        input_output_aliases={1: 0},
+        compiler_params=LIMIT,
+    )(near(mate), result)
     return (result.reshape(1, rows, tokens), gain_grad)
 
 

time: 53.9 us -> 53.9 us (level)
  no operation moved by 1% of the time
where the time goes in v8:
time: 53.9 us; the launch traced here: 53.8 us
  starting transfers between devices  22 us (41%)
  waiting for transfers between devices  19.3 us (36%)
  Pallas kernels  11.7 us (22%)
  between operations  0.75 us (1%)
    ppermute x11, starting transfers between devices, exchange(): return lax.ppermute(value, 'tensor', [(i, i ^ mask) for i in range(count)])  13 us
    ppermute x11, waiting for transfers between devices, exchange(): return lax.ppermute(value, 'tensor', [(i, i ^ mask) for i in range(count)])  9.47 us
    ppermute x6, starting transfers between devices, across(): lax.ppermute(value, 'section', [(s, s ^ 2 * distance) for s in range(laye...  8.91 us
    ppermute x6, waiting for transfers between devices, across(): lax.ppermute(value, 'section', [(s, s ^ 2 * distance) for s in range(laye...  7.6 us
    pallas_call x3, Pallas kernels, product(): pl.pallas_call(keep_kernel if extra else multiply, out_shape=out_shape, g...  7.56 us
    pallas_call x9, Pallas kernels, call(): pl.pallas_call(kernel, out_shape=out_shape, in_specs=[WHOLE] * len(arrays...  2.48 us
    ppermute x2, waiting for transfers between devices, swap(): return lax.ppermute(value, 'section', [(s, s ^ 1) for s in range(layers)])  2.19 us
  transfers between devices with their start and end apart: 19, of which 15 were waited for; matrix products, arithmetic and copies ran while one was open for 0% of the time, Pallas kernels for 15%

profile of v8, /device:TPU:0, one launch (start us, length us, event | category | flops | bytes accessed | tf_op | source)
XLA Modules:
  0.0 53.8 jit_solution(9150528878999939416)
XLA Ops:
  0.6 2.2 %shard_map.69 = (bf16[2,512,128]{2,1,0:T(8,128)(2,1)S(1)}, bf16[2,512,128]{2,1,0:T(8,128)(2,1)S(1)}) custom-call(bf16[8192,512]{1,0:T(8,128)(2,1)} %bitcast.23, bf16[8192,512]{1,0:T(8,128)(2,1)} %bitcast.24, bf16[128,512]{1,0:T(8,128)(2,1)} %bitcast.30), custom_call_target="tpu_custom_call" | custom-call | flops 268435456 | bytes 2621440 | tf_op jit(solution)/shard_map/pallas_call | solution.py:86
  2.9 3.0 %collective-permute-start = (bf16[2,512,128]{2,1,0:T(8,128)(2,1)S(1)}, bf16[2,512,128]{2,1,0:T(8,128)(2,1)S(1)}, u32[]{:S(2)}, u32[]{:S(2)}) collective-permute-start(bf16[2,512,128]{2,1,0:T(8,128)(2,1)S(1)} %get-tuple-element.35), channel_id=1, source_target_pairs={{0,1},{1,0},{2,3},{3,2},{4,5},{5,4},{6,7},{7,6},{8,9},{9,8},{10,11... | collective-permute-start | bytes 786440 | tf_op jit(solution)/shard_map/ppermute | solution.py:297
  5.9 1.5 %collective-permute-start.1 = (bf16[2,512,128]{2,1,0:T(8,128)(2,1)S(1)}, bf16[2,512,128]{2,1,0:T(8,128)(2,1)S(1)}, u32[]{:S(2)}, u32[]{:S(2)}) collective-permute-start(bf16[2,512,128]{2,1,0:T(8,128)(2,1)S(1)} %get-tuple-element.36), channel_id=1, source_target_pairs={{0,2},{1,3},{2,0},{3,1},{4,6},{5,7},{6,4},{7,5},{8,10},{9,11},{10,... | collective-permute-start | bytes 786440 | tf_op jit(solution)/shard_map/ppermute | solution.py:297
  7.4 2.2 %shard_map.70 = (bf16[2,512,128]{2,1,0:T(8,128)(2,1)S(1)}, bf16[2,512,128]{2,1,0:T(8,128)(2,1)S(1)}) custom-call(bf16[8192,512]{1,0:T(8,128)(2,1)} %bitcast.25, bf16[8192,512]{1,0:T(8,128)(2,1)} %bitcast.26, bf16[128,512]{1,0:T(8,128)(2,1)} %bitcast.31), custom_call_target="tpu_custom_call" | custom-call | flops 268435456 | bytes 2621440 | tf_op jit(solution)/shard_map/pallas_call | solution.py:86
  9.6 0.6 %collective-permute-start.2 = (bf16[2,512,128]{2,1,0:T(8,128)(2,1)S(1)}, bf16[2,512,128]{2,1,0:T(8,128)(2,1)S(1)}, u32[]{:S(2)}, u32[]{:S(2)}) collective-permute-start(bf16[2,512,128]{2,1,0:T(8,128)(2,1)S(1)} %get-tuple-element.37), channel_id=1, source_target_pairs={{0,1},{1,0},{2,3},{3,2},{4,5},{5,4},{6,7},{7,6},{8,9},{9,8},{10,11... | collective-permute-start | bytes 786440 | tf_op jit(solution)/shard_map/ppermute | solution.py:297
  10.3 3.2 %shard_map.68 = (bf16[2,1024,128]{2,1,0:T(8,128)(2,1)S(1)}, bf16[2,1024,128]{2,1,0:T(8,128)(2,1)S(1)}, f32[8,128]{1,0:T(8,128)S(1)}) custom-call(bf16[8192,512]{1,0:T(8,128)(2,1)} %bitcast.27, bf16[8192,512]{1,0:T(8,128)(2,1)} %bitcast.28, bf16[128,512]{1,0:T(8,128)(2,1)} %bitcast.32, bf16[2048,128]{1,0:T(8,128)(2,1)S(1)} %bitcast.12), custom_call_target="tpu_custom_call" | custom-call | flops 536870912 | bytes 5242880 | tf_op jit(solution)/shard_map/pallas_call | solution.py:86
  13.5 1.7 %collective-permute-done.1.refs_5_.refs_3_ = bf16[2,512,128]{2,1,0:T(8,128)(2,1)S(1)} collective-permute-done((bf16[2,512,128]{2,1,0:T(8,128)(2,1)S(1)}, bf16[2,512,128]{2,1,0:T(8,128)(2,1)S(1)}, u32[]{:S(2)}, u32[]{:S(2)}) %collective-permute-start.1) | collective-permute-done | bytes 262176 | tf_op jit(solution)/shard_map/ppermute | solution.py:297
  15.3 1.6 %collective-permute-start.4 = (bf16[2,512,128]{2,1,0:T(8,128)(2,1)S(1)}, bf16[2,512,128]{2,1,0:T(8,128)(2,1)S(1)}, u32[]{:S(2)}, u32[]{:S(2)}) collective-permute-start(bf16[2,512,128]{2,1,0:T(8,128)(2,1)S(1)} %get-tuple-element.39), channel_id=1, source_target_pairs={{0,2},{1,3},{2,0},{3,1},{4,6},{5,7},{6,4},{7,5},{8,10},{9,11},{10,... | collective-permute-start | bytes 786440 | tf_op jit(solution)/shard_map/ppermute | solution.py:297
  16.9 0.5 collective-permute-start.5
  17.4 1.3 %collective-permute-done.2.refs_2_.refs_4_ = bf16[2,512,128]{2,1,0:T(8,128)(2,1)S(1)} collective-permute-done((bf16[2,512,128]{2,1,0:T(8,128)(2,1)S(1)}, bf16[2,512,128]{2,1,0:T(8,128)(2,1)S(1)}, u32[]{:S(2)}, u32[]{:S(2)}) %collective-permute-start.2) | collective-permute-done | bytes 262176 | tf_op jit(solution)/shard_map/ppermute | solution.py:297
  18.8 1.9 %collective-permute-done.3.refs_3_.refs_5_ = bf16[2,512,128]{2,1,0:T(8,128)(2,1)S(1)} collective-permute-done((bf16[2,512,128]{2,1,0:T(8,128)(2,1)S(1)}, bf16[2,512,128]{2,1,0:T(8,128)(2,1)S(1)}, u32[]{:S(2)}, u32[]{:S(2)}) %collective-permute-start.3) | collective-permute-done | bytes 262176 | tf_op jit(solution)/shard_map/ppermute | solution.py:297
  20.8 1.6 %collective-permute-start.6 = (bf16[1,512,128]{2,1,0:T(8,128)(2,1)S(1)}, bf16[1,512,128]{2,1,0:T(8,128)(2,1)S(1)}, u32[]{:S(2)}, u32[]{:S(2)}) collective-permute-start(bf16[1,512,128]{2,1,0:T(8,128)(2,1)S(1)} %get-tuple-element.41), channel_id=1, source_target_pairs={{0,2},{1,3},{2,0},{3,1},{4,6},{5,7},{6,4},{7,5},{8,10},{9,11},{10,... | collective-permute-start | bytes 393224 | tf_op jit(solution)/shard_map/ppermute | solution.py:297
  23.3 3.0 %collective-permute-done.4.refs_6_.refs_4_ = bf16[2,512,128]{2,1,0:T(8,128)(2,1)S(1)} collective-permute-done((bf16[2,512,128]{2,1,0:T(8,128)(2,1)S(1)}, bf16[2,512,128]{2,1,0:T(8,128)(2,1)S(1)}, u32[]{:S(2)}, u32[]{:S(2)}) %collective-permute-start.4) | collective-permute-done | bytes 262176 | tf_op jit(solution)/shard_map/ppermute | solution.py:297
  26.4 1.6 %collective-permute-start.10 = (f32[16,128]{1,0:T(8,128)S(1)}, f32[16,128]{1,0:T(8,128)S(1)}, u32[]{:S(2)}, u32[]{:S(2)}) collective-permute-start(f32[16,128]{1,0:T(8,128)S(1)} %shard_map.75.refs_2_), channel_id=1, source_target_pairs={{0,3},{1,2},{2,1},{3,0},{4,7},{5,6},{6,5},{7,4},{8,11},{9,10},{10,... | collective-permute-start | bytes 24584 | tf_op jit(solution)/shard_map/ppermute | solution.py:297
  28.2 1.8 %collective-permute-start.9 = (f32[16,128]{1,0:T(8,128)S(1)}, f32[16,128]{1,0:T(8,128)S(1)}, u32[]{:S(2)}, u32[]{:S(2)}) collective-permute-start(f32[16,128]{1,0:T(8,128)S(1)} %shard_map.75.refs_2_), channel_id=1, source_target_pairs={{0,1},{1,0},{2,3},{3,2},{4,5},{5,4},{6,7},{7,6},{8,9},{9,8},{10,11... | collective-permute-start | bytes 24584 | tf_op jit(solution)/shard_map/ppermute | solution.py:297
  30.3 0.7 %collective-permute-done.10.refs_5_ = f32[16,128]{1,0:T(8,128)S(1)} collective-permute-done((f32[16,128]{1,0:T(8,128)S(1)}, f32[16,128]{1,0:T(8,128)S(1)}, u32[]{:S(2)}, u32[]{:S(2)}) %collective-permute-start.10) | collective-permute-done | bytes 8224 | tf_op jit(solution)/shard_map/ppermute | solution.py:297
  31.0 0.6 %collective-permute-done.8.refs_3_ = f32[16,128]{1,0:T(8,128)S(1)} collective-permute-done((f32[16,128]{1,0:T(8,128)S(1)}, f32[16,128]{1,0:T(8,128)S(1)}, u32[]{:S(2)}, u32[]{:S(2)}) %collective-permute-start.8) | collective-permute-done | bytes 8224 | tf_op jit(solution)/shard_map/ppermute | solution.py:297
  32.1 1.5 %collective-permute-done.11.came_ref = bf16[1024,128]{1,0:T(8,128)(2,1)S(1)} collective-permute-done((bf16[1024,128]{1,0:T(8,128)(2,1)S(1)}, bf16[1024,128]{1,0:T(8,128)(2,1)S(1)}, u32[]{:S(2)}, u32[]{:S(2)}) %collective-permute-start.11) | collective-permute-done | bytes 262176 | tf_op jit(solution)/shard_map/ppermute | solution.py:300
  33.7 3.7 %collective-permute-start.12 = (bf16[256,128]{1,0:T(8,128)(2,1)S(1)}, bf16[256,128]{1,0:T(8,128)(2,1)S(1)}, u32[]{:S(2)}, u32[]{:S(2)}) collective-permute-start(bf16[256,128]{1,0:T(8,128)(2,1)S(1)} %get-tuple-element.50), channel_id=1, source_target_pairs={{0,24},{4,28},{8,16},{12,20},{16,8},{20,12},{24,0},{28,4},{1,25},{... | collective-permute-start | bytes 196616 | tf_op jit(solution)/shard_map/ppermute | solution.py:305
  37.4 0.8 %collective-permute-start.14 = (bf16[256,128]{1,0:T(8,128)(2,1)S(1)}, bf16[256,128]{1,0:T(8,128)(2,1)S(1)}, u32[]{:S(2)}, u32[]{:S(2)}) collective-permute-start(bf16[256,128]{1,0:T(8,128)(2,1)S(1)} %get-tuple-element.52), channel_id=1, source_target_pairs={{0,16},{4,20},{8,24},{12,28},{16,0},{20,4},{24,8},{28,12},{1,17},{... | collective-permute-start | bytes 196616 | tf_op jit(solution)/shard_map/ppermute | solution.py:305
  38.2 0.9 %shard_map.78 = (f32[1,2048]{1,0:T(1,128)}, f32[8,128]{1,0:T(8,128)S(1)}) custom-call(f32[2,1024,128]{2,1,0:T(8,128)S(1)} %get-tuple-element.54.partial_ref, bf16[2048,128]{1,0:T(8,128)(2,1)S(1)} %bitcast.16, f32[8,128]{1,0:T(8,128)S(1)} %get-tuple-element.55.upside_ref), custom_call_target="tpu_custom_call" | custom-call | tf_op jit(solution)/shard_map/pallas_call | solution.py:274
  39.1 1.5 %collective-permute-done.12.refs_0_ = bf16[256,128]{1,0:T(8,128)(2,1)S(1)} collective-permute-done((bf16[256,128]{1,0:T(8,128)(2,1)S(1)}, bf16[256,128]{1,0:T(8,128)(2,1)S(1)}, u32[]{:S(2)}, u32[]{:S(2)}) %collective-permute-start.12) | collective-permute-done | bytes 65568 | tf_op jit(solution)/shard_map/ppermute | solution.py:305
  40.6 1.9 %collective-permute-done.13.refs_1_ = bf16[256,128]{1,0:T(8,128)(2,1)S(1)} collective-permute-done((bf16[256,128]{1,0:T(8,128)(2,1)S(1)}, bf16[256,128]{1,0:T(8,128)(2,1)S(1)}, u32[]{:S(2)}, u32[]{:S(2)}) %collective-permute-start.13) | collective-permute-done | bytes 65568 | tf_op jit(solution)/shard_map/ppermute | solution.py:305
  42.4 0.8 %collective-permute-done.14.refs_2_ = bf16[256,128]{1,0:T(8,128)(2,1)S(1)} collective-permute-done((bf16[256,128]{1,0:T(8,128)(2,1)S(1)}, bf16[256,128]{1,0:T(8,128)(2,1)S(1)}, u32[]{:S(2)}, u32[]{:S(2)}) %collective-permute-start.14) | collective-permute-done | bytes 65568 | tf_op jit(solution)/shard_map/ppermute | solution.py:305
  43.3 2.2 %collective-permute-start.15 = (bf16[256,128]{1,0:T(8,128)(2,1)S(1)}, bf16[256,128]{1,0:T(8,128)(2,1)S(1)}, u32[]{:S(2)}, u32[]{:S(2)}) collective-permute-start(bf16[256,128]{1,0:T(8,128)(2,1)S(1)} %get-tuple-element.57), channel_id=1, source_target_pairs={{0,24},{4,28},{8,16},{12,20},{16,8},{20,12},{24,0},{28,4},{1,25},{... | collective-permute-start | bytes 196616 | tf_op jit(solution)/shard_map/ppermute | solution.py:305
  46.0 1.9 %collective-permute-start.17 = (bf16[256,128]{1,0:T(8,128)(2,1)S(1)}, bf16[256,128]{1,0:T(8,128)(2,1)S(1)}, u32[]{:S(2)}, u32[]{:S(2)}) collective-permute-start(bf16[256,128]{1,0:T(8,128)(2,1)S(1)} %get-tuple-element.59), channel_id=1, source_target_pairs={{0,16},{4,20},{8,24},{12,28},{16,0},{20,4},{24,8},{28,12},{1,17},{... | collective-permute-start | bytes 196616 | tf_op jit(solution)/shard_map/ppermute | solution.py:305
  47.8 1.9 %collective-permute-done.15.refs_0_ = bf16[256,128]{1,0:T(8,128)(2,1)S(1)} collective-permute-done((bf16[256,128]{1,0:T(8,128)(2,1)S(1)}, bf16[256,128]{1,0:T(8,128)(2,1)S(1)}, u32[]{:S(2)}, u32[]{:S(2)}) %collective-permute-start.15) | collective-permute-done | bytes 65568 | tf_op jit(solution)/shard_map/ppermute | solution.py:305
  49.7 0.9 %collective-permute-done.16.refs_1_ = bf16[256,128]{1,0:T(8,128)(2,1)S(1)} collective-permute-done((bf16[256,128]{1,0:T(8,128)(2,1)S(1)}, bf16[256,128]{1,0:T(8,128)(2,1)S(1)}, u32[]{:S(2)}, u32[]{:S(2)}) %collective-permute-start.16) | collective-permute-done | bytes 65568 | tf_op jit(solution)/shard_map/ppermute | solution.py:305
  50.7 0.6 %collective-permute-done.17.refs_2_ = bf16[256,128]{1,0:T(8,128)(2,1)S(1)} collective-permute-done((bf16[256,128]{1,0:T(8,128)(2,1)S(1)}, bf16[256,128]{1,0:T(8,128)(2,1)S(1)}, u32[]{:S(2)}, u32[]{:S(2)}) %collective-permute-start.17) | collective-permute-done | bytes 65568 | tf_op jit(solution)/shard_map/ppermute | solution.py:305
  51.5 0.9 %shard_map.81.result_ref = bf16[2,1024,128]{2,1,0:T(8,128)(2,1)} custom-call(f32[2,1024,128]{2,1,0:T(8,128)S(1)} %get-tuple-element.48.branch_ref, bf16[2,1024,128]{2,1,0:T(8,128)(2,1)S(1)} %bitcast.20, bf16[1024,128]{1,0:T(8,128)(2,1)S(1)} %bitcast.21, bf16[1024,128]{1,0:T(8,128)(2,1)S(1)} %collective-permute-done.11.came_ref), custom_call_target="tpu_custom_call" | custom-call | tf_op jit(solution)/shard_map/pallas_call | solution.py:404
  52.4 0.7 %collective-permute-done.18.mate_ref = bf16[1024,128]{1,0:T(8,128)(2,1)S(1)} collective-permute-done((bf16[1024,128]{1,0:T(8,128)(2,1)S(1)}, bf16[1024,128]{1,0:T(8,128)(2,1)S(1)}, u32[]{:S(2)}, u32[]{:S(2)}) %collective-permute-start.18) | collective-permute-done | bytes 262176 | tf_op jit(solution)/shard_map/ppermute | solution.py:300
  53.1 0.7 %shard_map.82 = bf16[2,1024,128]{2,1,0:T(8,128)(2,1)} custom-call(bf16[1024,128]{1,0:T(8,128)(2,1)S(1)} %collective-permute-done.18.mate_ref, bf16[2,1024,128]{2,1,0:T(8,128)(2,1)} %shard_map.81.result_ref), custom_call_target="tpu_custom_call", output_to_operand_aliasing={{}: (1, {})} | custom-call | tf_op jit(solution)/shard_map/pallas_call | solution.py:412
  (27 shorter events, 3.3 us)
Async XLA Ops:
  2.9 10.6 %collective-permute-start = (bf16[2,512,128]{2,1,0:T(8,128)(2,1)S(1)}, bf16[2,512,128]{2,1,0:T(8,128)(2,1)S(1)}, u32[]{:S(2)}, u32[]{:S(2)}) collective-permute-start(bf16[2,512,128]{2,1,0:T(8,128)(2,1)S(1)} %get-tuple-element.35), channel_id=1, source_target_pairs={{0,1},{1,0},{2,3},{3,2},{4,5},{5,4},{6,7},{7,6},{8,9},{9,8},{10,11... | collective-permute-start | bytes 786440 | tf_op jit(solution)/shard_map/ppermute | solution.py:297
  5.9 4.4 %copy-start = (bf16[1,2048,128]{2,1,0:T(8,128)(2,1)S(1)}, bf16[1,2048,128]{2,1,0:T(8,128)(2,1)}, u32[]{:S(2)}) copy-start(bf16[1,2048,128]{2,1,0:T(8,128)(2,1)} %param.5) | copy-start | bytes 1572868
  5.9 9.2 %collective-permute-start.1 = (bf16[2,512,128]{2,1,0:T(8,128)(2,1)S(1)}, bf16[2,512,128]{2,1,0:T(8,128)(2,1)S(1)}, u32[]{:S(2)}, u32[]{:S(2)}) collective-permute-start(bf16[2,512,128]{2,1,0:T(8,128)(2,1)S(1)} %get-tuple-element.36), channel_id=1, source_target_pairs={{0,2},{1,3},{2,0},{3,1},{4,6},{5,7},{6,4},{7,5},{8,10},{9,11},{10,... | collective-permute-start | bytes 786440 | tf_op jit(solution)/shard_map/ppermute | solution.py:297
  9.6 9.2 %collective-permute-start.2 = (bf16[2,512,128]{2,1,0:T(8,128)(2,1)S(1)}, bf16[2,512,128]{2,1,0:T(8,128)(2,1)S(1)}, u32[]{:S(2)}, u32[]{:S(2)}) collective-permute-start(bf16[2,512,128]{2,1,0:T(8,128)(2,1)S(1)} %get-tuple-element.37), channel_id=1, source_target_pairs={{0,1},{1,0},{2,3},{3,2},{4,5},{5,4},{6,7},{7,6},{8,9},{9,8},{10,11... | collective-permute-start | bytes 786440 | tf_op jit(solution)/shard_map/ppermute | solution.py:297
  10.2 10.6 %collective-permute-start.3 = (bf16[2,512,128]{2,1,0:T(8,128)(2,1)S(1)}, bf16[2,512,128]{2,1,0:T(8,128)(2,1)S(1)}, u32[]{:S(2)}, u32[]{:S(2)}) collective-permute-start(bf16[2,512,128]{2,1,0:T(8,128)(2,1)S(1)} %get-tuple-element.38), channel_id=1, source_target_pairs={{0,2},{1,3},{2,0},{3,1},{4,6},{5,7},{6,4},{7,5},{8,10},{9,11},{10,... | collective-permute-start | bytes 786440 | tf_op jit(solution)/shard_map/ppermute | solution.py:297
  10.3 4.8 %copy-start.2 = (f32[1,2048]{1,0:T(1,128)S(1)}, f32[1,2048]{1,0:T(1,128)}, u32[]{:S(2)}) copy-start(f32[1,2048]{1,0:T(1,128)} %refs_7_.1) | copy-start | bytes 24580
  15.3 10.9 %collective-permute-start.4 = (bf16[2,512,128]{2,1,0:T(8,128)(2,1)S(1)}, bf16[2,512,128]{2,1,0:T(8,128)(2,1)S(1)}, u32[]{:S(2)}, u32[]{:S(2)}) collective-permute-start(bf16[2,512,128]{2,1,0:T(8,128)(2,1)S(1)} %get-tuple-element.39), channel_id=1, source_target_pairs={{0,2},{1,3},{2,0},{3,1},{4,6},{5,7},{6,4},{7,5},{8,10},{9,11},{10,... | collective-permute-start | bytes 786440 | tf_op jit(solution)/shard_map/ppermute | solution.py:297
  16.9 9.4 %collective-permute-start.5 = (bf16[2,512,128]{2,1,0:T(8,128)(2,1)S(1)}, bf16[2,512,128]{2,1,0:T(8,128)(2,1)S(1)}, u32[]{:S(2)}, u32[]{:S(2)}) collective-permute-start(bf16[2,512,128]{2,1,0:T(8,128)(2,1)S(1)} %get-tuple-element.40), channel_id=1, source_target_pairs={{0,1},{1,0},{2,3},{3,2},{4,5},{5,4},{6,7},{7,6},{8,9},{9,8},{10,11... | collective-permute-start | bytes 786440 | tf_op jit(solution)/shard_map/ppermute | solution.py:297
  20.8 9.2 %collective-permute-start.6 = (bf16[1,512,128]{2,1,0:T(8,128)(2,1)S(1)}, bf16[1,512,128]{2,1,0:T(8,128)(2,1)S(1)}, u32[]{:S(2)}, u32[]{:S(2)}) collective-permute-start(bf16[1,512,128]{2,1,0:T(8,128)(2,1)S(1)} %get-tuple-element.41), channel_id=1, source_target_pairs={{0,2},{1,3},{2,0},{3,1},{4,6},{5,7},{6,4},{7,5},{8,10},{9,11},{10,... | collective-permute-start | bytes 393224 | tf_op jit(solution)/shard_map/ppermute | solution.py:297
  22.4 7.6 %collective-permute-start.7 = (bf16[1,512,128]{2,1,0:T(8,128)(2,1)S(1)}, bf16[1,512,128]{2,1,0:T(8,128)(2,1)S(1)}, u32[]{:S(2)}, u32[]{:S(2)}) collective-permute-start(bf16[1,512,128]{2,1,0:T(8,128)(2,1)S(1)} %get-tuple-element.42), channel_id=1, source_target_pairs={{0,1},{1,0},{2,3},{3,2},{4,5},{5,4},{6,7},{7,6},{8,9},{9,8},{10,11... | collective-permute-start | bytes 393224 | tf_op jit(solution)/shard_map/ppermute | solution.py:297
  26.4 24.9 %copy-start.1 = (bf16[2048,128]{1,0:T(8,128)(2,1)S(1)}, bf16[2048,128]{1,0:T(8,128)(2,1)}, u32[]{:S(2)}) copy-start(bf16[2048,128]{1,0:T(8,128)(2,1)} %param.9) | copy-start | bytes 1572868
  26.4 4.6 %collective-permute-start.10 = (f32[16,128]{1,0:T(8,128)S(1)}, f32[16,128]{1,0:T(8,128)S(1)}, u32[]{:S(2)}, u32[]{:S(2)}) collective-permute-start(f32[16,128]{1,0:T(8,128)S(1)} %shard_map.75.refs_2_), channel_id=1, source_target_pairs={{0,3},{1,2},{2,1},{3,0},{4,7},{5,6},{6,5},{7,4},{8,11},{9,10},{10,... | collective-permute-start | bytes 24584 | tf_op jit(solution)/shard_map/ppermute | solution.py:297
  27.9 3.7 %collective-permute-start.8 = (f32[16,128]{1,0:T(8,128)S(1)}, f32[16,128]{1,0:T(8,128)S(1)}, u32[]{:S(2)}, u32[]{:S(2)}) collective-permute-start(f32[16,128]{1,0:T(8,128)S(1)} %shard_map.75.refs_2_), channel_id=1, source_target_pairs={{0,2},{1,3},{2,0},{3,1},{4,6},{5,7},{6,4},{7,5},{8,10},{9,11},{10,... | collective-permute-start | bytes 24584 | tf_op jit(solution)/shard_map/ppermute | solution.py:297
  28.2 3.7 %collective-permute-start.9 = (f32[16,128]{1,0:T(8,128)S(1)}, f32[16,128]{1,0:T(8,128)S(1)}, u32[]{:S(2)}, u32[]{:S(2)}) collective-permute-start(f32[16,128]{1,0:T(8,128)S(1)} %shard_map.75.refs_2_), channel_id=1, source_target_pairs={{0,1},{1,0},{2,3},{3,2},{4,5},{5,4},{6,7},{7,6},{8,9},{9,8},{10,11... | collective-permute-start | bytes 24584 | tf_op jit(solution)/shard_map/ppermute | solution.py:297
  32.0 1.6 %collective-permute-start.11 = (bf16[1024,128]{1,0:T(8,128)(2,1)S(1)}, bf16[1024,128]{1,0:T(8,128)(2,1)S(1)}, u32[]{:S(2)}, u32[]{:S(2)}) collective-permute-start(bf16[1024,128]{1,0:T(8,128)(2,1)S(1)} %get-tuple-element.49), channel_id=1, source_target_pairs={{0,4},{4,0},{8,12},{12,8},{16,20},{20,16},{24,28},{28,24},{1,5},{5... | collective-permute-start | bytes 786440 | tf_op jit(solution)/shard_map/ppermute | solution.py:300
  33.7 6.9 %collective-permute-start.12 = (bf16[256,128]{1,0:T(8,128)(2,1)S(1)}, bf16[256,128]{1,0:T(8,128)(2,1)S(1)}, u32[]{:S(2)}, u32[]{:S(2)}) collective-permute-start(bf16[256,128]{1,0:T(8,128)(2,1)S(1)} %get-tuple-element.50), channel_id=1, source_target_pairs={{0,24},{4,28},{8,16},{12,20},{16,8},{20,12},{24,0},{28,4},{1,25},{... | collective-permute-start | bytes 196616 | tf_op jit(solution)/shard_map/ppermute | solution.py:305
  37.4 5.1 %collective-permute-start.13 = (bf16[256,128]{1,0:T(8,128)(2,1)S(1)}, bf16[256,128]{1,0:T(8,128)(2,1)S(1)}, u32[]{:S(2)}, u32[]{:S(2)}) collective-permute-start(bf16[256,128]{1,0:T(8,128)(2,1)S(1)} %get-tuple-element.51), channel_id=1, source_target_pairs={{0,8},{4,12},{8,0},{12,4},{16,24},{20,28},{24,16},{28,20},{1,9},{5... | collective-permute-start | bytes 196616 | tf_op jit(solution)/shard_map/ppermute | solution.py:305
  37.4 5.9 %collective-permute-start.14 = (bf16[256,128]{1,0:T(8,128)(2,1)S(1)}, bf16[256,128]{1,0:T(8,128)(2,1)S(1)}, u32[]{:S(2)}, u32[]{:S(2)}) collective-permute-start(bf16[256,128]{1,0:T(8,128)(2,1)S(1)} %get-tuple-element.52), channel_id=1, source_target_pairs={{0,16},{4,20},{8,24},{12,28},{16,0},{20,4},{24,8},{28,12},{1,17},{... | collective-permute-start | bytes 196616 | tf_op jit(solution)/shard_map/ppermute | solution.py:305
  43.3 6.4 %collective-permute-start.15 = (bf16[256,128]{1,0:T(8,128)(2,1)S(1)}, bf16[256,128]{1,0:T(8,128)(2,1)S(1)}, u32[]{:S(2)}, u32[]{:S(2)}) collective-permute-start(bf16[256,128]{1,0:T(8,128)(2,1)S(1)} %get-tuple-element.57), channel_id=1, source_target_pairs={{0,24},{4,28},{8,16},{12,20},{16,8},{20,12},{24,0},{28,4},{1,25},{... | collective-permute-start | bytes 196616 | tf_op jit(solution)/shard_map/ppermute | solution.py:305
  45.6 5.1 %collective-permute-start.16 = (bf16[256,128]{1,0:T(8,128)(2,1)S(1)}, bf16[256,128]{1,0:T(8,128)(2,1)S(1)}, u32[]{:S(2)}, u32[]{:S(2)}) collective-permute-start(bf16[256,128]{1,0:T(8,128)(2,1)S(1)} %get-tuple-element.58), channel_id=1, source_target_pairs={{0,8},{4,12},{8,0},{12,4},{16,24},{20,28},{24,16},{28,20},{1,9},{5... | collective-permute-start | bytes 196616 | tf_op jit(solution)/shard_map/ppermute | solution.py:305
  46.0 5.3 %collective-permute-start.17 = (bf16[256,128]{1,0:T(8,128)(2,1)S(1)}, bf16[256,128]{1,0:T(8,128)(2,1)S(1)}, u32[]{:S(2)}, u32[]{:S(2)}) collective-permute-start(bf16[256,128]{1,0:T(8,128)(2,1)S(1)} %get-tuple-element.59), channel_id=1, source_target_pairs={{0,16},{4,20},{8,24},{12,28},{16,0},{20,4},{24,8},{28,12},{1,17},{... | collective-permute-start | bytes 196616 | tf_op jit(solution)/shard_map/ppermute | solution.py:305
  51.5 1.6 %collective-permute-start.18 = (bf16[1024,128]{1,0:T(8,128)(2,1)S(1)}, bf16[1024,128]{1,0:T(8,128)(2,1)S(1)}, u32[]{:S(2)}, u32[]{:S(2)}) collective-permute-start(bf16[1024,128]{1,0:T(8,128)(2,1)S(1)} %bitcast.22), channel_id=1, source_target_pairs={{0,4},{4,0},{8,12},{12,8},{16,20},{20,16},{24,28},{28,24},{1,5},{5... | collective-permute-start | bytes 786440 | tf_op jit(solution)/shard_map/ppermute | solution.py:300

commit v9 on v8

--- a/solution.py
+++ b/solution.py
@@ -245,29 +245,27 @@
 
 
 def mate_kernel(branch_ref, top_ref, came_ref, *refs):
-    later, (later_out, mate_out) = refs[:-2], refs[-2:]
+    later, (mine_out, mate_out) = refs[:-2], refs[-2:]
     core = lax.axis_index("section") & 1
     scale = core.astype(F32)
     for k, part in zip(order_of(len(later)), later):
         q = chip_of(k)
-        later_out[q] = part[...]
-        rest = top_ref[core, q].astype(F32) + came_ref[q].astype(F32) + branch_ref[core, q] * scale
-        mate_out[q] = (part[...].astype(F32) + rest).astype(mate_out.dtype)
-
-
-def first_end_kernel(branch_ref, top_ref, later_ref, came_ref, out_ref):
+        base = top_ref[core, q].astype(F32) + part[...].astype(F32)
+        came, own = came_ref[q].astype(F32), branch_ref[core, q]
+        mine_out[q] = (base + own + came * (1 - scale)).astype(mine_out.dtype)
+        mate_out[q] = (base + came + own * scale).astype(mate_out.dtype)
+
+
+def end_kernel(mine_ref, mate_ref, out_ref, done):
     core = lax.axis_index("section") & 1
-    pair = came_ref[...].astype(F32) * (1 - core).astype(F32)
-    total = branch_ref[core] + top_ref[core].astype(F32) + later_ref[...].astype(F32) + pair
-    out_ref[0] = total.astype(out_ref.dtype)
-
-
-def second_end_kernel(mate_ref, result_ref, out_ref, done):
-    del result_ref
-    other = 1 - (lax.axis_index("section") & 1)
-    copy = pltpu.make_async_copy(mate_ref, out_ref.at[other], done)
-    copy.start()
-    copy.wait()
+    copies = [
+        pltpu.make_async_copy(mine_ref, out_ref.at[core], done.at[0]),
+        pltpu.make_async_copy(mate_ref, out_ref.at[1 - core], done.at[1]),
+    ]
+    for copy in copies:
+        copy.start()
+    for copy in copies:
+        copy.wait()
 
 
 def call(kernel, out_shape, *arrays, cost=None):
@@ -391,7 +389,7 @@
     )(*(near(terms[k]) for k in order_of(chips)), done)
     later = [across(v, k) for k, v in enumerate(later)]
     top = top_grads.reshape(2, part, tokens)
-    later, mate = call(
+    mine, mate = call(
         mate_kernel,
         [whole] * 2,
         halves,
@@ -399,25 +397,15 @@
         pair.reshape(shape),
         *(later[k] for k in order_of(chips)),
     )
-    later, mate = later.reshape(part, tokens), swap(mate.reshape(part, tokens))
-    arrays = (branch, top, later, pair)
+    mine, mate = mine.reshape(part, tokens), swap(mate.reshape(part, tokens))
     result = pl.pallas_call(
-        first_end_kernel,
+        end_kernel,
         out_shape=jax.ShapeDtypeStruct((2, part, tokens), BF16),
-        grid=(1,),
-        in_specs=[WHOLE] * len(arrays),
-        out_specs=pl.BlockSpec((1, part, tokens), lambda i: (lax.axis_index("section") & 1, 0, 0)),
+        in_specs=[WHOLE] * 2,
+        out_specs=pl.BlockSpec(memory_space=pl.ANY),
+        scratch_shapes=[pltpu.SemaphoreType.DMA((2,))],
         compiler_params=LIMIT,
-    )(*(near(a) for a in arrays))
-    result = pl.pallas_call(
-        second_end_kernel,
-        out_shape=jax.ShapeDtypeStruct((2, part, tokens), BF16),
-        in_specs=[WHOLE, pl.BlockSpec(memory_space=pl.ANY)],
-        out_specs=pl.BlockSpec(memory_space=pl.ANY),
-        scratch_shapes=[pltpu.SemaphoreType.DMA],
-        input_output_aliases={1: 0},
-        compiler_params=LIMIT,
-    )(near(mate), result)
+    )(near(mine), near(mate))
     return (result.reshape(1, rows, tokens), gain_grad)
 
 

time: 53.9 us -> 54.2 us (level)
  waiting for transfers between devices: 19.3 us -> 20.1 us
  Pallas kernels: 11.7 us -> 11.1 us
    ppermute x2, waiting for transfers between devices: 2.19 us -> 3.04 us  [swap(): return lax.ppermute(value, 'section', [(s, s ^ 1) for s in range(layers)])]
    pallas_call x2 -> x1, Pallas kernels: 1.57 us -> 0.8 us  [local(): pl.pallas_call(end_kernel, out_shape=jax.ShapeDtypeStruct((2, part, token...]
  transfers between devices with their start and end apart: 19 -> 19, of which waited for: 15 -> 15; matrix products, arithmetic and copies ran while one was open for 0% -> 0% of each run, Pallas kernels for 15% -> 14%
where the time goes in v9:
time: 54.2 us; the launch traced here: 54 us
  starting transfers between devices  22 us (41%)
  waiting for transfers between devices  20.1 us (37%)
  Pallas kernels  11.1 us (20%)
  between operations  0.75 us (1%)
    ppermute x11, starting transfers between devices, exchange(): return lax.ppermute(value, 'tensor', [(i, i ^ mask) for i in range(count)])  13 us
    ppermute x11, waiting for transfers between devices, exchange(): return lax.ppermute(value, 'tensor', [(i, i ^ mask) for i in range(count)])  9.44 us
    ppermute x6, starting transfers between devices, across(): lax.ppermute(value, 'section', [(s, s ^ 2 * distance) for s in range(laye...  8.91 us
    ppermute x6, waiting for transfers between devices, across(): lax.ppermute(value, 'section', [(s, s ^ 2 * distance) for s in range(laye...  7.6 us
    pallas_call x3, Pallas kernels, product(): pl.pallas_call(keep_kernel if extra else multiply, out_shape=out_shape, g...  7.56 us
    ppermute x2, waiting for transfers between devices, swap(): return lax.ppermute(value, 'section', [(s, s ^ 1) for s in range(layers)])  3.04 us
    pallas_call x9, Pallas kernels, call(): pl.pallas_call(kernel, out_shape=out_shape, in_specs=[WHOLE] * len(arrays...  2.62 us
  transfers between devices with their start and end apart: 19, of which 15 were waited for; matrix products, arithmetic and copies ran while one was open for 0% of the time, Pallas kernels for 14%

profile of v9, /device:TPU:0, one launch (start us, length us, event | category | flops | bytes accessed | tf_op | source)
XLA Modules:
  0.0 54.0 jit_solution(1973256078770736952)
XLA Ops:
  0.6 2.2 %shard_map.69 = (bf16[2,512,128]{2,1,0:T(8,128)(2,1)S(1)}, bf16[2,512,128]{2,1,0:T(8,128)(2,1)S(1)}) custom-call(bf16[8192,512]{1,0:T(8,128)(2,1)} %bitcast.21, bf16[8192,512]{1,0:T(8,128)(2,1)} %bitcast.22, bf16[128,512]{1,0:T(8,128)(2,1)} %bitcast.27), custom_call_target="tpu_custom_call" | custom-call | flops 268435456 | bytes 2621440 | tf_op jit(solution)/shard_map/pallas_call | solution.py:86
  2.9 3.0 %collective-permute-start = (bf16[2,512,128]{2,1,0:T(8,128)(2,1)S(1)}, bf16[2,512,128]{2,1,0:T(8,128)(2,1)S(1)}, u32[]{:S(2)}, u32[]{:S(2)}) collective-permute-start(bf16[2,512,128]{2,1,0:T(8,128)(2,1)S(1)} %get-tuple-element.35), channel_id=1, source_target_pairs={{0,1},{1,0},{2,3},{3,2},{4,5},{5,4},{6,7},{7,6},{8,9},{9,8},{10,11... | collective-permute-start | bytes 786440 | tf_op jit(solution)/shard_map/ppermute | solution.py:295
  5.9 1.5 %collective-permute-start.1 = (bf16[2,512,128]{2,1,0:T(8,128)(2,1)S(1)}, bf16[2,512,128]{2,1,0:T(8,128)(2,1)S(1)}, u32[]{:S(2)}, u32[]{:S(2)}) collective-permute-start(bf16[2,512,128]{2,1,0:T(8,128)(2,1)S(1)} %get-tuple-element.36), channel_id=1, source_target_pairs={{0,2},{1,3},{2,0},{3,1},{4,6},{5,7},{6,4},{7,5},{8,10},{9,11},{10,... | collective-permute-start | bytes 786440 | tf_op jit(solution)/shard_map/ppermute | solution.py:295
  7.4 2.2 %shard_map.70 = (bf16[2,512,128]{2,1,0:T(8,128)(2,1)S(1)}, bf16[2,512,128]{2,1,0:T(8,128)(2,1)S(1)}) custom-call(bf16[8192,512]{1,0:T(8,128)(2,1)} %bitcast.23, bf16[8192,512]{1,0:T(8,128)(2,1)} %bitcast.24, bf16[128,512]{1,0:T(8,128)(2,1)} %bitcast.28), custom_call_target="tpu_custom_call" | custom-call | flops 268435456 | bytes 2621440 | tf_op jit(solution)/shard_map/pallas_call | solution.py:86
  9.6 0.6 %collective-permute-start.2 = (bf16[2,512,128]{2,1,0:T(8,128)(2,1)S(1)}, bf16[2,512,128]{2,1,0:T(8,128)(2,1)S(1)}, u32[]{:S(2)}, u32[]{:S(2)}) collective-permute-start(bf16[2,512,128]{2,1,0:T(8,128)(2,1)S(1)} %get-tuple-element.37), channel_id=1, source_target_pairs={{0,1},{1,0},{2,3},{3,2},{4,5},{5,4},{6,7},{7,6},{8,9},{9,8},{10,11... | collective-permute-start | bytes 786440 | tf_op jit(solution)/shard_map/ppermute | solution.py:295
  10.3 3.2 %shard_map.68 = (bf16[2,1024,128]{2,1,0:T(8,128)(2,1)S(1)}, bf16[2,1024,128]{2,1,0:T(8,128)(2,1)S(1)}, f32[8,128]{1,0:T(8,128)S(1)}) custom-call(bf16[8192,512]{1,0:T(8,128)(2,1)} %bitcast.25, bf16[8192,512]{1,0:T(8,128)(2,1)} %bitcast.26, bf16[128,512]{1,0:T(8,128)(2,1)} %bitcast.29, bf16[2048,128]{1,0:T(8,128)(2,1)S(1)} %bitcast.9), custom_call_target="tpu_custom_call" | custom-call | flops 536870912 | bytes 5242880 | tf_op jit(solution)/shard_map/pallas_call | solution.py:86
  13.5 1.7 %collective-permute-done.1.refs_5_.refs_3_ = bf16[2,512,128]{2,1,0:T(8,128)(2,1)S(1)} collective-permute-done((bf16[2,512,128]{2,1,0:T(8,128)(2,1)S(1)}, bf16[2,512,128]{2,1,0:T(8,128)(2,1)S(1)}, u32[]{:S(2)}, u32[]{:S(2)}) %collective-permute-start.1) | collective-permute-done | bytes 262176 | tf_op jit(solution)/shard_map/ppermute | solution.py:295
  15.3 1.6 %collective-permute-start.4 = (bf16[2,512,128]{2,1,0:T(8,128)(2,1)S(1)}, bf16[2,512,128]{2,1,0:T(8,128)(2,1)S(1)}, u32[]{:S(2)}, u32[]{:S(2)}) collective-permute-start(bf16[2,512,128]{2,1,0:T(8,128)(2,1)S(1)} %get-tuple-element.39), channel_id=1, source_target_pairs={{0,2},{1,3},{2,0},{3,1},{4,6},{5,7},{6,4},{7,5},{8,10},{9,11},{10,... | collective-permute-start | bytes 786440 | tf_op jit(solution)/shard_map/ppermute | solution.py:295
  16.9 0.5 collective-permute-start.5
  17.4 1.3 %collective-permute-done.2.refs_2_.refs_4_ = bf16[2,512,128]{2,1,0:T(8,128)(2,1)S(1)} collective-permute-done((bf16[2,512,128]{2,1,0:T(8,128)(2,1)S(1)}, bf16[2,512,128]{2,1,0:T(8,128)(2,1)S(1)}, u32[]{:S(2)}, u32[]{:S(2)}) %collective-permute-start.2) | collective-permute-done | bytes 262176 | tf_op jit(solution)/shard_map/ppermute | solution.py:295
  18.8 1.9 %collective-permute-done.3.refs_3_.refs_5_ = bf16[2,512,128]{2,1,0:T(8,128)(2,1)S(1)} collective-permute-done((bf16[2,512,128]{2,1,0:T(8,128)(2,1)S(1)}, bf16[2,512,128]{2,1,0:T(8,128)(2,1)S(1)}, u32[]{:S(2)}, u32[]{:S(2)}) %collective-permute-start.3) | collective-permute-done | bytes 262176 | tf_op jit(solution)/shard_map/ppermute | solution.py:295
  20.8 1.6 %collective-permute-start.6 = (bf16[1,512,128]{2,1,0:T(8,128)(2,1)S(1)}, bf16[1,512,128]{2,1,0:T(8,128)(2,1)S(1)}, u32[]{:S(2)}, u32[]{:S(2)}) collective-permute-start(bf16[1,512,128]{2,1,0:T(8,128)(2,1)S(1)} %get-tuple-element.41), channel_id=1, source_target_pairs={{0,2},{1,3},{2,0},{3,1},{4,6},{5,7},{6,4},{7,5},{8,10},{9,11},{10,... | collective-permute-start | bytes 393224 | tf_op jit(solution)/shard_map/ppermute | solution.py:295
  22.4 0.5 collective-permute-start.7
  23.3 3.0 %collective-permute-done.4.refs_6_.refs_4_ = bf16[2,512,128]{2,1,0:T(8,128)(2,1)S(1)} collective-permute-done((bf16[2,512,128]{2,1,0:T(8,128)(2,1)S(1)}, bf16[2,512,128]{2,1,0:T(8,128)(2,1)S(1)}, u32[]{:S(2)}, u32[]{:S(2)}) %collective-permute-start.4) | collective-permute-done | bytes 262176 | tf_op jit(solution)/shard_map/ppermute | solution.py:295
  26.4 1.6 %collective-permute-start.10 = (f32[16,128]{1,0:T(8,128)S(1)}, f32[16,128]{1,0:T(8,128)S(1)}, u32[]{:S(2)}, u32[]{:S(2)}) collective-permute-start(f32[16,128]{1,0:T(8,128)S(1)} %shard_map.75.refs_2_), channel_id=1, source_target_pairs={{0,3},{1,2},{2,1},{3,0},{4,7},{5,6},{6,5},{7,4},{8,11},{9,10},{10,... | collective-permute-start | bytes 24584 | tf_op jit(solution)/shard_map/ppermute | solution.py:295
  28.2 1.8 %collective-permute-start.9 = (f32[16,128]{1,0:T(8,128)S(1)}, f32[16,128]{1,0:T(8,128)S(1)}, u32[]{:S(2)}, u32[]{:S(2)}) collective-permute-start(f32[16,128]{1,0:T(8,128)S(1)} %shard_map.75.refs_2_), channel_id=1, source_target_pairs={{0,1},{1,0},{2,3},{3,2},{4,5},{5,4},{6,7},{7,6},{8,9},{9,8},{10,11... | collective-permute-start | bytes 24584 | tf_op jit(solution)/shard_map/ppermute | solution.py:295
  30.3 0.7 %collective-permute-done.10.refs_5_ = f32[16,128]{1,0:T(8,128)S(1)} collective-permute-done((f32[16,128]{1,0:T(8,128)S(1)}, f32[16,128]{1,0:T(8,128)S(1)}, u32[]{:S(2)}, u32[]{:S(2)}) %collective-permute-start.10) | collective-permute-done | bytes 8224 | tf_op jit(solution)/shard_map/ppermute | solution.py:295
  31.0 0.6 %collective-permute-done.8.refs_3_ = f32[16,128]{1,0:T(8,128)S(1)} collective-permute-done((f32[16,128]{1,0:T(8,128)S(1)}, f32[16,128]{1,0:T(8,128)S(1)}, u32[]{:S(2)}, u32[]{:S(2)}) %collective-permute-start.8) | collective-permute-done | bytes 8224 | tf_op jit(solution)/shard_map/ppermute | solution.py:295
  32.1 1.5 %collective-permute-done.11 = bf16[1024,128]{1,0:T(8,128)(2,1)S(1)} collective-permute-done((bf16[1024,128]{1,0:T(8,128)(2,1)S(1)}, bf16[1024,128]{1,0:T(8,128)(2,1)S(1)}, u32[]{:S(2)}, u32[]{:S(2)}) %collective-permute-start.11) | collective-permute-done | bytes 262176 | tf_op jit(solution)/shard_map/ppermute | solution.py:298
  33.7 3.7 %collective-permute-start.12 = (bf16[256,128]{1,0:T(8,128)(2,1)S(1)}, bf16[256,128]{1,0:T(8,128)(2,1)S(1)}, u32[]{:S(2)}, u32[]{:S(2)}) collective-permute-start(bf16[256,128]{1,0:T(8,128)(2,1)S(1)} %get-tuple-element.50), channel_id=1, source_target_pairs={{0,24},{4,28},{8,16},{12,20},{16,8},{20,12},{24,0},{28,4},{1,25},{... | collective-permute-start | bytes 196616 | tf_op jit(solution)/shard_map/ppermute | solution.py:303
  37.4 0.8 %collective-permute-start.14 = (bf16[256,128]{1,0:T(8,128)(2,1)S(1)}, bf16[256,128]{1,0:T(8,128)(2,1)S(1)}, u32[]{:S(2)}, u32[]{:S(2)}) collective-permute-start(bf16[256,128]{1,0:T(8,128)(2,1)S(1)} %get-tuple-element.52), channel_id=1, source_target_pairs={{0,16},{4,20},{8,24},{12,28},{16,0},{20,4},{24,8},{28,12},{1,17},{... | collective-permute-start | bytes 196616 | tf_op jit(solution)/shard_map/ppermute | solution.py:303
  38.2 0.9 %shard_map.78 = (f32[1,2048]{1,0:T(1,128)}, f32[8,128]{1,0:T(8,128)S(1)}) custom-call(f32[2,1024,128]{2,1,0:T(8,128)S(1)} %get-tuple-element.54.partial_ref, bf16[2048,128]{1,0:T(8,128)(2,1)S(1)} %bitcast.13, f32[8,128]{1,0:T(8,128)S(1)} %get-tuple-element.55.upside_ref), custom_call_target="tpu_custom_call" | custom-call | tf_op jit(solution)/shard_map/pallas_call | solution.py:272
  39.1 1.5 %collective-permute-done.12.refs_0_ = bf16[256,128]{1,0:T(8,128)(2,1)S(1)} collective-permute-done((bf16[256,128]{1,0:T(8,128)(2,1)S(1)}, bf16[256,128]{1,0:T(8,128)(2,1)S(1)}, u32[]{:S(2)}, u32[]{:S(2)}) %collective-permute-start.12) | collective-permute-done | bytes 65568 | tf_op jit(solution)/shard_map/ppermute | solution.py:303
  40.6 1.9 %collective-permute-done.13.refs_1_ = bf16[256,128]{1,0:T(8,128)(2,1)S(1)} collective-permute-done((bf16[256,128]{1,0:T(8,128)(2,1)S(1)}, bf16[256,128]{1,0:T(8,128)(2,1)S(1)}, u32[]{:S(2)}, u32[]{:S(2)}) %collective-permute-start.13) | collective-permute-done | bytes 65568 | tf_op jit(solution)/shard_map/ppermute | solution.py:303
  42.5 0.8 %collective-permute-done.14.refs_2_ = bf16[256,128]{1,0:T(8,128)(2,1)S(1)} collective-permute-done((bf16[256,128]{1,0:T(8,128)(2,1)S(1)}, bf16[256,128]{1,0:T(8,128)(2,1)S(1)}, u32[]{:S(2)}, u32[]{:S(2)}) %collective-permute-start.14) | collective-permute-done | bytes 65568 | tf_op jit(solution)/shard_map/ppermute | solution.py:303
  43.4 2.2 %collective-permute-start.15 = (bf16[256,128]{1,0:T(8,128)(2,1)S(1)}, bf16[256,128]{1,0:T(8,128)(2,1)S(1)}, u32[]{:S(2)}, u32[]{:S(2)}) collective-permute-start(bf16[256,128]{1,0:T(8,128)(2,1)S(1)} %get-tuple-element.57), channel_id=1, source_target_pairs={{0,24},{4,28},{8,16},{12,20},{16,8},{20,12},{24,0},{28,4},{1,25},{... | collective-permute-start | bytes 196616 | tf_op jit(solution)/shard_map/ppermute | solution.py:303
  46.0 1.9 %collective-permute-start.17 = (bf16[256,128]{1,0:T(8,128)(2,1)S(1)}, bf16[256,128]{1,0:T(8,128)(2,1)S(1)}, u32[]{:S(2)}, u32[]{:S(2)}) collective-permute-start(bf16[256,128]{1,0:T(8,128)(2,1)S(1)} %get-tuple-element.59), channel_id=1, source_target_pairs={{0,16},{4,20},{8,24},{12,28},{16,0},{20,4},{24,8},{28,12},{1,17},{... | collective-permute-start | bytes 196616 | tf_op jit(solution)/shard_map/ppermute | solution.py:303
  47.8 1.9 %collective-permute-done.15.refs_0_ = bf16[256,128]{1,0:T(8,128)(2,1)S(1)} collective-permute-done((bf16[256,128]{1,0:T(8,128)(2,1)S(1)}, bf16[256,128]{1,0:T(8,128)(2,1)S(1)}, u32[]{:S(2)}, u32[]{:S(2)}) %collective-permute-start.15) | collective-permute-done | bytes 65568 | tf_op jit(solution)/shard_map/ppermute | solution.py:303
  49.8 0.9 %collective-permute-done.16.refs_1_ = bf16[256,128]{1,0:T(8,128)(2,1)S(1)} collective-permute-done((bf16[256,128]{1,0:T(8,128)(2,1)S(1)}, bf16[256,128]{1,0:T(8,128)(2,1)S(1)}, u32[]{:S(2)}, u32[]{:S(2)}) %collective-permute-start.16) | collective-permute-done | bytes 65568 | tf_op jit(solution)/shard_map/ppermute | solution.py:303
  50.7 0.6 %collective-permute-done.17.refs_2_ = bf16[256,128]{1,0:T(8,128)(2,1)S(1)} collective-permute-done((bf16[256,128]{1,0:T(8,128)(2,1)S(1)}, bf16[256,128]{1,0:T(8,128)(2,1)S(1)}, u32[]{:S(2)}, u32[]{:S(2)}) %collective-permute-start.17) | collective-permute-done | bytes 65568 | tf_op jit(solution)/shard_map/ppermute | solution.py:303
  51.7 1.5 %collective-permute-done.18.mate_ref = bf16[1024,128]{1,0:T(8,128)(2,1)S(1)} collective-permute-done((bf16[1024,128]{1,0:T(8,128)(2,1)S(1)}, bf16[1024,128]{1,0:T(8,128)(2,1)S(1)}, u32[]{:S(2)}, u32[]{:S(2)}) %collective-permute-start.18) | collective-permute-done | bytes 262176 | tf_op jit(solution)/shard_map/ppermute | solution.py:298
  53.2 0.8 %shard_map.81 = bf16[2,1024,128]{2,1,0:T(8,128)(2,1)} custom-call(bf16[1024,128]{1,0:T(8,128)(2,1)S(1)} %bitcast.19, bf16[1024,128]{1,0:T(8,128)(2,1)S(1)} %collective-permute-done.18.mate_ref), custom_call_target="tpu_custom_call" | custom-call | tf_op jit(solution)/shard_map/pallas_call | solution.py:401
  (26 shorter events, 2.9 us)
Async XLA Ops:
  2.9 10.6 %collective-permute-start = (bf16[2,512,128]{2,1,0:T(8,128)(2,1)S(1)}, bf16[2,512,128]{2,1,0:T(8,128)(2,1)S(1)}, u32[]{:S(2)}, u32[]{:S(2)}) collective-permute-start(bf16[2,512,128]{2,1,0:T(8,128)(2,1)S(1)} %get-tuple-element.35), channel_id=1, source_target_pairs={{0,1},{1,0},{2,3},{3,2},{4,5},{5,4},{6,7},{7,6},{8,9},{9,8},{10,11... | collective-permute-start | bytes 786440 | tf_op jit(solution)/shard_map/ppermute | solution.py:295
  5.9 4.4 %copy-start = (bf16[1,2048,128]{2,1,0:T(8,128)(2,1)S(1)}, bf16[1,2048,128]{2,1,0:T(8,128)(2,1)}, u32[]{:S(2)}) copy-start(bf16[1,2048,128]{2,1,0:T(8,128)(2,1)} %param.5) | copy-start | bytes 1572868
  5.9 9.2 %collective-permute-start.1 = (bf16[2,512,128]{2,1,0:T(8,128)(2,1)S(1)}, bf16[2,512,128]{2,1,0:T(8,128)(2,1)S(1)}, u32[]{:S(2)}, u32[]{:S(2)}) collective-permute-start(bf16[2,512,128]{2,1,0:T(8,128)(2,1)S(1)} %get-tuple-element.36), channel_id=1, source_target_pairs={{0,2},{1,3},{2,0},{3,1},{4,6},{5,7},{6,4},{7,5},{8,10},{9,11},{10,... | collective-permute-start | bytes 786440 | tf_op jit(solution)/shard_map/ppermute | solution.py:295
  9.6 9.2 %collective-permute-start.2 = (bf16[2,512,128]{2,1,0:T(8,128)(2,1)S(1)}, bf16[2,512,128]{2,1,0:T(8,128)(2,1)S(1)}, u32[]{:S(2)}, u32[]{:S(2)}) collective-permute-start(bf16[2,512,128]{2,1,0:T(8,128)(2,1)S(1)} %get-tuple-element.37), channel_id=1, source_target_pairs={{0,1},{1,0},{2,3},{3,2},{4,5},{5,4},{6,7},{7,6},{8,9},{9,8},{10,11... | collective-permute-start | bytes 786440 | tf_op jit(solution)/shard_map/ppermute | solution.py:295
  10.2 10.6 %collective-permute-start.3 = (bf16[2,512,128]{2,1,0:T(8,128)(2,1)S(1)}, bf16[2,512,128]{2,1,0:T(8,128)(2,1)S(1)}, u32[]{:S(2)}, u32[]{:S(2)}) collective-permute-start(bf16[2,512,128]{2,1,0:T(8,128)(2,1)S(1)} %get-tuple-element.38), channel_id=1, source_target_pairs={{0,2},{1,3},{2,0},{3,1},{4,6},{5,7},{6,4},{7,5},{8,10},{9,11},{10,... | collective-permute-start | bytes 786440 | tf_op jit(solution)/shard_map/ppermute | solution.py:295
  10.3 4.8 %copy-start.2 = (f32[1,2048]{1,0:T(1,128)S(1)}, f32[1,2048]{1,0:T(1,128)}, u32[]{:S(2)}) copy-start(f32[1,2048]{1,0:T(1,128)} %refs_7_.1) | copy-start | bytes 24580
  15.3 10.9 %collective-permute-start.4 = (bf16[2,512,128]{2,1,0:T(8,128)(2,1)S(1)}, bf16[2,512,128]{2,1,0:T(8,128)(2,1)S(1)}, u32[]{:S(2)}, u32[]{:S(2)}) collective-permute-start(bf16[2,512,128]{2,1,0:T(8,128)(2,1)S(1)} %get-tuple-element.39), channel_id=1, source_target_pairs={{0,2},{1,3},{2,0},{3,1},{4,6},{5,7},{6,4},{7,5},{8,10},{9,11},{10,... | collective-permute-start | bytes 786440 | tf_op jit(solution)/shard_map/ppermute | solution.py:295
  16.9 9.4 %collective-permute-start.5 = (bf16[2,512,128]{2,1,0:T(8,128)(2,1)S(1)}, bf16[2,512,128]{2,1,0:T(8,128)(2,1)S(1)}, u32[]{:S(2)}, u32[]{:S(2)}) collective-permute-start(bf16[2,512,128]{2,1,0:T(8,128)(2,1)S(1)} %get-tuple-element.40), channel_id=1, source_target_pairs={{0,1},{1,0},{2,3},{3,2},{4,5},{5,4},{6,7},{7,6},{8,9},{9,8},{10,11... | collective-permute-start | bytes 786440 | tf_op jit(solution)/shard_map/ppermute | solution.py:295
  20.8 9.2 %collective-permute-start.6 = (bf16[1,512,128]{2,1,0:T(8,128)(2,1)S(1)}, bf16[1,512,128]{2,1,0:T(8,128)(2,1)S(1)}, u32[]{:S(2)}, u32[]{:S(2)}) collective-permute-start(bf16[1,512,128]{2,1,0:T(8,128)(2,1)S(1)} %get-tuple-element.41), channel_id=1, source_target_pairs={{0,2},{1,3},{2,0},{3,1},{4,6},{5,7},{6,4},{7,5},{8,10},{9,11},{10,... | collective-permute-start | bytes 393224 | tf_op jit(solution)/shard_map/ppermute | solution.py:295
  22.4 7.6 %collective-permute-start.7 = (bf16[1,512,128]{2,1,0:T(8,128)(2,1)S(1)}, bf16[1,512,128]{2,1,0:T(8,128)(2,1)S(1)}, u32[]{:S(2)}, u32[]{:S(2)}) collective-permute-start(bf16[1,512,128]{2,1,0:T(8,128)(2,1)S(1)} %get-tuple-element.42), channel_id=1, source_target_pairs={{0,1},{1,0},{2,3},{3,2},{4,5},{5,4},{6,7},{7,6},{8,9},{9,8},{10,11... | collective-permute-start | bytes 393224 | tf_op jit(solution)/shard_map/ppermute | solution.py:295
  26.4 24.9 %copy-start.1 = (bf16[2048,128]{1,0:T(8,128)(2,1)S(1)}, bf16[2048,128]{1,0:T(8,128)(2,1)}, u32[]{:S(2)}) copy-start(bf16[2048,128]{1,0:T(8,128)(2,1)} %param.9) | copy-start | bytes 1572868
  26.4 4.6 %collective-permute-start.10 = (f32[16,128]{1,0:T(8,128)S(1)}, f32[16,128]{1,0:T(8,128)S(1)}, u32[]{:S(2)}, u32[]{:S(2)}) collective-permute-start(f32[16,128]{1,0:T(8,128)S(1)} %shard_map.75.refs_2_), channel_id=1, source_target_pairs={{0,3},{1,2},{2,1},{3,0},{4,7},{5,6},{6,5},{7,4},{8,11},{9,10},{10,... | collective-permute-start | bytes 24584 | tf_op jit(solution)/shard_map/ppermute | solution.py:295
  28.0 3.7 %collective-permute-start.8 = (f32[16,128]{1,0:T(8,128)S(1)}, f32[16,128]{1,0:T(8,128)S(1)}, u32[]{:S(2)}, u32[]{:S(2)}) collective-permute-start(f32[16,128]{1,0:T(8,128)S(1)} %shard_map.75.refs_2_), channel_id=1, source_target_pairs={{0,2},{1,3},{2,0},{3,1},{4,6},{5,7},{6,4},{7,5},{8,10},{9,11},{10,... | collective-permute-start | bytes 24584 | tf_op jit(solution)/shard_map/ppermute | solution.py:295
  28.2 3.7 %collective-permute-start.9 = (f32[16,128]{1,0:T(8,128)S(1)}, f32[16,128]{1,0:T(8,128)S(1)}, u32[]{:S(2)}, u32[]{:S(2)}) collective-permute-start(f32[16,128]{1,0:T(8,128)S(1)} %shard_map.75.refs_2_), channel_id=1, source_target_pairs={{0,1},{1,0},{2,3},{3,2},{4,5},{5,4},{6,7},{7,6},{8,9},{9,8},{10,11... | collective-permute-start | bytes 24584 | tf_op jit(solution)/shard_map/ppermute | solution.py:295
  32.1 1.6 %collective-permute-start.11 = (bf16[1024,128]{1,0:T(8,128)(2,1)S(1)}, bf16[1024,128]{1,0:T(8,128)(2,1)S(1)}, u32[]{:S(2)}, u32[]{:S(2)}) collective-permute-start(bf16[1024,128]{1,0:T(8,128)(2,1)S(1)} %get-tuple-element.49), channel_id=1, source_target_pairs={{0,4},{4,0},{8,12},{12,8},{16,20},{20,16},{24,28},{28,24},{1,5},{5... | collective-permute-start | bytes 786440 | tf_op jit(solution)/shard_map/ppermute | solution.py:298
  33.7 6.9 %collective-permute-start.12 = (bf16[256,128]{1,0:T(8,128)(2,1)S(1)}, bf16[256,128]{1,0:T(8,128)(2,1)S(1)}, u32[]{:S(2)}, u32[]{:S(2)}) collective-permute-start(bf16[256,128]{1,0:T(8,128)(2,1)S(1)} %get-tuple-element.50), channel_id=1, source_target_pairs={{0,24},{4,28},{8,16},{12,20},{16,8},{20,12},{24,0},{28,4},{1,25},{... | collective-permute-start | bytes 196616 | tf_op jit(solution)/shard_map/ppermute | solution.py:303
  37.4 5.1 %collective-permute-start.13 = (bf16[256,128]{1,0:T(8,128)(2,1)S(1)}, bf16[256,128]{1,0:T(8,128)(2,1)S(1)}, u32[]{:S(2)}, u32[]{:S(2)}) collective-permute-start(bf16[256,128]{1,0:T(8,128)(2,1)S(1)} %get-tuple-element.51), channel_id=1, source_target_pairs={{0,8},{4,12},{8,0},{12,4},{16,24},{20,28},{24,16},{28,20},{1,9},{5... | collective-permute-start | bytes 196616 | tf_op jit(solution)/shard_map/ppermute | solution.py:303
  37.4 5.9 %collective-permute-start.14 = (bf16[256,128]{1,0:T(8,128)(2,1)S(1)}, bf16[256,128]{1,0:T(8,128)(2,1)S(1)}, u32[]{:S(2)}, u32[]{:S(2)}) collective-permute-start(bf16[256,128]{1,0:T(8,128)(2,1)S(1)} %get-tuple-element.52), channel_id=1, source_target_pairs={{0,16},{4,20},{8,24},{12,28},{16,0},{20,4},{24,8},{28,12},{1,17},{... | collective-permute-start | bytes 196616 | tf_op jit(solution)/shard_map/ppermute | solution.py:303
  43.4 6.4 %collective-permute-start.15 = (bf16[256,128]{1,0:T(8,128)(2,1)S(1)}, bf16[256,128]{1,0:T(8,128)(2,1)S(1)}, u32[]{:S(2)}, u32[]{:S(2)}) collective-permute-start(bf16[256,128]{1,0:T(8,128)(2,1)S(1)} %get-tuple-element.57), channel_id=1, source_target_pairs={{0,24},{4,28},{8,16},{12,20},{16,8},{20,12},{24,0},{28,4},{1,25},{... | collective-permute-start | bytes 196616 | tf_op jit(solution)/shard_map/ppermute | solution.py:303
  45.6 5.1 %collective-permute-start.16 = (bf16[256,128]{1,0:T(8,128)(2,1)S(1)}, bf16[256,128]{1,0:T(8,128)(2,1)S(1)}, u32[]{:S(2)}, u32[]{:S(2)}) collective-permute-start(bf16[256,128]{1,0:T(8,128)(2,1)S(1)} %get-tuple-element.58), channel_id=1, source_target_pairs={{0,8},{4,12},{8,0},{12,4},{16,24},{20,28},{24,16},{28,20},{1,9},{5... | collective-permute-start | bytes 196616 | tf_op jit(solution)/shard_map/ppermute | solution.py:303
  46.0 5.3 %collective-permute-start.17 = (bf16[256,128]{1,0:T(8,128)(2,1)S(1)}, bf16[256,128]{1,0:T(8,128)(2,1)S(1)}, u32[]{:S(2)}, u32[]{:S(2)}) collective-permute-start(bf16[256,128]{1,0:T(8,128)(2,1)S(1)} %get-tuple-element.59), channel_id=1, source_target_pairs={{0,16},{4,20},{8,24},{12,28},{16,0},{20,4},{24,8},{28,12},{1,17},{... | collective-permute-start | bytes 196616 | tf_op jit(solution)/shard_map/ppermute | solution.py:303
  51.6 1.6 %collective-permute-start.18 = (bf16[1024,128]{1,0:T(8,128)(2,1)S(1)}, bf16[1024,128]{1,0:T(8,128)(2,1)S(1)}, u32[]{:S(2)}, u32[]{:S(2)}) collective-permute-start(bf16[1024,128]{1,0:T(8,128)(2,1)S(1)} %bitcast.20), channel_id=1, source_target_pairs={{0,4},{4,0},{8,12},{12,8},{16,20},{20,16},{24,28},{28,24},{1,5},{5... | collective-permute-start | bytes 786440 | tf_op jit(solution)/shard_map/ppermute | solution.py:298
